TPU v7x, 128 devices: a whole 4x4x4 slice. The times are simulated.
128 devices in a mesh: feat: 32 (over x_lo, z, y), frames: 4 (over x_hi, core).
Axes of the slice: x: 4 (x_hi: 2, x_lo: 2; x = x_hi * 2 + x_lo), y: 4, z: 4, core: 2. Of those that a mesh axis runs over, the one named last changes fastest.
Arguments:
- trajectory: bfloat16 [768, 102400], P('frames', 'feat'), may hold values from -40 to 40, as said below
- segment_ids: int32 [768], replicated, may hold values from 0 to 3, never falling along the last dimension, each value on 1 to 384 neighbouring positions
- lag_frames: int32 [3], replicated, may hold values from 1 to 8
Outputs:
- band_tiles: bfloat16 [3, 102400, 3200], P(None, ('feat', 'frames'))
Inputs may be any that keep to these rules, and one draw needn't show every extreme that they name: trajectory values lie in this range.
All inputs are finite; a program needn't handle non-finite values.
Results may differ from a plain program's by a relative error of at most 0.0035.
Values may be sent and summed in bfloat16 or wider, within the bound.
No kernel may reach another device: no remote copies, remote signals or barrier semaphores. Data moves between devices by JAX's collectives and lax.ppermute only.
A program may use at most 128 MiB of HBM per device.

v0:
```python
import jax
import jax.numpy as jnp
from jax import lax
from jax.sharding import PartitionSpec as P

BAND = 3


def from_behind(block, axis, distance):
    devices = range(lax.axis_size(axis))
    route = [((i - distance) % len(devices), i) for i in devices]
    return lax.ppermute(block, axis, route)


def contract(left, right):
    return lax.dot_general(
        left, right, (((0,), (0,)), ((), ())), preferred_element_type=jnp.float32
    )


def further(first):
    result = [first]
    for offset in range(1, BAND):
        result.append(from_behind(result[-1], "feat", -1))
    return result


def local(trajectory, segment_ids, lag_frames):
    total_frames = segment_ids.shape[0]
    width = trajectory.shape[1]
    column_sums = lax.psum(jnp.sum(trajectory.astype(jnp.float32), axis=0), "frames")
    column_mean = column_sums / total_frames
    centered = (trajectory.astype(jnp.float32) - column_mean).astype(jnp.bfloat16)
    own_block = lax.all_gather(centered, "frames", axis=0, tiled=True)
    blocks = further(own_block)
    padded_ids = jnp.concatenate([segment_ids, jnp.full((total_frames,), -1, jnp.int32)])
    quarter = width // lax.axis_size("frames")
    start = lax.axis_index("frames") * quarter
    tiles = []
    for offset in range(BAND):
        lag = lag_frames[offset]
        lagged_ids = lax.dynamic_slice_in_dim(padded_ids, lag, total_frames, 0)
        paired = (segment_ids == lagged_ids).astype(jnp.bfloat16)
        factor = 0.5 / (total_frames - lag).astype(jnp.float32)

        def shifted(block_data):
            padded = jnp.concatenate([block_data, jnp.zeros_like(block_data)], axis=0)
            return lax.dynamic_slice_in_dim(padded, lag, total_frames, 0)

        own_rows = lax.dynamic_slice_in_dim(blocks[0], start, quarter, 1)
        lead_rows = own_rows * paired[:, None]
        lag_rows = shifted(own_rows)
        other = blocks[offset]
        lead_other = other * paired[:, None]
        lag_other = shifted(other)
        total = contract(lead_rows, lag_other) + contract(lag_rows, lead_other)
        tiles.append((total * factor).astype(jnp.bfloat16))
    return jnp.stack(tiles)


def solution(mesh):
    return jax.shard_map(
        local,
        mesh=mesh,
        in_specs=(P("frames", "feat"), P(), P()),
        out_specs=P(None, ("feat", "frames"), None),
        check_vma=False,
    )
```

profile of v0, /device:TPU:121, one launch (start us, length us, event | category | flops | bytes accessed | tf_op | source)
XLA Modules:
  0.0 327.7 jit_solution(18109831058542868596)
XLA Ops:
  6.5 0.0 copy-start
  6.5 0.0 copy-start.1
  6.5 0.0 all-gather.2.cloned.1.call-start
  6.5 1.5 convert_reduce_fusion
  8.0 12.7 %psum.7 = f32[3200]{0:T(1024)S(1)} all-reduce(f32[3200]{0:T(1024)S(1)} %convert_reduce_fusion), channel_id=1, replica_groups=mesh['feat'=32,'frames'=4] {'frames'}, use_global_device_ids=true, to_apply=%region_1.0 | all-reduce | flops 3200 | bytes 25600 | tf_op jit(solution)/shard_map/psum | solution.py:31
  20.8 2.5 fusion.9
  23.3 0.0 all-gather.2.cloned.1.call-update
  23.3 45.3 %all-gather.2.cloned.1.call-done = bf16[768,3200]{1,0:T(8,128)(2,1)} async-done(((bf16[192,3200]{1,0:T(8,128)(2,1)}), bf16[768,3200]{1,0:T(8,128)(2,1)}) %all-gather.2.cloned.1.call-update) | async-done | bytes 4915216 | tf_op jit(solution)/shard_map/all_gather | solution.py:34
  68.7 0.6 collective-permute-start
  69.2 111.3 %collective-permute-done = bf16[768,3200]{1,0:T(8,128)(2,1)} collective-permute-done((bf16[768,3200]{1,0:T(8,128)(2,1)}, bf16[768,3200]{1,0:T(8,128)(2,1)}, u32[]{:S(2)}, u32[]{:S(2)}) %collective-permute-start) | collective-permute-done | bytes 4915232 | tf_op jit(solution)/shard_map/ppermute | solution.py:12
  180.5 0.0 collective-permute-start.1
  180.5 0.0 copy-done
  180.6 0.7 fusion.37
  189.0 0.0 copy-done.1
  189.0 0.1 fusion.24
  189.1 0.0 slice-start
  189.1 2.3 constant_dynamic-slice_fusion
  191.4 0.0 slice-start.1
  191.4 7.1 %fusion.3 = f32[800,3200]{1,0:T(8,128)S(1)} fusion(s32[]{:T(128)S(6)} %select_n.9, bf16[768,3200]{1,0:T(8,128)(2,1)} %all-gather.2.cloned.1.call-done, bf16[768,800]{1,0:T(8,128)(2,1)S(1)} %constant_dynamic-slice_fusion, bf16[768]{0:T(1024)(128)(2,1)S(1)} %get-tuple-element.5), kind=kOutput, calls=%fused_computation.10 | convolution fusion | flops 3932774400 | bytes 16385540 | tf_op jit(solution)/shard_map/dot_general | solution.py:16
  198.5 0.0 slice-done
  198.5 0.0 slice-done.1
  198.5 7.7 %fusion = bf16[1,800,3200]{2,1,0:T(8,128)(2,1)} fusion(f32[800,3200]{1,0:T(8,128)S(1)} %fusion.3, f32[]{:T(128)S(6)} %div.17, bf16[768,3200]{1,0:T(8,128)(2,1)S(1)} %bitcast.10, bf16[768]{0:T(1024)(128)(2,1)S(1)} %get-tuple-element.5, s32[]{:T(128)S(6)} %select_n.9, bf16[768,800]{1,0:T(8,128)(2,1)S(1)} %constant_dynamic-slice_fusion), kind=kOutput, calls=%fused_computation.7 | convolution fusion | flops 3942297600 | bytes 21505544 | tf_op jit(solution)/shard_map/dot_general | solution.py:16
  206.3 7.2 %fusion.6 = f32[800,3200]{1,0:T(8,128)S(1)} fusion(bf16[768,3200]{1,0:T(8,128)(2,1)} %collective-permute-done, bf16[768]{0:T(1024)(128)(2,1)S(1)} %get-tuple-element.7, s32[]{:T(128)S(6)} %select_n.10, bf16[768,800]{1,0:T(8,128)(2,1)S(1)} %constant_dynamic-slice_fusion), kind=kOutput, calls=%fused_computation.13 | convolution fusion | flops 3934617600 | bytes 16385540 | tf_op jit(solution)/shard_map/dot_general | solution.py:16
  213.5 9.9 %fusion.1 = bf16[1,800,3200]{2,1,0:T(8,128)(2,1)} fusion(f32[800,3200]{1,0:T(8,128)S(1)} %fusion.6, f32[]{:T(128)S(6)} %div.18, s32[]{:T(128)S(6)} %select_n.10, bf16[768,3200]{1,0:T(8,128)(2,1)} %collective-permute-done, bf16[768,800]{1,0:T(8,128)(2,1)S(1)} %constant_dynamic-slice_fusion, bf16[768]{0:T(1024)(128)(2,1)S(1)} %get-tuple-element.7), kind=kOutput, calls=%fused_computation.8 | convolution fusion | flops 3940454400 | bytes 21505544 | tf_op jit(solution)/shard_map/dot_general | solution.py:16
  223.4 68.2 %collective-permute-done.1 = bf16[768,3200]{1,0:T(8,128)(2,1)} collective-permute-done((bf16[768,3200]{1,0:T(8,128)(2,1)}, bf16[768,3200]{1,0:T(8,128)(2,1)}, u32[]{:S(2)}, u32[]{:S(2)}) %collective-permute-start.1) | collective-permute-done | bytes 4915232 | tf_op jit(solution)/shard_map/ppermute | solution.py:12
  291.5 0.0 slice-start.2
  291.5 7.7 %fusion.4 = f32[800,3200]{1,0:T(8,128)S(1)} fusion(bf16[768,3200]{1,0:T(8,128)(2,1)} %collective-permute-done.1, bf16[768]{0:T(1024)(128)(2,1)S(1)} %get-tuple-element.6, s32[]{:T(128)S(6)} %select_n.11, bf16[768,800]{1,0:T(8,128)(2,1)S(1)} %constant_dynamic-slice_fusion), kind=kOutput, calls=%fused_computation.11 | convolution fusion | flops 3934617600 | bytes 16385540 | tf_op jit(solution)/shard_map/dot_general | solution.py:16
  299.2 0.0 slice-start.3
  299.2 10.1 %fusion.2 = bf16[1,800,3200]{2,1,0:T(8,128)(2,1)} fusion(f32[800,3200]{1,0:T(8,128)S(1)} %fusion.4, f32[]{:T(128)S(6)} %div.19, s32[]{:T(128)S(6)} %select_n.11, bf16[768,3200]{1,0:T(8,128)(2,1)} %collective-permute-done.1, bf16[768,800]{1,0:T(8,128)(2,1)S(1)} %constant_dynamic-slice_fusion, bf16[768]{0:T(1024)(128)(2,1)S(1)} %get-tuple-element.6), kind=kOutput, calls=%fused_computation.9 | convolution fusion | flops 3940454400 | bytes 21505544 | tf_op jit(solution)/shard_map/dot_general | solution.py:16
  309.3 0.0 slice-done.2
  309.3 0.0 slice-done.3
  309.3 11.5 %pad_maximum_fusion = bf16[3,800,3200]{2,1,0:T(8,128)(2,1)} fusion(bf16[1,800,3200]{2,1,0:T(8,128)(2,1)} %fusion.2, bf16[1,800,3200]{2,1,0:T(8,128)(2,1)} %fusion.1, bf16[1,800,3200]{2,1,0:T(8,128)(2,1)S(1)} %bitcast.12), kind=kLoop, calls=%fused_computation | loop fusion | flops 15360000 | bytes 30720000 | tf_op jit(solution)/shard_map/stack | solution.py:58
  (3 shorter events, 0.0 us)
Async XLA Ops:
  6.5 174.0 %copy-start = (s32[3]{0:T(128)S(1)}, s32[3]{0:T(128)}, u32[]{:S(2)}) copy-start(s32[3]{0:T(128)} %param.5) | copy-start | bytes 40
  6.5 182.5 %copy-start.1 = (s32[768]{0:T(1024)S(1)}, s32[768]{0:T(1024)}, u32[]{:S(2)}) copy-start(s32[768]{0:T(1024)} %param.4) | copy-start | bytes 9220
  6.5 62.1 %all-gather.2.cloned.1.call-start = ((), (), s32[]{:S(2)}) async-start(), calls=%async_computation | async-start | bytes 6144000 | tf_op jit(solution)/shard_map/all_gather | solution.py:34
  68.7 111.9 %collective-permute-start = (bf16[768,3200]{1,0:T(8,128)(2,1)}, bf16[768,3200]{1,0:T(8,128)(2,1)}, u32[]{:S(2)}, u32[]{:S(2)}) collective-permute-start(bf16[768,3200]{1,0:T(8,128)(2,1)} %all-gather.2.cloned.1.call-done), channel_id=1, source_target_pairs={{4,0},{8,4},{12,8},{16,12},{20,16},{24,20},{28,24},{32,28},{36,32}... | collective-permute-start | bytes 14745608 | tf_op jit(solution)/shard_map/ppermute | solution.py:12
  180.5 111.0 %collective-permute-start.1 = (bf16[768,3200]{1,0:T(8,128)(2,1)}, bf16[768,3200]{1,0:T(8,128)(2,1)}, u32[]{:S(2)}, u32[]{:S(2)}) collective-permute-start(bf16[768,3200]{1,0:T(8,128)(2,1)} %collective-permute-done), channel_id=1, source_target_pairs={{4,0},{8,4},{12,8},{16,12},{20,16},{24,20},{28,24},{32,28},{36,32}... | collective-permute-start | bytes 14745608 | tf_op jit(solution)/shard_map/ppermute | solution.py:12
  189.1 9.4 %slice-start = ((s8[4915200]{0:T(1024)(128)(4,1)}), s8[4194304]{0:T(1024)(128)(4,1)S(1)}, s32[]{:S(2)}) async-start(s8[4915200]{0:T(1024)(128)(4,1)} %bitcast.9), calls=%async_computation.1 | async-start | bytes 8388608
  191.4 7.2 %slice-start.1 = ((s8[4915200]{0:T(1024)(128)(4,1)}), s8[720896]{0:T(1024)(128)(4,1)S(1)}, s32[]{:S(2)}) async-start(s8[4915200]{0:T(1024)(128)(4,1)} %bitcast.9), calls=%async_computation.2 | async-start | bytes 1441792
  291.5 17.8 %slice-start.2 = ((s8[5120000]{0:T(1024)(128)(4,1)}), s8[4194304]{0:T(1024)(128)(4,1)S(1)}, s32[]{:S(2)}) async-start(s8[5120000]{0:T(1024)(128)(4,1)} %bitcast.11), calls=%async_computation.3 | async-start | bytes 8388608
  299.2 10.1 %slice-start.3 = ((s8[5120000]{0:T(1024)(128)(4,1)}), s8[925696]{0:T(1024)(128)(4,1)S(1)}, s32[]{:S(2)}) async-start(s8[5120000]{0:T(1024)(128)(4,1)} %bitcast.11), calls=%async_computation.4 | async-start | bytes 1851392
Sparse Core Ops, SparseCore 0:
  23.5 45.1 all-gather.1
where the time goes:
time: 330 us; the launch traced here: 328 us
  waiting for transfers between devices  225 us (68%)
  matrix products  49.7 us (15%)
  between operations  21.3 us (6%)
  other arithmetic  15.6 us (5%)
  blocking collectives  12.7 us (4%)
    ppermute x2, waiting for transfers between devices, from_behind(): return lax.ppermute(block, axis, route)  180 us
    dot_general x6, matrix products, contract(): lax.dot_general(left, right, (((0,), (0,)), ((), ())), preferred_element_...  49.7 us
    all_gather x1, waiting for transfers between devices, local(): own_block = lax.all_gather(centered, 'frames', axis=0, tiled=True)  45.3 us
    psum x1, blocking collectives, local(): lax.psum(jnp.sum(trajectory.astype(jnp.float32), axis=0), 'frames')  12.7 us
    another operation x1, other arithmetic, local(): return jnp.stack(tiles)  11.5 us
  transfers between devices with their start and end apart: 3, of which 3 were waited for; matrix products, arithmetic and copies ran while one was open for 11% of the time, Pallas kernels for 0%

commit v1 on v0

v1 whole, which is shorter than its diff:
```python
import functools

import jax
import jax.numpy as jnp
from jax import lax
from jax.experimental import pallas as pl
from jax.experimental.pallas import tpu as pltpu
from jax.sharding import PartitionSpec as P

BAND = 3
AXES = ("feat", "frames")
F32, BF16 = jnp.float32, jnp.bfloat16
CHUNK = 512
VMEM = 60 << 20


def spans(width):
    return [(c, min(CHUNK, width - c)) for c in range(0, width, CHUNK)]


def center(raw, out, start, size):
    frames = raw.shape[0]
    cols = pl.ds(start, size)
    total = jnp.zeros((8, size), F32)
    for r in range(0, frames, 16):
        x = raw[pl.ds(r, 16), cols].astype(F32)
        total = total + (x[:8] + x[8:])
    mean = jnp.sum(total, axis=0, keepdims=True) / frames
    for r in range(0, frames, 16):
        x = raw[pl.ds(r, 16), cols].astype(F32)
        out[pl.ds(r, 16), cols] = (x - mean).astype(BF16)


def load(place, pieces, raw, sems):
    width = raw.shape[1]
    copies = []
    for i, (c, w) in enumerate(spans(width)):
        row = []
        for j, (piece, (flip, first)) in enumerate(zip(pieces, place)):
            rows = piece.shape[0]
            me = lax.bitwise_xor(sems[0], flip)
            at = pl.multiple_of(me * sems[2] + first, 16)
            copy = pltpu.make_async_copy(
                piece.at[:, pl.ds(c, w)],
                raw.at[pl.ds(at, rows), pl.ds(c, w)],
                sems[1].at[i, j],
            )
            copy.start()
            row.append(copy)
        copies.append(row)
    return copies


def multiply(k, y, cent, factor, tile, out, copies, raw, out_sems):
    width = cent.shape[1]
    half = tile.shape[0]
    stores = []
    for i, (c, w) in enumerate(spans(width)):
        for copy in copies[i]:
            copy.wait()
        center(raw, cent, c, w)
        both = jnp.dot(y[...], cent[:, pl.ds(c, w)], preferred_element_type=F32)
        total = both[:half] + both[half:]
        tile[:, pl.ds(c, w)] = (total * factor).astype(BF16)
        store = pltpu.make_async_copy(
            tile.at[:, pl.ds(c, w)], out.at[k, :, pl.ds(c, w)], out_sems.at[i]
        )
        store.start()
        stores.append(store)
    for store in stores:
        store.wait()


def first_kernel(place, frames, n, me_ref, lag_ref, col_ids, row_ids, *refs):
    pieces = refs[:n]
    out, y_out = refs[n], refs[n + 1]
    raw, cent, tile, y0, lagged, in_sems, out_sems = refs[n + 2:]
    f = me_ref[0]
    copies = load(place, pieces, raw, (f, in_sems, frames // 4))
    width = raw.shape[1]
    quarter = width // 4
    for i, (c, w) in enumerate(spans(width)):
        for copy in copies[i]:
            copy.wait()
        center(raw, cent, c, w)
    begin = f * quarter
    aligned = pl.multiple_of((begin // 128) * 128, 128)
    window = lagged.shape[0]
    rest = pl.multiple_of(begin - aligned, 32)
    same = col_ids[...] == row_ids[...]
    shape = (frames, frames)
    gap = lax.broadcasted_iota(jnp.int32, shape, 1) - lax.broadcasted_iota(jnp.int32, shape, 0)
    for k in range(BAND):
        lag = lag_ref[k]
        ahead = jnp.where(jnp.logical_and(same, gap == lag), 1.0, 0.0)
        back = jnp.where(jnp.logical_and(same, gap == -lag), 1.0, 0.0)
        pair = (ahead + back).astype(BF16)
        lagged[...] = lax.dot_general(
            cent[:, pl.ds(aligned, window)], pair, (((0,), (0,)), ((), ())),
            preferred_element_type=F32,
        )
        rows = lagged[pl.ds(rest, quarter), :]
        high = rows.astype(BF16)
        low = (rows - high.astype(F32)).astype(BF16)
        if k == 0:
            y0[pl.ds(0, quarter), :] = high
            y0[pl.ds(quarter, quarter), :] = low
        else:
            y_out[k - 1, pl.ds(0, quarter), :] = high
            y_out[k - 1, pl.ds(quarter, quarter), :] = low
    stores = []
    factor = 0.5 / (frames - lag_ref[0]).astype(F32)
    for i, (c, w) in enumerate(spans(width)):
        both = jnp.dot(y0[...], cent[:, pl.ds(c, w)], preferred_element_type=F32)
        total = both[:quarter] + both[quarter:]
        tile[:, pl.ds(c, w)] = (total * factor).astype(BF16)
        store = pltpu.make_async_copy(
            tile.at[:, pl.ds(c, w)], out.at[0, :, pl.ds(c, w)], out_sems.at[i]
        )
        store.start()
        stores.append(store)
    for store in stores:
        store.wait()


def first_tile(me, lags, ids, placed, frames):
    place, pieces = [p for p, _ in placed], [a for _, a in placed]
    width = pieces[0].shape[1]
    quarter = width // 4
    n, spans_n = len(pieces), len(spans(width))
    window = -(-(quarter + 96) // 128) * 128
    smem = pl.BlockSpec(memory_space=pltpu.SMEM)
    vmem = pl.BlockSpec(memory_space=pltpu.VMEM)
    hbm = pl.BlockSpec(memory_space=pl.ANY)
    return pl.pallas_call(
        functools.partial(first_kernel, place, frames, n),
        out_shape=(
            jax.ShapeDtypeStruct((BAND, quarter, width), BF16),
            jax.ShapeDtypeStruct((BAND - 1, 2 * quarter, frames), BF16),
        ),
        in_specs=[smem, smem, vmem, vmem] + [hbm] * n,
        out_specs=(hbm, vmem),
        scratch_shapes=[
            pltpu.VMEM((frames, width), BF16),
            pltpu.VMEM((frames, width), BF16),
            pltpu.VMEM((quarter, width), BF16),
            pltpu.VMEM((2 * quarter, frames), BF16),
            pltpu.VMEM((window, frames), F32),
            pltpu.SemaphoreType.DMA((spans_n, n)),
            pltpu.SemaphoreType.DMA((spans_n,)),
        ],
        compiler_params=pltpu.CompilerParams(vmem_limit_bytes=VMEM),
        name="first_tile",
    )(me, lags, ids[:, None], ids[None, :], *pieces)


def later_kernel(k, place, frames, n, me_ref, lag_ref, y, *refs):
    pieces = refs[:n]
    out = refs[n + 1]
    raw, cent, tile, in_sems, out_sems = refs[n + 2:]
    copies = load(place, pieces, raw, (me_ref[0], in_sems, frames // 4))
    factor = 0.5 / (frames - lag_ref[k]).astype(F32)
    multiply(k, y.at[0], cent, factor, tile, out, copies, raw, out_sems)


def later_tile(k, me, lags, y, placed, tiles, frames):
    place, pieces = [p for p, _ in placed], [a for _, a in placed]
    width = pieces[0].shape[1]
    quarter = width // 4
    n, spans_n = len(pieces), len(spans(width))
    smem = pl.BlockSpec(memory_space=pltpu.SMEM)
    hbm = pl.BlockSpec(memory_space=pl.ANY)
    y_spec = pl.BlockSpec((1, 2 * quarter, frames), lambda i: (k - 1, 0, 0))
    return pl.pallas_call(
        functools.partial(later_kernel, k, place, frames, n),
        out_shape=jax.ShapeDtypeStruct(tiles.shape, tiles.dtype),
        grid=(1,),
        in_specs=[smem, smem, y_spec] + [hbm] * (n + 1),
        out_specs=hbm,
        scratch_shapes=[
            pltpu.VMEM((frames, width), BF16),
            pltpu.VMEM((frames, width), BF16),
            pltpu.VMEM((quarter, width), BF16),
            pltpu.SemaphoreType.DMA((spans_n, n)),
            pltpu.SemaphoreType.DMA((spans_n,)),
        ],
        input_output_aliases={3 + n: 0},
        compiler_params=pltpu.CompilerParams(vmem_limit_bytes=VMEM),
        name="later_tile",
    )(me, lags, y, *pieces, tiles)


def local(trajectory, segment_ids, lag_frames):
    blocks_n, parts = lax.axis_size("feat"), lax.axis_size("frames")
    frames = segment_ids.shape[0]
    me = lax.axis_index("frames").astype(jnp.int32).reshape(1)

    def move(array, back, flip):
        route = [
            (b * parts + f, ((b - back) % blocks_n) * parts + (f ^ flip))
            for b in range(blocks_n) for f in range(parts)
        ]
        return lax.ppermute(array, AXES, route)

    own = trajectory
    across = move(own, 0, 2)
    next_own = move(own, 1, 0)
    own_core = move(own, 0, 1)
    after_own = move(own, 2, 0)
    across_core = move(across, 0, 1)
    next_across = move(across, 1, 0)
    next_core = move(next_own, 0, 1)
    next_across_core = move(next_across, 0, 1)
    after_across = move(after_own, 0, 2)
    after_core = move(after_own, 0, 1)
    after_across_core = move(after_across, 0, 1)

    def placed(*four):
        return [((flip, 0), a) for flip, a in enumerate(four)]

    tiles, y = first_tile(
        me, lag_frames, segment_ids, placed(own, own_core, across, across_core), frames
    )
    tiles = later_tile(
        1, me, lag_frames, y,
        placed(next_own, next_core, next_across, next_across_core), tiles, frames,
    )
    tiles = later_tile(
        2, me, lag_frames, y,
        placed(after_own, after_core, after_across, after_across_core), tiles, frames,
    )
    return tiles


def solution(mesh):
    return jax.shard_map(
        local,
        mesh=mesh,
        in_specs=(P("frames", "feat"), P(), P()),
        out_specs=P(None, ("feat", "frames"), None),
        check_vma=False,
    )
```

time: 330 us -> 194 us (0.59)
  the two profiles are of different devices: /device:TPU:121 before, /device:TPU:1 now
where the time goes in v1:
time: 194 us
  waiting for transfers between devices  108 us (56%)
  Pallas kernels  52.5 us (27%)
  starting transfers between devices  30.4 us (16%)
  local copies, waits for them, and re-layouts  2.89 us (1%)
    ppermute x11, waiting for transfers between devices, move(): return lax.ppermute(array, AXES, route)  108 us
    pallas_call x2, Pallas kernels, later_tile(): pl.pallas_call(functools.partial(later_kernel, k, place, frames, n), out_...  31.2 us
    ppermute x11, starting transfers between devices, move(): return lax.ppermute(array, AXES, route)  30.4 us
    pallas_call x1, Pallas kernels, first_tile(): pl.pallas_call(functools.partial(first_kernel, place, frames, n), out_sha...  21.3 us
  transfers between devices with their start and end apart: 11, of which 5 were waited for; matrix products, arithmetic and copies ran while one was open for 1% of the time, Pallas kernels for 19%

profile of v1, /device:TPU:1, one launch (start us, length us, event | category | flops | bytes accessed | tf_op | source)
XLA Modules:
  0.0 194.1 jit_solution(4274407285134671397)
XLA Ops:
  0.0 3.6 %collective-permute-start.1 = (bf16[192,3200]{1,0:T(8,128)(2,1)}, bf16[192,3200]{1,0:T(8,128)(2,1)}, u32[]{:S(2)}, u32[]{:S(2)}) collective-permute-start(bf16[192,3200]{1,0:T(8,128)(2,1)} %refs_0_.1), channel_id=1, source_target_pairs={{0,2},{1,3},{2,0},{3,1},{4,6},{5,7},{6,4},{7,5},{8,10},{9,11},{10,... | collective-permute-start | bytes 3686408 | tf_op jit(solution)/shard_map/ppermute | solution.py:203
  3.6 6.4 %collective-permute-start.3 = (bf16[192,3200]{1,0:T(8,128)(2,1)}, bf16[192,3200]{1,0:T(8,128)(2,1)S(1)}, u32[]{:S(2)}, u32[]{:S(2)}) collective-permute-start(bf16[192,3200]{1,0:T(8,128)(2,1)} %refs_0_.1), channel_id=1, source_target_pairs={{0,120},{1,121},{2,122},{3,123},{4,124},{5,125},{6,126},{7,127},{8... | collective-permute-start | bytes 3686408 | tf_op jit(solution)/shard_map/ppermute | solution.py:203
  10.0 0.8 collective-permute-start.7
  10.8 19.4 %collective-permute-done.1.refs_2_ = bf16[192,3200]{1,0:T(8,128)(2,1)} collective-permute-done((bf16[192,3200]{1,0:T(8,128)(2,1)}, bf16[192,3200]{1,0:T(8,128)(2,1)}, u32[]{:S(2)}, u32[]{:S(2)}) %collective-permute-start.1) | collective-permute-done | bytes 1228832 | tf_op jit(solution)/shard_map/ppermute | solution.py:203
  30.2 7.5 %collective-permute-start.9 = (bf16[192,3200]{1,0:T(8,128)(2,1)}, bf16[192,3200]{1,0:T(8,128)(2,1)}, u32[]{:S(2)}, u32[]{:S(2)}) collective-permute-start(bf16[192,3200]{1,0:T(8,128)(2,1)} %collective-permute-done.1.refs_2_), channel_id=1, source_target_pairs={{0,124},{1,125},{2,126},{3,127},{4,0},{5,1},{6,2},{7,3},{8,4},{9,5... | collective-permute-start | bytes 3686408 | tf_op jit(solution)/shard_map/ppermute | solution.py:203
  37.7 1.8 collective-permute-start
  39.5 16.4 %collective-permute-done.3.refs_0_ = bf16[192,3200]{1,0:T(8,128)(2,1)S(1)} collective-permute-done((bf16[192,3200]{1,0:T(8,128)(2,1)}, bf16[192,3200]{1,0:T(8,128)(2,1)S(1)}, u32[]{:S(2)}, u32[]{:S(2)}) %collective-permute-start.3) | collective-permute-done | bytes 1228832 | tf_op jit(solution)/shard_map/ppermute | solution.py:203
  55.9 0.0 copy-start
  55.9 0.0 collective-permute-start.5
  55.9 3.1 %collective-permute-start.2 = (bf16[192,3200]{1,0:T(8,128)(2,1)}, bf16[192,3200]{1,0:T(8,128)(2,1)}, u32[]{:S(2)}, u32[]{:S(2)}) collective-permute-start(bf16[192,3200]{1,0:T(8,128)(2,1)} %collective-permute-done.1.refs_2_), channel_id=1, source_target_pairs={{0,1},{1,0},{2,3},{3,2},{4,5},{5,4},{6,7},{7,6},{8,9},{9,8},{10,11... | collective-permute-start | bytes 3686408 | tf_op jit(solution)/shard_map/ppermute | solution.py:203
  59.1 24.2 %collective-permute-done.7.refs_0_ = bf16[192,3200]{1,0:T(8,128)(2,1)S(1)} collective-permute-done((bf16[192,3200]{1,0:T(8,128)(2,1)}, bf16[192,3200]{1,0:T(8,128)(2,1)S(1)}, u32[]{:S(2)}, u32[]{:S(2)}) %collective-permute-start.7) | collective-permute-done | bytes 1228832 | tf_op jit(solution)/shard_map/ppermute | solution.py:203
  83.3 0.0 copy-start.1
  83.3 2.7 %collective-permute-start.8 = (bf16[192,3200]{1,0:T(8,128)(2,1)S(1)}, bf16[192,3200]{1,0:T(8,128)(2,1)}, u32[]{:S(2)}, u32[]{:S(2)}) collective-permute-start(bf16[192,3200]{1,0:T(8,128)(2,1)S(1)} %collective-permute-done.7.refs_0_), channel_id=1, source_target_pairs={{0,1},{1,0},{2,3},{3,2},{4,5},{5,4},{6,7},{7,6},{8,9},{9,8},{10,11... | collective-permute-start | bytes 3686408 | tf_op jit(solution)/shard_map/ppermute | solution.py:203
  86.0 23.6 %collective-permute-done.9.refs_2_ = bf16[192,3200]{1,0:T(8,128)(2,1)} collective-permute-done((bf16[192,3200]{1,0:T(8,128)(2,1)}, bf16[192,3200]{1,0:T(8,128)(2,1)}, u32[]{:S(2)}, u32[]{:S(2)}) %collective-permute-start.9) | collective-permute-done | bytes 1228832 | tf_op jit(solution)/shard_map/ppermute | solution.py:203
  109.6 2.7 %collective-permute-start.10 = (bf16[192,3200]{1,0:T(8,128)(2,1)}, bf16[192,3200]{1,0:T(8,128)(2,1)}, u32[]{:S(2)}, u32[]{:S(2)}) collective-permute-start(bf16[192,3200]{1,0:T(8,128)(2,1)} %collective-permute-done.9.refs_2_), channel_id=1, source_target_pairs={{0,1},{1,0},{2,3},{3,2},{4,5},{5,4},{6,7},{7,6},{8,9},{9,8},{10,11... | collective-permute-start | bytes 3686408 | tf_op jit(solution)/shard_map/ppermute | solution.py:203
  112.3 0.0 collective-permute-done.refs_1_
  112.3 0.0 copy-start.2
  112.3 0.1 collective-permute-start.4
  112.4 24.4 %collective-permute-done.5.refs_2_ = bf16[192,3200]{1,0:T(8,128)(2,1)} collective-permute-done((bf16[192,3200]{1,0:T(8,128)(2,1)S(1)}, bf16[192,3200]{1,0:T(8,128)(2,1)}, u32[]{:S(2)}, u32[]{:S(2)}) %collective-permute-start.5) | collective-permute-done | bytes 1228832 | tf_op jit(solution)/shard_map/ppermute | solution.py:203
  136.8 0.0 copy-done.2
  136.8 1.7 collective-permute-start.6
  138.5 1.6 broadcast_in_dim.8.col_ids
  140.1 1.3 broadcast_in_dim.7.row_ids
  141.4 0.0 collective-permute-done.2.refs_3_
  141.4 21.3 %first_tile.1 = (bf16[3,800,3200]{2,1,0:T(8,128)(2,1)}, bf16[2,1600,768]{2,1,0:T(8,128)(2,1)}) custom-call(s32[1]{0:T(128)} %bitcast.me_ref, s32[3]{0:T(128)} %lag_ref.5, s32[768,1]{1,0:T(8,128)} %broadcast_in_dim.8.col_ids, s32[1,768]{1,0:T(1,128)} %broadcast_in_dim.7.row_ids, bf16[192,3200]{1,0:T(8,128)(2,1)} %refs_0_.1, bf16[192,3200]{1,0:T(8,128)(2,1)} %copy-done.2, ...), custom_call_target="tpu_custom_call" | custom-call | tf_op jit(solution)/shard_map/first_tile/pallas_call | solution.py:135
  162.7 0.0 copy-done
  162.7 0.0 copy-done.1
  162.7 0.0 collective-permute-done.8.refs_1_
  162.7 0.0 collective-permute-done.10.refs_3_
  162.7 15.6 %later_tile.2.refs_4_ = bf16[3,800,3200]{2,1,0:T(8,128)(2,1)} custom-call(s32[1]{0:T(128)} %bitcast.me_ref, s32[3]{0:T(128)} %lag_ref.5, bf16[2,1600,768]{2,1,0:T(8,128)(2,1)} %get-tuple-element.7.y, bf16[192,3200]{1,0:T(8,128)(2,1)} %copy-done.1, bf16[192,3200]{1,0:T(8,128)(2,1)} %collective-permute-done.8.refs_1_, ...), custom_call_target="tpu_custom_call", output_to_operand_aliasing={{}: (7, {})} | custom-call | tf_op jit(solution)/shard_map/later_tile/pallas_call | solution.py:174
  178.3 0.0 collective-permute-done.4.refs_1_
  178.3 0.0 collective-permute-done.6.refs_3_
  178.3 15.6 %later_tile.3 = bf16[3,800,3200]{2,1,0:T(8,128)(2,1)} custom-call(s32[1]{0:T(128)} %bitcast.me_ref, s32[3]{0:T(128)} %lag_ref.5, bf16[2,1600,768]{2,1,0:T(8,128)(2,1)} %get-tuple-element.7.y, bf16[192,3200]{1,0:T(8,128)(2,1)} %copy-done, bf16[192,3200]{1,0:T(8,128)(2,1)} %collective-permute-done.4.refs_1_, ...), custom_call_target="tpu_custom_call", output_to_operand_aliasing={{}: (7, {})} | custom-call | tf_op jit(solution)/shard_map/later_tile/pallas_call | solution.py:174
Async XLA Ops:
  0.0 30.2 %collective-permute-start.1 = (bf16[192,3200]{1,0:T(8,128)(2,1)}, bf16[192,3200]{1,0:T(8,128)(2,1)}, u32[]{:S(2)}, u32[]{:S(2)}) collective-permute-start(bf16[192,3200]{1,0:T(8,128)(2,1)} %refs_0_.1), channel_id=1, source_target_pairs={{0,2},{1,3},{2,0},{3,1},{4,6},{5,7},{6,4},{7,5},{8,10},{9,11},{10,... | collective-permute-start | bytes 3686408 | tf_op jit(solution)/shard_map/ppermute | solution.py:203
  3.6 52.3 %collective-permute-start.3 = (bf16[192,3200]{1,0:T(8,128)(2,1)}, bf16[192,3200]{1,0:T(8,128)(2,1)S(1)}, u32[]{:S(2)}, u32[]{:S(2)}) collective-permute-start(bf16[192,3200]{1,0:T(8,128)(2,1)} %refs_0_.1), channel_id=1, source_target_pairs={{0,120},{1,121},{2,122},{3,123},{4,124},{5,125},{6,126},{7,127},{8... | collective-permute-start | bytes 3686408 | tf_op jit(solution)/shard_map/ppermute | solution.py:203
  10.0 73.3 %collective-permute-start.7 = (bf16[192,3200]{1,0:T(8,128)(2,1)}, bf16[192,3200]{1,0:T(8,128)(2,1)S(1)}, u32[]{:S(2)}, u32[]{:S(2)}) collective-permute-start(bf16[192,3200]{1,0:T(8,128)(2,1)} %refs_0_.1), channel_id=1, source_target_pairs={{0,124},{1,125},{2,126},{3,127},{4,0},{5,1},{6,2},{7,3},{8,4},{9,5... | collective-permute-start | bytes 3686408 | tf_op jit(solution)/shard_map/ppermute | solution.py:203
  30.2 79.5 %collective-permute-start.9 = (bf16[192,3200]{1,0:T(8,128)(2,1)}, bf16[192,3200]{1,0:T(8,128)(2,1)}, u32[]{:S(2)}, u32[]{:S(2)}) collective-permute-start(bf16[192,3200]{1,0:T(8,128)(2,1)} %collective-permute-done.1.refs_2_), channel_id=1, source_target_pairs={{0,124},{1,125},{2,126},{3,127},{4,0},{5,1},{6,2},{7,3},{8,4},{9,5... | collective-permute-start | bytes 3686408 | tf_op jit(solution)/shard_map/ppermute | solution.py:203
  37.7 74.7 %collective-permute-start = (bf16[192,3200]{1,0:T(8,128)(2,1)}, bf16[192,3200]{1,0:T(8,128)(2,1)S(1)}, u32[]{:S(2)}, u32[]{:S(2)}) collective-permute-start(bf16[192,3200]{1,0:T(8,128)(2,1)} %refs_0_.1), channel_id=1, source_target_pairs={{0,1},{1,0},{2,3},{3,2},{4,5},{5,4},{6,7},{7,6},{8,9},{9,8},{10,11... | collective-permute-start | bytes 3686408 | tf_op jit(solution)/shard_map/ppermute | solution.py:203
  55.9 106.8 %copy-start = (bf16[192,3200]{1,0:T(8,128)(2,1)}, bf16[192,3200]{1,0:T(8,128)(2,1)S(1)}, u32[]{:S(2)}) copy-start(bf16[192,3200]{1,0:T(8,128)(2,1)S(1)} %collective-permute-done.3.refs_0_) | copy-start | bytes 3686404
  55.9 80.9 %collective-permute-start.5 = (bf16[192,3200]{1,0:T(8,128)(2,1)S(1)}, bf16[192,3200]{1,0:T(8,128)(2,1)}, u32[]{:S(2)}, u32[]{:S(2)}) collective-permute-start(bf16[192,3200]{1,0:T(8,128)(2,1)S(1)} %collective-permute-done.3.refs_0_), channel_id=1, source_target_pairs={{0,2},{1,3},{2,0},{3,1},{4,6},{5,7},{6,4},{7,5},{8,10},{9,11},{10,... | collective-permute-start | bytes 3686408 | tf_op jit(solution)/shard_map/ppermute | solution.py:203
  55.9 85.4 %collective-permute-start.2 = (bf16[192,3200]{1,0:T(8,128)(2,1)}, bf16[192,3200]{1,0:T(8,128)(2,1)}, u32[]{:S(2)}, u32[]{:S(2)}) collective-permute-start(bf16[192,3200]{1,0:T(8,128)(2,1)} %collective-permute-done.1.refs_2_), channel_id=1, source_target_pairs={{0,1},{1,0},{2,3},{3,2},{4,5},{5,4},{6,7},{7,6},{8,9},{9,8},{10,11... | collective-permute-start | bytes 3686408 | tf_op jit(solution)/shard_map/ppermute | solution.py:203
  83.3 79.4 %copy-start.1 = (bf16[192,3200]{1,0:T(8,128)(2,1)}, bf16[192,3200]{1,0:T(8,128)(2,1)S(1)}, u32[]{:S(2)}) copy-start(bf16[192,3200]{1,0:T(8,128)(2,1)S(1)} %collective-permute-done.7.refs_0_) | copy-start | bytes 3686404
  83.3 79.4 %collective-permute-start.8 = (bf16[192,3200]{1,0:T(8,128)(2,1)S(1)}, bf16[192,3200]{1,0:T(8,128)(2,1)}, u32[]{:S(2)}, u32[]{:S(2)}) collective-permute-start(bf16[192,3200]{1,0:T(8,128)(2,1)S(1)} %collective-permute-done.7.refs_0_), channel_id=1, source_target_pairs={{0,1},{1,0},{2,3},{3,2},{4,5},{5,4},{6,7},{7,6},{8,9},{9,8},{10,11... | collective-permute-start | bytes 3686408 | tf_op jit(solution)/shard_map/ppermute | solution.py:203
  109.6 53.1 %collective-permute-start.10 = (bf16[192,3200]{1,0:T(8,128)(2,1)}, bf16[192,3200]{1,0:T(8,128)(2,1)}, u32[]{:S(2)}, u32[]{:S(2)}) collective-permute-start(bf16[192,3200]{1,0:T(8,128)(2,1)} %collective-permute-done.9.refs_2_), channel_id=1, source_target_pairs={{0,1},{1,0},{2,3},{3,2},{4,5},{5,4},{6,7},{7,6},{8,9},{9,8},{10,11... | collective-permute-start | bytes 3686408 | tf_op jit(solution)/shard_map/ppermute | solution.py:203
  112.3 24.4 %copy-start.2 = (bf16[192,3200]{1,0:T(8,128)(2,1)}, bf16[192,3200]{1,0:T(8,128)(2,1)S(1)}, u32[]{:S(2)}) copy-start(bf16[192,3200]{1,0:T(8,128)(2,1)S(1)} %collective-permute-done.refs_1_) | copy-start | bytes 3686404
  112.3 66.0 %collective-permute-start.4 = (bf16[192,3200]{1,0:T(8,128)(2,1)S(1)}, bf16[192,3200]{1,0:T(8,128)(2,1)}, u32[]{:S(2)}, u32[]{:S(2)}) collective-permute-start(bf16[192,3200]{1,0:T(8,128)(2,1)S(1)} %collective-permute-done.3.refs_0_), channel_id=1, source_target_pairs={{0,1},{1,0},{2,3},{3,2},{4,5},{5,4},{6,7},{7,6},{8,9},{9,8},{10,11... | collective-permute-start | bytes 3686408 | tf_op jit(solution)/shard_map/ppermute | solution.py:203
  136.8 41.5 %collective-permute-start.6 = (bf16[192,3200]{1,0:T(8,128)(2,1)}, bf16[192,3200]{1,0:T(8,128)(2,1)}, u32[]{:S(2)}, u32[]{:S(2)}) collective-permute-start(bf16[192,3200]{1,0:T(8,128)(2,1)} %collective-permute-done.5.refs_2_), channel_id=1, source_target_pairs={{0,1},{1,0},{2,3},{3,2},{4,5},{5,4},{6,7},{7,6},{8,9},{9,8},{10,11... | collective-permute-start | bytes 3686408 | tf_op jit(solution)/shard_map/ppermute | solution.py:203

commit v2 on v0

v2 whole, which is shorter than its diff:
```python
import functools

import jax
import jax.numpy as jnp
from jax import lax
from jax.experimental import pallas as pl
from jax.experimental.pallas import tpu as pltpu
from jax.sharding import PartitionSpec as P

BAND = 3
AXES = ("feat", "frames")
F32, BF16 = jnp.float32, jnp.bfloat16
CHUNK = 512
SPLIT = 2048
VMEM = 60 << 20


def spans(first, last):
    return [(c, min(CHUNK, last - c)) for c in range(first, last, CHUNK)]


def center(raw, out, cols):
    frames = raw.shape[0]
    total = jnp.zeros((8, cols.size), F32)
    for r in range(0, frames, 16):
        x = raw[pl.ds(r, 16), cols].astype(F32)
        total = total + (x[:8] + x[8:])
    mean = jnp.sum(total, axis=0, keepdims=True) / frames
    for r in range(0, frames, 16):
        x = raw[pl.ds(r, 16), cols].astype(F32)
        out[pl.ds(r, 16), cols] = (x - mean).astype(BF16)


def start_loads(f, places, pieces, raw, sems, first, last):
    part = raw.shape[0] // 4
    copies = []
    for i, (c, w) in enumerate(spans(first, last)):
        row = []
        for flip, base, j in places:
            piece = pieces[j]
            if base <= c < base + piece.shape[1]:
                at = pl.multiple_of(lax.bitwise_xor(f, flip) * part, 16)
                copy = pltpu.make_async_copy(
                    piece.at[:, pl.ds(c - base, w)],
                    raw.at[pl.ds(at, part), pl.ds(c - first, w)],
                    sems.at[i, flip],
                )
                copy.start()
                row.append(copy)
        copies.append(row)
    return copies


def product(k, y, cent, tile, out, factor, c, w, first, sem):
    here = pl.ds(c - first, w)
    total = jnp.dot(y, cent[:, here], preferred_element_type=F32)
    tile[:, here] = (total * factor).astype(BF16)
    store = pltpu.make_async_copy(tile.at[:, here], out.at[k, :, pl.ds(c, w)], sem)
    store.start()
    return store


def first_kernel(places, frames, n, me_ref, lag_ref, col_ids, row_ids, *refs):
    pieces = refs[:n]
    out, y_out = refs[n], refs[n + 1]
    raw, cent, tile, lagged, in_sems, out_sems = refs[n + 2:]
    f = me_ref[0]
    width = raw.shape[1]
    quarter = width // 4
    copies = start_loads(f, places, pieces, raw, in_sems, 0, width)
    for i, (c, w) in enumerate(spans(0, width)):
        for copy in copies[i]:
            copy.wait()
        center(raw, cent, pl.ds(c, w))
    begin = f * quarter
    aligned = pl.multiple_of((begin // 128) * 128, 128)
    window = lagged.shape[0]
    rest = pl.multiple_of(begin - aligned, 32)
    mine = cent[:, pl.ds(aligned, window)].T
    same = col_ids[...] == row_ids[...]
    shape = (frames, frames)
    gap = lax.broadcasted_iota(jnp.int32, shape, 1) - lax.broadcasted_iota(jnp.int32, shape, 0)
    for k in range(BAND):
        lag = lag_ref[k]
        ahead = jnp.where(jnp.logical_and(same, gap == lag), 1.0, 0.0)
        back = jnp.where(jnp.logical_and(same, gap == -lag), 1.0, 0.0)
        pair = (ahead + back).astype(BF16)
        lagged[...] = jnp.dot(mine, pair, preferred_element_type=F32)
        y_out[k] = lagged[pl.ds(rest, quarter), :].astype(BF16)
    factor = 0.5 / (frames - lag_ref[0]).astype(F32)
    stores = [
        product(0, y_out[0], cent, tile, out, factor, c, w, 0, out_sems.at[i])
        for i, (c, w) in enumerate(spans(0, width))
    ]
    for store in stores:
        store.wait()


SMEM_SPEC = pl.BlockSpec(memory_space=pltpu.SMEM)
VMEM_SPEC = pl.BlockSpec(memory_space=pltpu.VMEM)
HBM_SPEC = pl.BlockSpec(memory_space=pl.ANY)


def cost(frames, quarter, columns, extra=0):
    return pl.CostEstimate(
        flops=2 * frames * quarter * (2 * columns + extra),
        bytes_accessed=2 * columns * (frames + quarter),
        transcendentals=0,
    )


def listed(placed):
    places = [(flip, base, j) for j, (flip, base, _) in enumerate(placed)]
    return places, [array for _, _, array in placed]


def first_tile(me, lags, ids, placed, frames):
    places, pieces = listed(placed)
    width = pieces[0].shape[1]
    quarter = width // 4
    n, count = len(pieces), len(spans(0, width))
    window = -(-(quarter + 96) // 128) * 128
    return pl.pallas_call(
        functools.partial(first_kernel, places, frames, n),
        out_shape=(
            jax.ShapeDtypeStruct((BAND, quarter, width), BF16),
            jax.ShapeDtypeStruct((BAND, quarter, frames), BF16),
        ),
        in_specs=[SMEM_SPEC, SMEM_SPEC, VMEM_SPEC, VMEM_SPEC] + [HBM_SPEC] * n,
        out_specs=(HBM_SPEC, VMEM_SPEC),
        scratch_shapes=[
            pltpu.VMEM((frames, width), BF16),
            pltpu.VMEM((frames, width), BF16),
            pltpu.VMEM((quarter, width), BF16),
            pltpu.VMEM((window, frames), F32),
            pltpu.SemaphoreType.DMA((count, 4)),
            pltpu.SemaphoreType.DMA((count,)),
        ],
        compiler_params=pltpu.CompilerParams(vmem_limit_bytes=VMEM),
        cost_estimate=cost(frames, quarter, width, 3 * frames),
        name="first_tile",
    )(me, lags, ids[:, None], ids[None, :], *pieces)


def later_kernel(k, places, frames, n, first, last, me_ref, lag_ref, y, *refs):
    pieces = refs[:n]
    out, token = refs[n + 1], refs[n + 2]
    raw, cent, tile, in_sems, out_sems = refs[n + 3:]
    token[0] = 0
    copies = start_loads(me_ref[0], places, pieces, raw, in_sems, first, last)
    factor = 0.5 / (frames - lag_ref[k]).astype(F32)
    steps = spans(first, last)
    stores = []
    for i in range(len(steps) + 1):
        if i < len(steps):
            c, w = steps[i]
            for copy in copies[i]:
                copy.wait()
            center(raw, cent, pl.ds(c - first, w))
        if i > 0:
            c, w = steps[i - 1]
            stores.append(
                product(k, y[0], cent, tile, out, factor, c, w, first, out_sems.at[i - 1])
            )
    for store in stores:
        store.wait()


def later_tile(k, me, lags, y, placed, tiles, frames, first, last):
    places, pieces = listed(placed)
    columns = last - first
    quarter = tiles.shape[1]
    n, count = len(pieces), len(spans(first, last))
    y_spec = pl.BlockSpec((1, quarter, frames), lambda i: (k, 0, 0))
    return pl.pallas_call(
        functools.partial(later_kernel, k, places, frames, n, first, last),
        out_shape=(
            jax.ShapeDtypeStruct(tiles.shape, tiles.dtype),
            jax.ShapeDtypeStruct((1,), jnp.int32),
        ),
        grid=(1,),
        in_specs=[SMEM_SPEC, SMEM_SPEC, y_spec] + [HBM_SPEC] * (n + 1),
        out_specs=(HBM_SPEC, SMEM_SPEC),
        scratch_shapes=[
            pltpu.VMEM((frames, columns), BF16),
            pltpu.VMEM((frames, columns), BF16),
            pltpu.VMEM((quarter, columns), BF16),
            pltpu.SemaphoreType.DMA((count, 4)),
            pltpu.SemaphoreType.DMA((count,)),
        ],
        input_output_aliases={3 + n: 0},
        compiler_params=pltpu.CompilerParams(vmem_limit_bytes=VMEM),
        cost_estimate=cost(frames, quarter, columns),
        name="later_tile",
    )(me, lags, y, *pieces, tiles)


def after(array, *done):
    return lax.optimization_barrier((array, *done))[0]


def local(trajectory, segment_ids, lag_frames):
    blocks_n, parts = lax.axis_size("feat"), lax.axis_size("frames")
    frames = segment_ids.shape[0]
    width = trajectory.shape[1]
    half = blocks_n // 2
    me = lax.axis_index("frames").astype(jnp.int32).reshape(1)

    def move(array, to):
        route = []
        for b in range(blocks_n):
            for f in range(parts):
                to_b, to_f = to(b, f)
                route.append((b * parts + f, to_b * parts + to_f))
        return lax.ppermute(array, AXES, route)

    def wraps(b, k):
        return b % half >= half - k

    def core(array):
        return move(array, lambda b, f: (b, f ^ 1))

    def ring(array, k):
        return move(array, lambda b, f: (b - b % half + (b - k) % half, f))

    def straight(array, k):
        return move(array, lambda b, f: ((b + half * wraps(b, k)) % blocks_n, f))

    def cross(array, k):
        return move(array, lambda b, f: ((b + half * wraps(b, k)) % blocks_n, f ^ 2))

    own = trajectory
    across = cross(own, 0)
    next_ring = ring(own, 1)
    own_core = core(own)
    after_ring = ring(after(own, next_ring), 2)
    next_across = cross(next_ring, 1)
    next_own = straight(next_ring, 1)
    across_core = core(across)
    tiles, y = first_tile(
        me, lag_frames, segment_ids,
        [(0, 0, own), (1, 0, own_core), (2, 0, across), (3, 0, across_core)], frames,
    )
    next_core = core(next_own)
    next_across_core = core(next_across)
    after_ring = after(after_ring, y)
    after_across_a = cross(after_ring[:, :SPLIT], 2)
    after_across_b = cross(after_ring[:, SPLIT:], 2)
    after_own = straight(after_ring, 2)
    after_core = core(after_own)
    tiles, token = later_tile(
        1, me, lag_frames, y,
        [(0, 0, next_own), (1, 0, next_core), (2, 0, next_across), (3, 0, next_across_core)],
        tiles, frames, 0, width,
    )
    after_across_a = after(after_across_a, token)
    after_across_core_a = core(after_across_a)
    after_across_core_b = core(after_across_b)
    tiles, token = later_tile(
        2, me, lag_frames, y,
        [(0, 0, after_own), (1, 0, after_core), (2, 0, after_across_a), (3, 0, after_across_core_a)],
        tiles, frames, 0, SPLIT,
    )
    tiles, token = later_tile(
        2, me, lag_frames, y,
        [(0, 0, after_own), (1, 0, after_core), (2, SPLIT, after_across_b), (3, SPLIT, after_across_core_b)],
        tiles, frames, SPLIT, width,
    )
    return tiles


def solution(mesh):
    return jax.shard_map(
        local,
        mesh=mesh,
        in_specs=(P("frames", "feat"), P(), P()),
        out_specs=P(None, ("feat", "frames"), None),
        check_vma=False,
    )
```

time: 330 us -> 137 us (0.42)
  waiting for transfers between devices: 225 us -> 68.6 us
  matrix products: 49.7 us -> 0 us
  Pallas kernels: 0 us -> 40.6 us
  starting transfers between devices: 0.56 us -> 22.3 us
  between operations: 21.3 us -> 0.31 us
  other arithmetic: 15.6 us -> 0 us
  blocking collectives: 12.7 us -> 0 us
    ppermute x2 -> x15, waiting for transfers between devices: 180 us -> 68.6 us  [move(): return lax.ppermute(array, AXES, route)]
    dot_general x6 -> x0, matrix products: 49.7 us -> none  [contract(): lax.dot_general(left, right, (((0,), (0,)), ((), ())), preferred_element_...]
    all_gather x1 -> x0, waiting for transfers between devices: 45.3 us -> none  [local(): own_block = lax.all_gather(centered, 'frames', axis=0, tiled=True)]
    pallas_call x0 -> x4, Pallas kernels: none -> 40.6 us  [the longest x3 25 us: later_tile(): pl.pallas_call(functools.partial(later_kernel, k, places, frames, n, firs...]
    ppermute x2 -> x15, starting transfers between devices: 0.56 us -> 22.3 us  [move(): return lax.ppermute(array, AXES, route)]
    psum x1 -> x0, blocking collectives: 12.7 us -> none  [local(): lax.psum(jnp.sum(trajectory.astype(jnp.float32), axis=0), 'frames')]
    another operation x1 -> x0, other arithmetic: 11.5 us -> none  [local(): return jnp.stack(tiles)]
  transfers between devices with their start and end apart: 3 -> 15, of which waited for: 3 -> 5; matrix products, arithmetic and copies ran while one was open for 11% -> 2% of each run, Pallas kernels for 0% -> 25%
where the time goes in v2:
time: 137 us
  waiting for transfers between devices  68.6 us (50%)
  Pallas kernels  40.6 us (30%)
  starting transfers between devices  22.3 us (16%)
  local copies, waits for them, and re-layouts  5.07 us (4%)
    ppermute x15, waiting for transfers between devices, move(): return lax.ppermute(array, AXES, route)  68.6 us
    pallas_call x3, Pallas kernels, later_tile(): pl.pallas_call(functools.partial(later_kernel, k, places, frames, n, firs...  25 us
    ppermute x15, starting transfers between devices, move(): return lax.ppermute(array, AXES, route)  22.3 us
    pallas_call x1, Pallas kernels, first_tile(): pl.pallas_call(functools.partial(first_kernel, places, frames, n), out_sh...  15.6 us
  transfers between devices with their start and end apart: 15, of which 5 were waited for; matrix products, arithmetic and copies ran while one was open for 2% of the time, Pallas kernels for 25%

profile of v2, /device:TPU:121, one launch (start us, length us, event | category | flops | bytes accessed | tf_op | source)
XLA Modules:
  0.0 136.9 jit_solution(13853399437000027975)
XLA Ops:
  0.0 2.7 %collective-permute-start.1 = (bf16[192,3200]{1,0:T(8,128)(2,1)}, bf16[192,3200]{1,0:T(8,128)(2,1)}, u32[]{:S(2)}, u32[]{:S(2)}) collective-permute-start(bf16[192,3200]{1,0:T(8,128)(2,1)} %refs_0_.1), channel_id=1, source_target_pairs={{0,2},{1,3},{2,0},{3,1},{4,6},{5,7},{6,4},{7,5},{8,10},{9,11},{10,... | collective-permute-start | bytes 3686408 | tf_op jit(solution)/shard_map/ppermute | solution.py:215
  2.7 0.5 collective-permute-start.3
  3.2 1.2 collective-permute-start
  4.4 25.3 %collective-permute-done.1.refs_2_ = bf16[192,3200]{1,0:T(8,128)(2,1)} collective-permute-done((bf16[192,3200]{1,0:T(8,128)(2,1)}, bf16[192,3200]{1,0:T(8,128)(2,1)}, u32[]{:S(2)}, u32[]{:S(2)}) %collective-permute-start.1) | collective-permute-done | bytes 1228832 | tf_op jit(solution)/shard_map/ppermute | solution.py:215
  29.7 1.5 %collective-permute-start.2 = (bf16[192,3200]{1,0:T(8,128)(2,1)}, bf16[192,3200]{1,0:T(8,128)(2,1)}, u32[]{:S(2)}, u32[]{:S(2)}) collective-permute-start(bf16[192,3200]{1,0:T(8,128)(2,1)} %collective-permute-done.1.refs_2_), channel_id=1, source_target_pairs={{0,1},{1,0},{2,3},{3,2},{4,5},{5,4},{6,7},{7,6},{8,9},{9,8},{10,11... | collective-permute-start | bytes 3686408 | tf_op jit(solution)/shard_map/ppermute | solution.py:215
  31.3 2.6 %collective-permute-done.3 = bf16[192,3200]{1,0:T(8,128)(2,1)S(1)} collective-permute-done((bf16[192,3200]{1,0:T(8,128)(2,1)}, bf16[192,3200]{1,0:T(8,128)(2,1)S(1)}, u32[]{:S(2)}, u32[]{:S(2)}) %collective-permute-start.3) | collective-permute-done | bytes 1228832 | tf_op jit(solution)/shard_map/ppermute | solution.py:215
  33.8 0.0 collective-permute-start.4
  33.9 1.3 broadcast_in_dim.7.row_ids
  35.1 1.6 %broadcast_in_dim.8.col_ids = s32[768,1]{1,0:T(8,128)} reshape(s32[768]{0:T(1024)} %param.4) | data formatting | bytes 6144 | tf_op jit(solution)/shard_map/broadcast_in_dim | solution.py:142
  36.7 0.9 collective-permute-start.13
  37.6 1.9 %collective-permute-start.11 = (bf16[192,3200]{1,0:T(8,128)(2,1)S(1)}, bf16[192,3200]{1,0:T(8,128)(2,1)}, u32[]{:S(2)}, u32[]{:S(2)}) collective-permute-start(bf16[192,3200]{1,0:T(8,128)(2,1)S(1)} %collective-permute-done.3), channel_id=1, source_target_pairs={{0,0},{1,1},{2,2},{3,3},{4,4},{5,5},{6,6},{7,7},{8,8},{9,9},{10,10... | collective-permute-start | bytes 3686408 | tf_op jit(solution)/shard_map/ppermute | solution.py:215
  39.5 0.0 collective-permute-done.refs_1_
  39.5 0.0 collective-permute-done.2.refs_3_
  39.5 15.6 %first_tile.1 = (bf16[3,800,3200]{2,1,0:T(8,128)(2,1)}, bf16[3,800,768]{2,1,0:T(8,128)(2,1)}) custom-call(s32[1]{0:T(128)} %bitcast.me_ref, s32[3]{0:T(128)} %lag_ref.7, s32[768,1]{1,0:T(8,128)} %broadcast_in_dim.8.col_ids, s32[1,768]{1,0:T(1,128)} %broadcast_in_dim.7.row_ids, bf16[192,3200]{1,0:T(8,128)(2,1)} %refs_0_.1, ...), custom_call_target="tpu_custom_call" | custom-call | flops 10695475200 | bytes 10035200 | tf_op jit(solution)/shard_map/first_tile/pallas_call | solution.py:123
  55.2 9.2 %collective-permute-done.4 = bf16[192,3200]{1,0:T(8,128)(2,1)S(1)} collective-permute-done((bf16[192,3200]{1,0:T(8,128)(2,1)}, bf16[192,3200]{1,0:T(8,128)(2,1)S(1)}, u32[]{:S(2)}, u32[]{:S(2)}) %collective-permute-start.4) | collective-permute-done | bytes 1228832 | tf_op jit(solution)/shard_map/ppermute | solution.py:215
  64.3 2.2 %collective-permute-start.5 = (bf16[192,3200]{1,0:T(8,128)(2,1)S(1)}, bf16[192,3200]{1,0:T(8,128)(2,1)S(1)}, u32[]{:S(2)}, u32[]{:S(2)}) collective-permute-start(bf16[192,3200]{1,0:T(8,128)(2,1)S(1)} %collective-permute-done.4), channel_id=1, source_target_pairs={{0,0},{1,1},{2,2},{3,3},{4,4},{5,5},{6,6},{7,7},{8,8},{9,9},{10,10... | collective-permute-start | bytes 3686408 | tf_op jit(solution)/shard_map/ppermute | solution.py:215
  66.5 0.0 collective-permute-done.13.refs_2_
  66.5 3.1 %collective-permute-start.14 = (bf16[192,3200]{1,0:T(8,128)(2,1)}, bf16[192,3200]{1,0:T(8,128)(2,1)}, u32[]{:S(2)}, u32[]{:S(2)}) collective-permute-start(bf16[192,3200]{1,0:T(8,128)(2,1)} %collective-permute-done.13.refs_2_), channel_id=1, source_target_pairs={{0,1},{1,0},{2,3},{3,2},{4,5},{5,4},{6,7},{7,6},{8,9},{9,8},{10,11... | collective-permute-start | bytes 3686408 | tf_op jit(solution)/shard_map/ppermute | solution.py:215
  69.7 0.0 collective-permute-done.11.refs_0_
  69.7 0.1 collective-permute-start.12
  69.8 0.1 slice.7
  69.9 1.8 %collective-permute-start.9 = (bf16[192,2048]{1,0:T(8,128)(2,1)S(1)}, bf16[192,2048]{1,0:T(8,128)(2,1)}, u32[]{:S(2)}, u32[]{:S(2)}) collective-permute-start(bf16[192,2048]{1,0:T(8,128)(2,1)S(1)} %slice.7), channel_id=1, source_target_pairs={{0,2},{1,3},{2,0},{3,1},{4,6},{5,7},{6,4},{7,5},{8,10},{9,11},{10,... | collective-permute-start | bytes 2359304 | tf_op jit(solution)/shard_map/ppermute | solution.py:215
  71.7 20.3 %collective-permute-done.5.refs_0_ = bf16[192,3200]{1,0:T(8,128)(2,1)S(1)} collective-permute-done((bf16[192,3200]{1,0:T(8,128)(2,1)S(1)}, bf16[192,3200]{1,0:T(8,128)(2,1)S(1)}, u32[]{:S(2)}, u32[]{:S(2)}) %collective-permute-start.5) | collective-permute-done | bytes 1228832 | tf_op jit(solution)/shard_map/ppermute | solution.py:215
  91.9 0.0 copy-start
  91.9 3.7 %collective-permute-start.6 = (bf16[192,3200]{1,0:T(8,128)(2,1)S(1)}, bf16[192,3200]{1,0:T(8,128)(2,1)S(1)}, u32[]{:S(2)}, u32[]{:S(2)}) collective-permute-start(bf16[192,3200]{1,0:T(8,128)(2,1)S(1)} %collective-permute-done.5.refs_0_), channel_id=1, source_target_pairs={{0,1},{1,0},{2,3},{3,2},{4,5},{5,4},{6,7},{7,6},{8,9},{9,8},{10,11... | collective-permute-start | bytes 3686408 | tf_op jit(solution)/shard_map/ppermute | solution.py:215
  95.7 1.5 %collective-permute-start.7 = (bf16[192,1152]{1,0:T(8,128)(2,1)S(1)}, bf16[192,1152]{1,0:T(8,128)(2,1)S(1)}, u32[]{:S(2)}, u32[]{:S(2)}) collective-permute-start(bf16[192,1152]{1,0:T(8,128)(2,1)S(1)} %slice.6), channel_id=1, source_target_pairs={{0,2},{1,3},{2,0},{3,1},{4,6},{5,7},{6,4},{7,5},{8,10},{9,11},{10,... | collective-permute-start | bytes 1327112 | tf_op jit(solution)/shard_map/ppermute | solution.py:215
  97.2 0.0 collective-permute-done.9.refs_2_
  97.2 0.3 collective-permute-start.10
  97.5 11.3 %collective-permute-done.7.refs_2_ = bf16[192,1152]{1,0:T(8,128)(2,1)S(1)} collective-permute-done((bf16[192,1152]{1,0:T(8,128)(2,1)S(1)}, bf16[192,1152]{1,0:T(8,128)(2,1)S(1)}, u32[]{:S(2)}, u32[]{:S(2)}) %collective-permute-start.7) | collective-permute-done | bytes 442400 | tf_op jit(solution)/shard_map/ppermute | solution.py:215
  108.8 0.0 copy-start.3
  108.8 0.8 collective-permute-start.8
  109.6 0.0 collective-permute-done.14.refs_3_
  109.6 0.0 collective-permute-done.12.refs_1_
  109.6 10.3 %later_tile.3 = (bf16[3,800,3200]{2,1,0:T(8,128)(2,1)}, s32[1]{0:T(128)}) custom-call(s32[1]{0:T(128)} %bitcast.me_ref, s32[3]{0:T(128)} %lag_ref.7, bf16[3,800,768]{2,1,0:T(8,128)(2,1)} %get-tuple-element.12.y, bf16[192,3200]{1,0:T(8,128)(2,1)} %collective-permute-done.11.refs_0_, ...), custom_call_target="tpu_custom_call", output_to_operand_aliasing={{0}: (7, {})} | custom-call | flops 7864320000 | bytes 10035200 | tf_op jit(solution)/shard_map/later_tile/pallas_call | solution.py:175
  119.9 0.0 copy-done
  119.9 0.0 copy-done.3
  119.9 0.0 collective-permute-done.10.refs_3_
  119.9 0.0 copy-start.2
  119.9 0.0 collective-permute-done.6.refs_1_
  119.9 0.0 copy-start.1
  120.0 0.9 copy-done.2
  120.8 0.4 copy-done.1
  121.2 7.9 %later_tile.4 = (bf16[3,800,3200]{2,1,0:T(8,128)(2,1)}, s32[1]{0:T(128)}) custom-call(s32[1]{0:T(128)} %bitcast.me_ref, s32[3]{0:T(128)} %lag_ref.7, bf16[3,800,768]{2,1,0:T(8,128)(2,1)} %get-tuple-element.12.y, bf16[192,3200]{1,0:T(8,128)(2,1)} %copy-done, bf16[192,3200]{1,0:T(8,128)(2,1)} %copy-done.1, ...), custom_call_target="tpu_custom_call", output_to_operand_aliasing={{0}: (7, {})} | custom-call | flops 5033164800 | bytes 6422528 | tf_op jit(solution)/shard_map/later_tile/pallas_call | solution.py:175
  129.2 0.0 collective-permute-done.8.refs_3_
  129.2 0.0 copy-start.4
  129.2 0.8 copy-done.4
  130.0 6.7 %later_tile.5 = (bf16[3,800,3200]{2,1,0:T(8,128)(2,1)}, s32[1]{0:T(128)}) custom-call(s32[1]{0:T(128)} %bitcast.me_ref, s32[3]{0:T(128)} %lag_ref.7, bf16[3,800,768]{2,1,0:T(8,128)(2,1)} %get-tuple-element.12.y, bf16[192,3200]{1,0:T(8,128)(2,1)} %copy-done, bf16[192,3200]{1,0:T(8,128)(2,1)} %copy-done.1, ...), custom_call_target="tpu_custom_call", output_to_operand_aliasing={{0}: (7, {})} | custom-call | flops 2831155200 | bytes 3612672 | tf_op jit(solution)/shard_map/later_tile/pallas_call | solution.py:175
  (1 shorter events, 0.0 us)
Async XLA Ops:
  0.0 29.7 %collective-permute-start.1 = (bf16[192,3200]{1,0:T(8,128)(2,1)}, bf16[192,3200]{1,0:T(8,128)(2,1)}, u32[]{:S(2)}, u32[]{:S(2)}) collective-permute-start(bf16[192,3200]{1,0:T(8,128)(2,1)} %refs_0_.1), channel_id=1, source_target_pairs={{0,2},{1,3},{2,0},{3,1},{4,6},{5,7},{6,4},{7,5},{8,10},{9,11},{10,... | collective-permute-start | bytes 3686408 | tf_op jit(solution)/shard_map/ppermute | solution.py:215
  2.7 31.1 %collective-permute-start.3 = (bf16[192,3200]{1,0:T(8,128)(2,1)}, bf16[192,3200]{1,0:T(8,128)(2,1)S(1)}, u32[]{:S(2)}, u32[]{:S(2)}) collective-permute-start(bf16[192,3200]{1,0:T(8,128)(2,1)} %refs_0_.1), channel_id=1, source_target_pairs={{0,60},{1,61},{2,62},{3,63},{4,0},{5,1},{6,2},{7,3},{8,4},{9,5},{1... | collective-permute-start | bytes 3686408 | tf_op jit(solution)/shard_map/ppermute | solution.py:215
  3.2 36.3 %collective-permute-start = (bf16[192,3200]{1,0:T(8,128)(2,1)}, bf16[192,3200]{1,0:T(8,128)(2,1)}, u32[]{:S(2)}, u32[]{:S(2)}) collective-permute-start(bf16[192,3200]{1,0:T(8,128)(2,1)} %refs_0_.1), channel_id=1, source_target_pairs={{0,1},{1,0},{2,3},{3,2},{4,5},{5,4},{6,7},{7,6},{8,9},{9,8},{10,11... | collective-permute-start | bytes 3686408 | tf_op jit(solution)/shard_map/ppermute | solution.py:215
  29.7 9.8 %collective-permute-start.2 = (bf16[192,3200]{1,0:T(8,128)(2,1)}, bf16[192,3200]{1,0:T(8,128)(2,1)}, u32[]{:S(2)}, u32[]{:S(2)}) collective-permute-start(bf16[192,3200]{1,0:T(8,128)(2,1)} %collective-permute-done.1.refs_2_), channel_id=1, source_target_pairs={{0,1},{1,0},{2,3},{3,2},{4,5},{5,4},{6,7},{7,6},{8,9},{9,8},{10,11... | collective-permute-start | bytes 3686408 | tf_op jit(solution)/shard_map/ppermute | solution.py:215
  33.8 30.5 %collective-permute-start.4 = (bf16[192,3200]{1,0:T(8,128)(2,1)}, bf16[192,3200]{1,0:T(8,128)(2,1)S(1)}, u32[]{:S(2)}, u32[]{:S(2)}) collective-permute-start(bf16[192,3200]{1,0:T(8,128)(2,1)} %refs_0_.1), channel_id=1, source_target_pairs={{0,56},{1,57},{2,58},{3,59},{4,60},{5,61},{6,62},{7,63},{8,0},{9,1... | collective-permute-start | bytes 3686408 | tf_op jit(solution)/shard_map/ppermute | solution.py:215
  36.7 29.8 %collective-permute-start.13 = (bf16[192,3200]{1,0:T(8,128)(2,1)S(1)}, bf16[192,3200]{1,0:T(8,128)(2,1)}, u32[]{:S(2)}, u32[]{:S(2)}) collective-permute-start(bf16[192,3200]{1,0:T(8,128)(2,1)S(1)} %collective-permute-done.3), channel_id=1, source_target_pairs={{0,2},{1,3},{2,0},{3,1},{4,6},{5,7},{6,4},{7,5},{8,10},{9,11},{10,... | collective-permute-start | bytes 3686408 | tf_op jit(solution)/shard_map/ppermute | solution.py:215
  37.6 32.1 %collective-permute-start.11 = (bf16[192,3200]{1,0:T(8,128)(2,1)S(1)}, bf16[192,3200]{1,0:T(8,128)(2,1)}, u32[]{:S(2)}, u32[]{:S(2)}) collective-permute-start(bf16[192,3200]{1,0:T(8,128)(2,1)S(1)} %collective-permute-done.3), channel_id=1, source_target_pairs={{0,0},{1,1},{2,2},{3,3},{4,4},{5,5},{6,6},{7,7},{8,8},{9,9},{10,10... | collective-permute-start | bytes 3686408 | tf_op jit(solution)/shard_map/ppermute | solution.py:215
  64.3 27.6 %collective-permute-start.5 = (bf16[192,3200]{1,0:T(8,128)(2,1)S(1)}, bf16[192,3200]{1,0:T(8,128)(2,1)S(1)}, u32[]{:S(2)}, u32[]{:S(2)}) collective-permute-start(bf16[192,3200]{1,0:T(8,128)(2,1)S(1)} %collective-permute-done.4), channel_id=1, source_target_pairs={{0,0},{1,1},{2,2},{3,3},{4,4},{5,5},{6,6},{7,7},{8,8},{9,9},{10,10... | collective-permute-start | bytes 3686408 | tf_op jit(solution)/shard_map/ppermute | solution.py:215
  66.5 43.0 %collective-permute-start.14 = (bf16[192,3200]{1,0:T(8,128)(2,1)}, bf16[192,3200]{1,0:T(8,128)(2,1)}, u32[]{:S(2)}, u32[]{:S(2)}) collective-permute-start(bf16[192,3200]{1,0:T(8,128)(2,1)} %collective-permute-done.13.refs_2_), channel_id=1, source_target_pairs={{0,1},{1,0},{2,3},{3,2},{4,5},{5,4},{6,7},{7,6},{8,9},{9,8},{10,11... | collective-permute-start | bytes 3686408 | tf_op jit(solution)/shard_map/ppermute | solution.py:215
  69.7 39.9 %collective-permute-start.12 = (bf16[192,3200]{1,0:T(8,128)(2,1)}, bf16[192,3200]{1,0:T(8,128)(2,1)}, u32[]{:S(2)}, u32[]{:S(2)}) collective-permute-start(bf16[192,3200]{1,0:T(8,128)(2,1)} %collective-permute-done.11.refs_0_), channel_id=1, source_target_pairs={{0,1},{1,0},{2,3},{3,2},{4,5},{5,4},{6,7},{7,6},{8,9},{9,8},{10,11... | collective-permute-start | bytes 3686408 | tf_op jit(solution)/shard_map/ppermute | solution.py:215
  69.9 27.3 %collective-permute-start.9 = (bf16[192,2048]{1,0:T(8,128)(2,1)S(1)}, bf16[192,2048]{1,0:T(8,128)(2,1)}, u32[]{:S(2)}, u32[]{:S(2)}) collective-permute-start(bf16[192,2048]{1,0:T(8,128)(2,1)S(1)} %slice.7), channel_id=1, source_target_pairs={{0,2},{1,3},{2,0},{3,1},{4,6},{5,7},{6,4},{7,5},{8,10},{9,11},{10,... | collective-permute-start | bytes 2359304 | tf_op jit(solution)/shard_map/ppermute | solution.py:215
  91.9 28.0 %copy-start = (bf16[192,3200]{1,0:T(8,128)(2,1)}, bf16[192,3200]{1,0:T(8,128)(2,1)S(1)}, u32[]{:S(2)}) copy-start(bf16[192,3200]{1,0:T(8,128)(2,1)S(1)} %collective-permute-done.5.refs_0_) | copy-start | bytes 3686404
  91.9 28.0 %collective-permute-start.6 = (bf16[192,3200]{1,0:T(8,128)(2,1)S(1)}, bf16[192,3200]{1,0:T(8,128)(2,1)S(1)}, u32[]{:S(2)}, u32[]{:S(2)}) collective-permute-start(bf16[192,3200]{1,0:T(8,128)(2,1)S(1)} %collective-permute-done.5.refs_0_), channel_id=1, source_target_pairs={{0,1},{1,0},{2,3},{3,2},{4,5},{5,4},{6,7},{7,6},{8,9},{9,8},{10,11... | collective-permute-start | bytes 3686408 | tf_op jit(solution)/shard_map/ppermute | solution.py:215
  95.7 13.1 %collective-permute-start.7 = (bf16[192,1152]{1,0:T(8,128)(2,1)S(1)}, bf16[192,1152]{1,0:T(8,128)(2,1)S(1)}, u32[]{:S(2)}, u32[]{:S(2)}) collective-permute-start(bf16[192,1152]{1,0:T(8,128)(2,1)S(1)} %slice.6), channel_id=1, source_target_pairs={{0,2},{1,3},{2,0},{3,1},{4,6},{5,7},{6,4},{7,5},{8,10},{9,11},{10,... | collective-permute-start | bytes 1327112 | tf_op jit(solution)/shard_map/ppermute | solution.py:215
  97.2 22.7 %collective-permute-start.10 = (bf16[192,2048]{1,0:T(8,128)(2,1)}, bf16[192,2048]{1,0:T(8,128)(2,1)S(1)}, u32[]{:S(2)}, u32[]{:S(2)}) collective-permute-start(bf16[192,2048]{1,0:T(8,128)(2,1)} %collective-permute-done.9.refs_2_), channel_id=1, source_target_pairs={{0,1},{1,0},{2,3},{3,2},{4,5},{5,4},{6,7},{7,6},{8,9},{9,8},{10,11... | collective-permute-start | bytes 2359304 | tf_op jit(solution)/shard_map/ppermute | solution.py:215
  108.8 11.1 %copy-start.3 = (bf16[192,1152]{1,0:T(8,128)(2,1)}, bf16[192,1152]{1,0:T(8,128)(2,1)S(1)}, u32[]{:S(2)}) copy-start(bf16[192,1152]{1,0:T(8,128)(2,1)S(1)} %collective-permute-done.7.refs_2_) | copy-start | bytes 1327108
  108.8 20.4 %collective-permute-start.8 = (bf16[192,1152]{1,0:T(8,128)(2,1)S(1)}, bf16[192,1152]{1,0:T(8,128)(2,1)S(1)}, u32[]{:S(2)}, u32[]{:S(2)}) collective-permute-start(bf16[192,1152]{1,0:T(8,128)(2,1)S(1)} %collective-permute-done.7.refs_2_), channel_id=1, source_target_pairs={{0,1},{1,0},{2,3},{3,2},{4,5},{5,4},{6,7},{7,6},{8,9},{9,8},{10,11... | collective-permute-start | bytes 1327112 | tf_op jit(solution)/shard_map/ppermute | solution.py:215
  119.9 0.9 copy-start.2
  119.9 1.3 copy-start.1
  129.2 0.8 copy-start.4

commit v3 on v2

v3 whole, which is shorter than its diff:
```python
import functools

import jax
import jax.numpy as jnp
from jax import lax
from jax.experimental import pallas as pl
from jax.experimental.pallas import tpu as pltpu
from jax.sharding import PartitionSpec as P

BAND = 3
AXES = ("feat", "frames")
F32, BF16 = jnp.float32, jnp.bfloat16
CHUNK = 512
VMEM = 32 << 20


def spans(first, last):
    return [(c, min(CHUNK, last - c)) for c in range(first, last, CHUNK)]


def center(sources, out, cols):
    frames = out.shape[0]
    part = sources[0].shape[0]
    groups = [(j, r) for j in range(len(sources)) for r in range(0, part, 16)]
    total = jnp.zeros((8, cols.size), F32)
    for j, r in groups:
        x = sources[j][pl.ds(r, 16), cols].astype(F32)
        total = total + (x[:8] + x[8:])
    mean = jnp.sum(total, axis=0, keepdims=True) / frames
    for j, r in groups:
        x = sources[j][pl.ds(r, 16), cols].astype(F32)
        out[pl.ds(j * part + r, 16), cols] = (x - mean).astype(BF16)


def start_loads(places, pieces, raw, sems, first, last):
    part = raw.shape[0] // 4
    copies = []
    for flip, base, j in places:
        piece = pieces[j]
        begin, end = max(base, first), min(base + piece.shape[1], last)
        copy = pltpu.make_async_copy(
            piece.at[:, pl.ds(begin - base, end - begin)],
            raw.at[pl.ds(flip * part, part), pl.ds(begin - first, end - begin)],
            sems.at[j],
        )
        copy.start()
        copies.append(copy)
    return copies


def product(k, y, cent, tile, out, factor, c, w, first, sem):
    here = pl.ds(c - first, w)
    total = jnp.dot(y, cent[:, here], preferred_element_type=F32)
    tile[:, here] = (total * factor).astype(BF16)
    store = pltpu.make_async_copy(tile.at[:, here], out.at[k, :, pl.ds(c, w)], sem)
    store.start()
    return store


def border(ids, value, frames):
    def halve(_, span):
        low, high = span
        mid = lax.min((low + high) // 2, frames - 1)
        before = jnp.logical_and(low < high, ids[mid] < value)
        after_ = jnp.logical_and(low < high, jnp.logical_not(before))
        return lax.select(before, mid + 1, low), lax.select(after_, mid, high)

    steps = frames.bit_length()
    return lax.fori_loop(0, steps, halve, (jnp.int32(0), jnp.int32(frames)))[0]


def codes(shape, axis, f, borders):
    row = lax.broadcasted_iota(jnp.int32, shape, axis)
    part = max(shape) // 4
    code = row
    for flip in range(4):
        shift = (lax.bitwise_xor(f, flip) - flip) * part
        here = jnp.logical_and(row >= flip * part, row < (flip + 1) * part)
        code = jnp.where(here, row + shift, code)
    frame = code
    for at in borders:
        code = code + jnp.where(frame >= at, 4096, 0)
    return code


def first_kernel(places, frames, n, me_ref, lag_ref, ids_ref, *refs):
    pieces = refs[:n]
    out, y_out = refs[n], refs[n + 1]
    raw, cent, tile, lagged, in_sems, out_sems = refs[n + 2:]
    f = me_ref[0]
    width = raw.shape[1]
    quarter = width // 4
    copies = start_loads(places, pieces, raw, in_sems, 0, width)
    for copy in copies:
        copy.wait()
    for c, w in spans(0, width):
        center([raw], cent, pl.ds(c, w))
    begin = f * quarter
    aligned = pl.multiple_of((begin // 128) * 128, 128)
    window = lagged.shape[0]
    rest = pl.multiple_of(begin - aligned, 32)
    mine = cent[:, pl.ds(aligned, window)].T
    borders = [border(ids_ref, value, frames) for value in (1, 2, 3)]
    gap = codes((1, frames), 1, f, borders) - codes((frames, 1), 0, f, borders)
    for k in range(BAND):
        lag = lag_ref[k]
        ahead = jnp.where(gap == lag, 1.0, 0.0)
        back = jnp.where(gap == -lag, 1.0, 0.0)
        pair = (ahead + back).astype(BF16)
        lagged[...] = jnp.dot(mine, pair, preferred_element_type=F32)
        y_out[k] = lagged[pl.ds(rest, quarter), :].astype(BF16)
    factor = 0.5 / (frames - lag_ref[0]).astype(F32)
    stores = [
        product(0, y_out[0], cent, tile, out, factor, c, w, 0, out_sems.at[i])
        for i, (c, w) in enumerate(spans(0, width))
    ]
    for store in stores:
        store.wait()


SMEM_SPEC = pl.BlockSpec(memory_space=pltpu.SMEM)
VMEM_SPEC = pl.BlockSpec(memory_space=pltpu.VMEM)
HBM_SPEC = pl.BlockSpec(memory_space=pl.ANY)


def cost(frames, quarter, columns, extra=0):
    return pl.CostEstimate(
        flops=2 * frames * quarter * (2 * columns + extra),
        bytes_accessed=2 * columns * (frames + quarter),
        transcendentals=0,
    )


def listed(placed):
    places = [(flip, base, j) for j, (flip, base, _) in enumerate(placed)]
    return places, [array for _, _, array in placed]


def first_tile(me, lags, ids, placed, frames):
    places, pieces = listed(placed)
    width = pieces[0].shape[1]
    quarter = width // 4
    n, count = len(pieces), len(spans(0, width))
    window = -(-(quarter + 96) // 128) * 128
    return pl.pallas_call(
        functools.partial(first_kernel, places, frames, n),
        out_shape=(
            jax.ShapeDtypeStruct((BAND, quarter, width), BF16),
            jax.ShapeDtypeStruct((BAND, quarter, frames), BF16),
        ),
        in_specs=[SMEM_SPEC] * 3 + [HBM_SPEC] * n,
        out_specs=(HBM_SPEC, VMEM_SPEC),
        scratch_shapes=[
            pltpu.VMEM((frames, width), BF16),
            pltpu.VMEM((frames, width), BF16),
            pltpu.VMEM((quarter, width), BF16),
            pltpu.VMEM((window, frames), F32),
            pltpu.SemaphoreType.DMA((n,)),
            pltpu.SemaphoreType.DMA((count,)),
        ],
        compiler_params=pltpu.CompilerParams(vmem_limit_bytes=VMEM),
        cost_estimate=cost(frames, quarter, width, 3 * frames),
        name="first_tile",
    )(me, lags, ids, *pieces)


def later_kernel(k, places, frames, n, first, last, resident, lags, y_in, *refs):
    pieces = refs[:n]
    out = refs[n + 1]
    cent, tile, y, lag_ref, y_sem, lag_sem, out_sems = refs[n + 2:n + 9]
    lag_copy = pltpu.make_async_copy(lags, lag_ref, lag_sem)
    lag_copy.start()
    y_copy = pltpu.make_async_copy(y_in.at[k], y, y_sem)
    y_copy.start()
    if resident:
        sources, copies = pieces, []
    else:
        raw, in_sems = refs[n + 9:]
        sources = [raw]
        copies = start_loads(places, pieces, raw, in_sems, first, last)
    steps = spans(first, last)
    stores = []
    for copy in copies:
        copy.wait()
    y_copy.wait()
    lag_copy.wait()
    factor = 0.5 / (frames - lag_ref[k]).astype(F32)
    for i in range(len(steps) + 1):
        if i < len(steps):
            c, w = steps[i]
            center(sources, cent, pl.ds(c - first, w))
        if i > 0:
            c, w = steps[i - 1]
            stores.append(
                product(k, y[...], cent, tile, out, factor, c, w, first, out_sems.at[i - 1])
            )
    for store in stores:
        store.wait()


def later_tile(k, lags, y, placed, tiles, frames, first, last, resident=False):
    places, pieces = listed(placed)
    columns = last - first
    quarter = tiles.shape[1]
    n, count = len(pieces), len(spans(first, last))
    scratch = [
        pltpu.VMEM((frames, columns), BF16),
        pltpu.VMEM((quarter, columns), BF16),
        pltpu.VMEM((quarter, frames), BF16),
        pltpu.SMEM((BAND,), jnp.int32),
        pltpu.SemaphoreType.DMA,
        pltpu.SemaphoreType.DMA,
        pltpu.SemaphoreType.DMA((count,)),
    ]
    if not resident:
        scratch += [pltpu.VMEM((frames, columns), BF16), pltpu.SemaphoreType.DMA((n,))]
    piece_spec = VMEM_SPEC if resident else HBM_SPEC
    return pl.pallas_call(
        functools.partial(later_kernel, k, places, frames, n, first, last, resident),
        out_shape=jax.ShapeDtypeStruct(tiles.shape, tiles.dtype),
        in_specs=[HBM_SPEC] * 2 + [piece_spec] * n + [HBM_SPEC],
        out_specs=HBM_SPEC,
        scratch_shapes=scratch,
        input_output_aliases={2 + n: 0},
        compiler_params=pltpu.CompilerParams(vmem_limit_bytes=VMEM),
        cost_estimate=cost(frames, quarter, columns),
        name="later_tile",
    )(lags, y, *pieces, tiles)


def after(array, *done):
    return lax.optimization_barrier((array, *done))[0]


def local(trajectory, segment_ids, lag_frames):
    blocks_n, parts = lax.axis_size("feat"), lax.axis_size("frames")
    frames = segment_ids.shape[0]
    width = trajectory.shape[1]
    half = blocks_n // 2
    me = lax.axis_index("frames").astype(jnp.int32).reshape(1)

    def move(array, to):
        route = []
        for b in range(blocks_n):
            for f in range(parts):
                to_b, to_f = to(b, f)
                route.append((b * parts + f, to_b * parts + to_f))
        return lax.ppermute(array, AXES, route)

    def wraps(b, k):
        return b % half >= half - k

    def core(array):
        return move(array, lambda b, f: (b, f ^ 1))

    def ring(array, k):
        return move(array, lambda b, f: (b - b % half + (b - k) % half, f))

    def wrap(array, k):
        route = [
            (b * parts + f, (b + half) % blocks_n * parts + f)
            for b in range(blocks_n) for f in range(parts) if wraps(b, k)
        ]
        return lax.ppermute(array, AXES, route)

    def straight(array, wrapped, k):
        return jnp.where(wraps(lax.axis_index("feat"), k), wrapped, array)

    def cross(array, k):
        return move(array, lambda b, f: ((b + half * wraps(b, k)) % blocks_n, f ^ 2))

    own = trajectory
    own_core = core(own)
    across = cross(own, 0)
    next_ring = ring(own, 1)
    after_ring = ring(after(own, next_ring), 2)
    next_across = cross(next_ring, 1)
    next_wrap = wrap(next_ring, 1)
    across_core = core(across)
    tiles, y = first_tile(
        me, lag_frames, segment_ids,
        [(0, 0, own), (1, 0, own_core), (2, 0, across), (3, 0, across_core)], frames,
    )
    next_across, next_wrap = lax.optimization_barrier((next_across, next_wrap, y))[:2]
    after_ring = after(after_ring, y)
    after_across = cross(after_ring, 2)
    after_wrap = wrap(after_ring, 2)
    next_own = straight(next_ring, next_wrap, 1)
    next_core = core(next_own)
    next_across_core = core(next_across)
    tiles = later_tile(
        1, lag_frames, y,
        [(0, 0, next_own), (1, 0, next_core), (2, 0, next_across), (3, 0, next_across_core)],
        tiles, frames, 0, width,
    )
    after_across, after_wrap, tiles = lax.optimization_barrier((after_across, after_wrap, tiles))
    after_across_core = core(after_across)
    after_own = straight(after_ring, after_wrap, 2)
    after_core = core(after_own)
    return later_tile(
        2, lag_frames, y,
        [(0, 0, after_own), (1, 0, after_core), (2, 0, after_across), (3, 0, after_across_core)],
        tiles, frames, 0, width, True,
    )


def solution(mesh):
    return jax.shard_map(
        local,
        mesh=mesh,
        in_specs=(P("frames", "feat"), P(), P()),
        out_specs=P(None, ("feat", "frames"), None),
        check_vma=False,
    )
```

time: 137 us -> 116 us (0.85)
  Pallas kernels: 40.6 us -> 30.1 us
  waiting for transfers between devices: 68.6 us -> 58.1 us
  starting transfers between devices: 22.3 us -> 19.4 us
  other arithmetic: 0 us -> 2.86 us
    ppermute x15 -> x11, waiting for transfers between devices: 68.6 us -> 54.6 us  [move(): return lax.ppermute(array, AXES, route)]
    pallas_call x3 -> x2, Pallas kernels: 25 us -> 15.7 us  [later_tile(): pl.pallas_call(functools.partial(later_kernel, k, places, frames, n, firs...]
    ppermute x15 -> x11, starting transfers between devices: 22.3 us -> 15.4 us  [move(): return lax.ppermute(array, AXES, route)]
    ppermute x0 -> x2, starting transfers between devices: none -> 4 us  [wrap(): return lax.ppermute(array, AXES, route)]
    ppermute x0 -> x2, waiting for transfers between devices: none -> 3.46 us  [wrap(): return lax.ppermute(array, AXES, route)]
    broadcast_in_dim x2 -> x0, local copies, waits for them, and re-layouts: 2.87 us -> none  [the longest x1 1.59 us: first_tile(): ids[:, None]]
    select_n x0 -> x2, other arithmetic: none -> 2.86 us  [straight(): return jnp.where(wraps(lax.axis_index('feat'), k), wrapped, array)]
    unnamed x10 -> x12, local copies, waits for them, and re-layouts: 2.09 us -> 4.67 us
  transfers between devices with their start and end apart: 15 -> 13, of which waited for: 5 -> 9; matrix products, arithmetic and copies ran while one was open for 2% -> 1% of each run, Pallas kernels for 25% -> 19%
where the time goes in v3:
time: 116 us; the launch traced here: 115 us
  waiting for transfers between devices  58.1 us (50%)
  Pallas kernels  30.1 us (26%)
  starting transfers between devices  19.4 us (17%)
  local copies, waits for them, and re-layouts  4.67 us (4%)
  other arithmetic  2.86 us (2%)
    ppermute x11, waiting for transfers between devices, move(): return lax.ppermute(array, AXES, route)  54.6 us
    pallas_call x2, Pallas kernels, later_tile(): pl.pallas_call(functools.partial(later_kernel, k, places, frames, n, firs...  15.7 us
    ppermute x11, starting transfers between devices, move(): return lax.ppermute(array, AXES, route)  15.4 us
    pallas_call x1, Pallas kernels, first_tile(): pl.pallas_call(functools.partial(first_kernel, places, frames, n), out_sh...  14.4 us
    unnamed x12, local copies, waits for them, and re-layouts  4.67 us
    ppermute x2, starting transfers between devices, wrap(): return lax.ppermute(array, AXES, route)  4 us
    ppermute x2, waiting for transfers between devices, wrap(): return lax.ppermute(array, AXES, route)  3.46 us
    select_n x2, other arithmetic, straight(): return jnp.where(wraps(lax.axis_index('feat'), k), wrapped, array)  2.86 us
  transfers between devices with their start and end apart: 13, of which 9 were waited for; matrix products, arithmetic and copies ran while one was open for 1% of the time, Pallas kernels for 19%

profile of v3, /device:TPU:121, one launch (start us, length us, event | category | flops | bytes accessed | tf_op | source)
XLA Modules:
  0.0 115.3 jit_solution(4033826933095738875)
XLA Ops:
  0.0 2.7 %collective-permute-start.1 = (bf16[192,3200]{1,0:T(8,128)(2,1)}, bf16[192,3200]{1,0:T(8,128)(2,1)S(1)}, u32[]{:S(2)}, u32[]{:S(2)}) collective-permute-start(bf16[192,3200]{1,0:T(8,128)(2,1)} %refs_0_.1), channel_id=1, source_target_pairs={{0,2},{1,3},{2,0},{3,1},{4,6},{5,7},{6,4},{7,5},{8,10},{9,11},{10,... | collective-permute-start | bytes 3686408 | tf_op jit(solution)/shard_map/ppermute | solution.py:248
  2.7 0.5 collective-permute-start.3
  3.2 1.2 %collective-permute-start = (bf16[192,3200]{1,0:T(8,128)(2,1)}, bf16[192,3200]{1,0:T(8,128)(2,1)}, u32[]{:S(2)}, u32[]{:S(2)}) collective-permute-start(bf16[192,3200]{1,0:T(8,128)(2,1)} %refs_0_.1), channel_id=1, source_target_pairs={{0,1},{1,0},{2,3},{3,2},{4,5},{5,4},{6,7},{7,6},{8,9},{9,8},{10,11... | collective-permute-start | bytes 3686408 | tf_op jit(solution)/shard_map/ppermute | solution.py:248
  4.4 25.3 %collective-permute-done.1.refs_2_ = bf16[192,3200]{1,0:T(8,128)(2,1)S(1)} collective-permute-done((bf16[192,3200]{1,0:T(8,128)(2,1)}, bf16[192,3200]{1,0:T(8,128)(2,1)S(1)}, u32[]{:S(2)}, u32[]{:S(2)}) %collective-permute-start.1) | collective-permute-done | bytes 1228832 | tf_op jit(solution)/shard_map/ppermute | solution.py:248
  29.7 1.4 %collective-permute-start.2 = (bf16[192,3200]{1,0:T(8,128)(2,1)S(1)}, bf16[192,3200]{1,0:T(8,128)(2,1)}, u32[]{:S(2)}, u32[]{:S(2)}) collective-permute-start(bf16[192,3200]{1,0:T(8,128)(2,1)S(1)} %collective-permute-done.1.refs_2_), channel_id=1, source_target_pairs={{0,1},{1,0},{2,3},{3,2},{4,5},{5,4},{6,7},{7,6},{8,9},{9,8},{10,11... | collective-permute-start | bytes 3686408 | tf_op jit(solution)/shard_map/ppermute | solution.py:248
  31.2 2.8 %collective-permute-done.3 = bf16[192,3200]{1,0:T(8,128)(2,1)} collective-permute-done((bf16[192,3200]{1,0:T(8,128)(2,1)}, bf16[192,3200]{1,0:T(8,128)(2,1)}, u32[]{:S(2)}, u32[]{:S(2)}) %collective-permute-start.3) | collective-permute-done | bytes 1228832 | tf_op jit(solution)/shard_map/ppermute | solution.py:248
  34.0 0.9 collective-permute-start.7
  34.8 1.9 %collective-permute-start.8 = (bf16[192,3200]{1,0:T(8,128)(2,1)}, bf16[192,3200]{1,0:T(8,128)(2,1)}, u32[]{:S(2)}, u32[]{:S(2)}) collective-permute-start(bf16[192,3200]{1,0:T(8,128)(2,1)} %collective-permute-done.3), channel_id=1, source_target_pairs={{60,124},{61,125},{62,126},{63,127},{124,60},{125,61},{126,62},{12... | collective-permute-start | bytes 3686408 | tf_op jit(solution)/shard_map/ppermute | solution.py:264
  36.7 0.1 collective-permute-start.4
  36.8 0.0 collective-permute-done.refs_1_
  36.8 0.0 collective-permute-done.2.refs_3_
  36.9 0.0 copy-start.2
  36.9 0.6 copy-done.2
  37.5 0.0 copy-start.4
  37.5 1.3 %copy-done.4 = bf16[192,3200]{1,0:T(8,128)(2,1)S(1)} copy-done((bf16[192,3200]{1,0:T(8,128)(2,1)S(1)}, bf16[192,3200]{1,0:T(8,128)(2,1)}, u32[]{:S(2)}) %copy-start.4) | copy-done | bytes 1228824
  38.8 0.0 copy-start.5
  38.8 0.7 copy-done.5
  39.5 14.4 %first_tile.1 = (bf16[3,800,3200]{2,1,0:T(8,128)(2,1)}, bf16[3,800,768]{2,1,0:T(8,128)(2,1)S(1)}) custom-call(s32[1]{0:T(128)} %bitcast.me_ref, s32[3]{0:T(128)S(1)} %copy-done.2, s32[768]{0:T(1024)S(1)} %copy-done.5, bf16[192,3200]{1,0:T(8,128)(2,1)S(1)} %copy-done.4, bf16[192,3200]{1,0:T(8,128)(2,1)} %collective-permute-done.refs_1_, ...), custom_call_target="tpu_custom_call" | custom-call | flops 10695475200 | bytes 10035200 | tf_op jit(solution)/shard_map/first_tile/pallas_call | solution.py:145
  53.9 0.0 copy-start
  53.9 8.2 %collective-permute-done.7.refs_2_ = bf16[192,3200]{1,0:T(8,128)(2,1)S(1)} collective-permute-done((bf16[192,3200]{1,0:T(8,128)(2,1)}, bf16[192,3200]{1,0:T(8,128)(2,1)S(1)}, u32[]{:S(2)}, u32[]{:S(2)}) %collective-permute-start.7) | collective-permute-done | bytes 1228832 | tf_op jit(solution)/shard_map/ppermute | solution.py:248
  62.1 1.3 %collective-permute-done.8 = bf16[192,3200]{1,0:T(8,128)(2,1)} collective-permute-done((bf16[192,3200]{1,0:T(8,128)(2,1)}, bf16[192,3200]{1,0:T(8,128)(2,1)}, u32[]{:S(2)}, u32[]{:S(2)}) %collective-permute-start.8) | collective-permute-done | bytes 1228832 | tf_op jit(solution)/shard_map/ppermute | solution.py:264
  63.4 0.0 copy-start.3
  63.4 1.4 %broadcast_select_fusion.refs_0_ = bf16[192,3200]{1,0:T(8,128)(2,1)S(1)} fusion(bf16[192,3200]{1,0:T(8,128)(2,1)} %collective-permute-done.8, bf16[192,3200]{1,0:T(8,128)(2,1)} %collective-permute-done.3, pred[]{:T(512)S(6)} %ge.7), kind=kLoop, calls=%fused_computation | loop fusion | flops 614400 | bytes 3686401 | tf_op jit(solution)/shard_map/jit(_where)/select_n | solution.py:267
  64.8 0.0 copy-done
  64.8 3.1 %collective-permute-start.9 = (bf16[192,3200]{1,0:T(8,128)(2,1)S(1)}, bf16[192,3200]{1,0:T(8,128)(2,1)}, u32[]{:S(2)}, u32[]{:S(2)}) collective-permute-start(bf16[192,3200]{1,0:T(8,128)(2,1)S(1)} %broadcast_select_fusion.refs_0_), channel_id=1, source_target_pairs={{0,1},{1,0},{2,3},{3,2},{4,5},{5,4},{6,7},{7,6},{8,9},{9,8},{10,11... | collective-permute-start | bytes 3686408 | tf_op jit(solution)/shard_map/ppermute | solution.py:248
  68.0 0.1 collective-permute-start.10
  68.1 0.0 collective-permute-done.4
  68.1 1.8 %collective-permute-start.5 = (bf16[192,3200]{1,0:T(8,128)(2,1)}, bf16[192,3200]{1,0:T(8,128)(2,1)}, u32[]{:S(2)}, u32[]{:S(2)}) collective-permute-start(bf16[192,3200]{1,0:T(8,128)(2,1)} %collective-permute-done.4), channel_id=1, source_target_pairs={{0,2},{1,3},{2,0},{3,1},{4,6},{5,7},{6,4},{7,5},{8,10},{9,11},{10,... | collective-permute-start | bytes 3686408 | tf_op jit(solution)/shard_map/ppermute | solution.py:248
  69.9 2.1 %collective-permute-start.6 = (bf16[192,3200]{1,0:T(8,128)(2,1)}, bf16[192,3200]{1,0:T(8,128)(2,1)}, u32[]{:S(2)}, u32[]{:S(2)}) collective-permute-start(bf16[192,3200]{1,0:T(8,128)(2,1)} %collective-permute-done.4), channel_id=1, source_target_pairs={{56,120},{57,121},{58,122},{59,123},{60,124},{61,125},{62,126},{63... | collective-permute-start | bytes 3686408 | tf_op jit(solution)/shard_map/ppermute | solution.py:264
  72.0 0.0 collective-permute-done.9.refs_1_
  72.0 0.4 collective-permute-done.10.refs_3_
  72.4 0.0 copy-done.3
  72.4 0.0 copy-start.1
  72.4 2.0 %copy-done.1 = bf16[3,800,768]{2,1,0:T(8,128)(2,1)S(1)} copy-done((bf16[3,800,768]{2,1,0:T(8,128)(2,1)S(1)}, bf16[3,800,768]{2,1,0:T(8,128)(2,1)}, u32[]{:S(2)}) %copy-start.1) | copy-done | bytes 3686424
  74.5 8.1 %later_tile.2.refs_4_ = bf16[3,800,3200]{2,1,0:T(8,128)(2,1)} custom-call(s32[3]{0:T(128)S(1)} %copy-done.3, bf16[3,800,768]{2,1,0:T(8,128)(2,1)S(1)} %copy-done.1, bf16[192,3200]{1,0:T(8,128)(2,1)S(1)} %broadcast_select_fusion.refs_0_, bf16[192,3200]{1,0:T(8,128)(2,1)} %collective-permute-done.9.refs_1_, ...), custom_call_target="tpu_custom_call", output_to_operand_aliasing={{}: (6, {})} | custom-call | flops 7864320000 | bytes 10035200 | tf_op jit(solution)/shard_map/later_tile/pallas_call | solution.py:218
  82.5 13.5 %collective-permute-done.5.refs_2_ = bf16[192,3200]{1,0:T(8,128)(2,1)} collective-permute-done((bf16[192,3200]{1,0:T(8,128)(2,1)}, bf16[192,3200]{1,0:T(8,128)(2,1)}, u32[]{:S(2)}, u32[]{:S(2)}) %collective-permute-start.5) | collective-permute-done | bytes 1228832 | tf_op jit(solution)/shard_map/ppermute | solution.py:248
  96.0 2.2 %collective-permute-done.6 = bf16[192,3200]{1,0:T(8,128)(2,1)} collective-permute-done((bf16[192,3200]{1,0:T(8,128)(2,1)}, bf16[192,3200]{1,0:T(8,128)(2,1)}, u32[]{:S(2)}, u32[]{:S(2)}) %collective-permute-start.6) | collective-permute-done | bytes 1228832 | tf_op jit(solution)/shard_map/ppermute | solution.py:264
  98.2 1.4 %broadcast_select_fusion.1.refs_0_ = bf16[192,3200]{1,0:T(8,128)(2,1)S(1)} fusion(bf16[192,3200]{1,0:T(8,128)(2,1)} %collective-permute-done.6, bf16[192,3200]{1,0:T(8,128)(2,1)} %collective-permute-done.4, pred[]{:T(512)S(6)} %ge.6), kind=kLoop, calls=%fused_computation.1 | loop fusion | flops 614400 | bytes 3686401 | tf_op jit(solution)/shard_map/jit(_where)/select_n | solution.py:267
  99.6 3.4 %collective-permute-start.11 = (bf16[192,3200]{1,0:T(8,128)(2,1)S(1)}, bf16[192,3200]{1,0:T(8,128)(2,1)S(1)}, u32[]{:S(2)}, u32[]{:S(2)}) collective-permute-start(bf16[192,3200]{1,0:T(8,128)(2,1)S(1)} %broadcast_select_fusion.1.refs_0_), channel_id=1, source_target_pairs={{0,1},{1,0},{2,3},{3,2},{4,5},{5,4},{6,7},{7,6},{8,9},{9,8},{10,11... | collective-permute-start | bytes 3686408 | tf_op jit(solution)/shard_map/ppermute | solution.py:248
  103.0 0.1 collective-permute-start.12
  103.1 3.3 %collective-permute-done.11.refs_1_ = bf16[192,3200]{1,0:T(8,128)(2,1)S(1)} collective-permute-done((bf16[192,3200]{1,0:T(8,128)(2,1)S(1)}, bf16[192,3200]{1,0:T(8,128)(2,1)S(1)}, u32[]{:S(2)}, u32[]{:S(2)}) %collective-permute-start.11) | collective-permute-done | bytes 1228832 | tf_op jit(solution)/shard_map/ppermute | solution.py:248
  106.4 1.1 collective-permute-done.12.refs_3_
  107.5 7.6 %later_tile.3 = bf16[3,800,3200]{2,1,0:T(8,128)(2,1)} custom-call(s32[3]{0:T(128)S(1)} %copy-done.3, bf16[3,800,768]{2,1,0:T(8,128)(2,1)S(1)} %copy-done.1, bf16[192,3200]{1,0:T(8,128)(2,1)S(1)} %broadcast_select_fusion.1.refs_0_, bf16[192,3200]{1,0:T(8,128)(2,1)S(1)} %collective-permute-done.11.refs_1_, ...), custom_call_target="tpu_custom_call", output_to_operand_aliasing={{}: (6, {})} | custom-call | flops 7864320000 | bytes 10035200 | tf_op jit(solution)/shard_map/later_tile/pallas_call | solution.py:218
Async XLA Ops:
  0.0 29.7 %collective-permute-start.1 = (bf16[192,3200]{1,0:T(8,128)(2,1)}, bf16[192,3200]{1,0:T(8,128)(2,1)S(1)}, u32[]{:S(2)}, u32[]{:S(2)}) collective-permute-start(bf16[192,3200]{1,0:T(8,128)(2,1)} %refs_0_.1), channel_id=1, source_target_pairs={{0,2},{1,3},{2,0},{3,1},{4,6},{5,7},{6,4},{7,5},{8,10},{9,11},{10,... | collective-permute-start | bytes 3686408 | tf_op jit(solution)/shard_map/ppermute | solution.py:248
  2.7 31.2 %collective-permute-start.3 = (bf16[192,3200]{1,0:T(8,128)(2,1)}, bf16[192,3200]{1,0:T(8,128)(2,1)}, u32[]{:S(2)}, u32[]{:S(2)}) collective-permute-start(bf16[192,3200]{1,0:T(8,128)(2,1)} %refs_0_.1), channel_id=1, source_target_pairs={{0,60},{1,61},{2,62},{3,63},{4,0},{5,1},{6,2},{7,3},{8,4},{9,5},{1... | collective-permute-start | bytes 3686408 | tf_op jit(solution)/shard_map/ppermute | solution.py:248
  3.2 33.6 %collective-permute-start = (bf16[192,3200]{1,0:T(8,128)(2,1)}, bf16[192,3200]{1,0:T(8,128)(2,1)}, u32[]{:S(2)}, u32[]{:S(2)}) collective-permute-start(bf16[192,3200]{1,0:T(8,128)(2,1)} %refs_0_.1), channel_id=1, source_target_pairs={{0,1},{1,0},{2,3},{3,2},{4,5},{5,4},{6,7},{7,6},{8,9},{9,8},{10,11... | collective-permute-start | bytes 3686408 | tf_op jit(solution)/shard_map/ppermute | solution.py:248
  29.7 7.1 %collective-permute-start.2 = (bf16[192,3200]{1,0:T(8,128)(2,1)S(1)}, bf16[192,3200]{1,0:T(8,128)(2,1)}, u32[]{:S(2)}, u32[]{:S(2)}) collective-permute-start(bf16[192,3200]{1,0:T(8,128)(2,1)S(1)} %collective-permute-done.1.refs_2_), channel_id=1, source_target_pairs={{0,1},{1,0},{2,3},{3,2},{4,5},{5,4},{6,7},{7,6},{8,9},{9,8},{10,11... | collective-permute-start | bytes 3686408 | tf_op jit(solution)/shard_map/ppermute | solution.py:248
  34.0 28.2 %collective-permute-start.7 = (bf16[192,3200]{1,0:T(8,128)(2,1)}, bf16[192,3200]{1,0:T(8,128)(2,1)S(1)}, u32[]{:S(2)}, u32[]{:S(2)}) collective-permute-start(bf16[192,3200]{1,0:T(8,128)(2,1)} %collective-permute-done.3), channel_id=1, source_target_pairs={{0,2},{1,3},{2,0},{3,1},{4,6},{5,7},{6,4},{7,5},{8,10},{9,11},{10,... | collective-permute-start | bytes 3686408 | tf_op jit(solution)/shard_map/ppermute | solution.py:248
  34.8 28.6 %collective-permute-start.8 = (bf16[192,3200]{1,0:T(8,128)(2,1)}, bf16[192,3200]{1,0:T(8,128)(2,1)}, u32[]{:S(2)}, u32[]{:S(2)}) collective-permute-start(bf16[192,3200]{1,0:T(8,128)(2,1)} %collective-permute-done.3), channel_id=1, source_target_pairs={{60,124},{61,125},{62,126},{63,127},{124,60},{125,61},{126,62},{12... | collective-permute-start | bytes 3686408 | tf_op jit(solution)/shard_map/ppermute | solution.py:264
  36.7 31.3 %collective-permute-start.4 = (bf16[192,3200]{1,0:T(8,128)(2,1)}, bf16[192,3200]{1,0:T(8,128)(2,1)}, u32[]{:S(2)}, u32[]{:S(2)}) collective-permute-start(bf16[192,3200]{1,0:T(8,128)(2,1)} %refs_0_.1), channel_id=1, source_target_pairs={{0,56},{1,57},{2,58},{3,59},{4,60},{5,61},{6,62},{7,63},{8,0},{9,1... | collective-permute-start | bytes 3686408 | tf_op jit(solution)/shard_map/ppermute | solution.py:248
  36.9 0.7 copy-start.2
  37.5 1.3 %copy-start.4 = (bf16[192,3200]{1,0:T(8,128)(2,1)S(1)}, bf16[192,3200]{1,0:T(8,128)(2,1)}, u32[]{:S(2)}) copy-start(bf16[192,3200]{1,0:T(8,128)(2,1)} %refs_0_.1) | copy-start | bytes 3686404
  38.8 0.7 copy-start.5
  53.9 10.9 %copy-start = (bf16[3,800,768]{2,1,0:T(8,128)(2,1)}, bf16[3,800,768]{2,1,0:T(8,128)(2,1)S(1)}, u32[]{:S(2)}) copy-start(bf16[3,800,768]{2,1,0:T(8,128)(2,1)S(1)} %get-tuple-element.14.y_in) | copy-start | bytes 11059204
  63.4 9.0 %copy-start.3 = (s32[3]{0:T(128)S(1)}, s32[3]{0:T(128)}, u32[]{:S(2)}) copy-start(s32[3]{0:T(128)} %lags.3) | copy-start | bytes 40
  64.8 7.2 %collective-permute-start.9 = (bf16[192,3200]{1,0:T(8,128)(2,1)S(1)}, bf16[192,3200]{1,0:T(8,128)(2,1)}, u32[]{:S(2)}, u32[]{:S(2)}) collective-permute-start(bf16[192,3200]{1,0:T(8,128)(2,1)S(1)} %broadcast_select_fusion.refs_0_), channel_id=1, source_target_pairs={{0,1},{1,0},{2,3},{3,2},{4,5},{5,4},{6,7},{7,6},{8,9},{9,8},{10,11... | collective-permute-start | bytes 3686408 | tf_op jit(solution)/shard_map/ppermute | solution.py:248
  68.0 4.4 %collective-permute-start.10 = (bf16[192,3200]{1,0:T(8,128)(2,1)S(1)}, bf16[192,3200]{1,0:T(8,128)(2,1)}, u32[]{:S(2)}, u32[]{:S(2)}) collective-permute-start(bf16[192,3200]{1,0:T(8,128)(2,1)S(1)} %collective-permute-done.7.refs_2_), channel_id=1, source_target_pairs={{0,1},{1,0},{2,3},{3,2},{4,5},{5,4},{6,7},{7,6},{8,9},{9,8},{10,11... | collective-permute-start | bytes 3686408 | tf_op jit(solution)/shard_map/ppermute | solution.py:248
  68.1 27.9 %collective-permute-start.5 = (bf16[192,3200]{1,0:T(8,128)(2,1)}, bf16[192,3200]{1,0:T(8,128)(2,1)}, u32[]{:S(2)}, u32[]{:S(2)}) collective-permute-start(bf16[192,3200]{1,0:T(8,128)(2,1)} %collective-permute-done.4), channel_id=1, source_target_pairs={{0,2},{1,3},{2,0},{3,1},{4,6},{5,7},{6,4},{7,5},{8,10},{9,11},{10,... | collective-permute-start | bytes 3686408 | tf_op jit(solution)/shard_map/ppermute | solution.py:248
  69.9 28.3 %collective-permute-start.6 = (bf16[192,3200]{1,0:T(8,128)(2,1)}, bf16[192,3200]{1,0:T(8,128)(2,1)}, u32[]{:S(2)}, u32[]{:S(2)}) collective-permute-start(bf16[192,3200]{1,0:T(8,128)(2,1)} %collective-permute-done.4), channel_id=1, source_target_pairs={{56,120},{57,121},{58,122},{59,123},{60,124},{61,125},{62,126},{63... | collective-permute-start | bytes 3686408 | tf_op jit(solution)/shard_map/ppermute | solution.py:264
  72.4 2.0 %copy-start.1 = (bf16[3,800,768]{2,1,0:T(8,128)(2,1)S(1)}, bf16[3,800,768]{2,1,0:T(8,128)(2,1)}, u32[]{:S(2)}) copy-start(bf16[3,800,768]{2,1,0:T(8,128)(2,1)} %copy-done) | copy-start | bytes 11059204
  99.6 6.8 %collective-permute-start.11 = (bf16[192,3200]{1,0:T(8,128)(2,1)S(1)}, bf16[192,3200]{1,0:T(8,128)(2,1)S(1)}, u32[]{:S(2)}, u32[]{:S(2)}) collective-permute-start(bf16[192,3200]{1,0:T(8,128)(2,1)S(1)} %broadcast_select_fusion.1.refs_0_), channel_id=1, source_target_pairs={{0,1},{1,0},{2,3},{3,2},{4,5},{5,4},{6,7},{7,6},{8,9},{9,8},{10,11... | collective-permute-start | bytes 3686408 | tf_op jit(solution)/shard_map/ppermute | solution.py:248
  103.0 4.5 %collective-permute-start.12 = (bf16[192,3200]{1,0:T(8,128)(2,1)}, bf16[192,3200]{1,0:T(8,128)(2,1)S(1)}, u32[]{:S(2)}, u32[]{:S(2)}) collective-permute-start(bf16[192,3200]{1,0:T(8,128)(2,1)} %collective-permute-done.5.refs_2_), channel_id=1, source_target_pairs={{0,1},{1,0},{2,3},{3,2},{4,5},{5,4},{6,7},{7,6},{8,9},{9,8},{10,11... | collective-permute-start | bytes 3686408 | tf_op jit(solution)/shard_map/ppermute | solution.py:248

commit v4 on v3

--- a/solution.py
+++ b/solution.py
@@ -18,18 +18,29 @@
     return [(c, min(CHUNK, last - c)) for c in range(first, last, CHUNK)]
 
 
-def center(sources, out, cols):
+def center(sources, out, cols, wrapped=None):
     frames = out.shape[0]
-    part = sources[0].shape[0]
+    part = frames // len(sources)
     groups = [(j, r) for j in range(len(sources)) for r in range(0, part, 16)]
+
+    def get(j, r):
+        if not isinstance(sources[j], tuple):
+            return sources[j][pl.ds(r, 16), cols]
+        plain, other = (ref[pl.ds(r, 16), cols] for ref in sources[j])
+        return lax.select(wrapped, other, plain)
+
     total = jnp.zeros((8, cols.size), F32)
     for j, r in groups:
-        x = sources[j][pl.ds(r, 16), cols].astype(F32)
+        x = get(j, r)
+        if isinstance(sources[j], tuple):
+            out[pl.ds(j * part + r, 16), cols] = x
+        x = x.astype(F32)
         total = total + (x[:8] + x[8:])
     mean = jnp.sum(total, axis=0, keepdims=True) / frames
     for j, r in groups:
-        x = sources[j][pl.ds(r, 16), cols].astype(F32)
-        out[pl.ds(j * part + r, 16), cols] = (x - mean).astype(BF16)
+        there = pl.ds(j * part + r, 16)
+        x = out[there, cols] if isinstance(sources[j], tuple) else get(j, r)
+        out[there, cols] = (x.astype(F32) - mean).astype(BF16)
 
 
 def start_loads(places, pieces, raw, sems, first, last):
@@ -164,68 +175,47 @@
     )(me, lags, ids, *pieces)
 
 
-def later_kernel(k, places, frames, n, first, last, resident, lags, y_in, *refs):
-    pieces = refs[:n]
-    out = refs[n + 1]
-    cent, tile, y, lag_ref, y_sem, lag_sem, out_sems = refs[n + 2:n + 9]
-    lag_copy = pltpu.make_async_copy(lags, lag_ref, lag_sem)
-    lag_copy.start()
-    y_copy = pltpu.make_async_copy(y_in.at[k], y, y_sem)
-    y_copy.start()
-    if resident:
-        sources, copies = pieces, []
-    else:
-        raw, in_sems = refs[n + 9:]
-        sources = [raw]
-        copies = start_loads(places, pieces, raw, in_sems, first, last)
-    steps = spans(first, last)
+def later_kernel(k, frames, flags, y, *refs):
+    ring, beside, core_wrap, across, across_core = refs[:5]
+    out, cent, tile, flag, flag_sem, out_sems = refs[6:]
+    copy = pltpu.make_async_copy(flags, flag, flag_sem)
+    copy.start()
+    copy.wait()
+    wrapped = flag[BAND + k] > 0
+    sources = [(ring, beside), (beside, core_wrap), across, across_core]
+    factor = 0.5 / (frames - flag[k]).astype(F32)
+    steps = spans(0, tile.shape[1])
     stores = []
-    for copy in copies:
-        copy.wait()
-    y_copy.wait()
-    lag_copy.wait()
-    factor = 0.5 / (frames - lag_ref[k]).astype(F32)
     for i in range(len(steps) + 1):
         if i < len(steps):
-            c, w = steps[i]
-            center(sources, cent, pl.ds(c - first, w))
+            center(sources, cent, pl.ds(*steps[i]), wrapped)
         if i > 0:
             c, w = steps[i - 1]
-            stores.append(
-                product(k, y[...], cent, tile, out, factor, c, w, first, out_sems.at[i - 1])
-            )
+            stores.append(product(k, y[k], cent, tile, out, factor, c, w, 0, out_sems.at[i - 1]))
     for store in stores:
         store.wait()
 
 
-def later_tile(k, lags, y, placed, tiles, frames, first, last, resident=False):
-    places, pieces = listed(placed)
-    columns = last - first
-    quarter = tiles.shape[1]
-    n, count = len(pieces), len(spans(first, last))
-    scratch = [
-        pltpu.VMEM((frames, columns), BF16),
-        pltpu.VMEM((quarter, columns), BF16),
-        pltpu.VMEM((quarter, frames), BF16),
-        pltpu.SMEM((BAND,), jnp.int32),
-        pltpu.SemaphoreType.DMA,
-        pltpu.SemaphoreType.DMA,
-        pltpu.SemaphoreType.DMA((count,)),
-    ]
-    if not resident:
-        scratch += [pltpu.VMEM((frames, columns), BF16), pltpu.SemaphoreType.DMA((n,))]
-    piece_spec = VMEM_SPEC if resident else HBM_SPEC
+def later_tile(k, flags, y, pieces, tiles, frames):
+    quarter, width = tiles.shape[1:]
+    n, count = len(pieces), len(spans(0, width))
     return pl.pallas_call(
-        functools.partial(later_kernel, k, places, frames, n, first, last, resident),
+        functools.partial(later_kernel, k, frames),
         out_shape=jax.ShapeDtypeStruct(tiles.shape, tiles.dtype),
-        in_specs=[HBM_SPEC] * 2 + [piece_spec] * n + [HBM_SPEC],
+        in_specs=[HBM_SPEC] + [VMEM_SPEC] * (n + 1) + [HBM_SPEC],
         out_specs=HBM_SPEC,
-        scratch_shapes=scratch,
+        scratch_shapes=[
+            pltpu.VMEM((frames, width), BF16),
+            pltpu.VMEM((quarter, width), BF16),
+            pltpu.SMEM(flags.shape, jnp.int32),
+            pltpu.SemaphoreType.DMA,
+            pltpu.SemaphoreType.DMA((count,)),
+        ],
         input_output_aliases={2 + n: 0},
         compiler_params=pltpu.CompilerParams(vmem_limit_bytes=VMEM),
-        cost_estimate=cost(frames, quarter, columns),
+        cost_estimate=cost(frames, quarter, width),
         name="later_tile",
-    )(lags, y, *pieces, tiles)
+    )(flags, y, *pieces, tiles)
 
 
 def after(array, *done):
@@ -256,51 +246,54 @@
     def ring(array, k):
         return move(array, lambda b, f: (b - b % half + (b - k) % half, f))
 
-    def wrap(array, k):
+    def beside(array, k):
+        return move(array, lambda b, f: ((b + half) % blocks_n, f) if wraps(b, k) else (b, f ^ 1))
+
+    def swap_wrapped(array, k):
         route = [
-            (b * parts + f, (b + half) % blocks_n * parts + f)
+            (b * parts + f, b * parts + (f ^ 1))
             for b in range(blocks_n) for f in range(parts) if wraps(b, k)
         ]
         return lax.ppermute(array, AXES, route)
 
-    def straight(array, wrapped, k):
-        return jnp.where(wraps(lax.axis_index("feat"), k), wrapped, array)
-
     def cross(array, k):
         return move(array, lambda b, f: ((b + half * wraps(b, k)) % blocks_n, f ^ 2))
 
     own = trajectory
+    flags = jnp.concatenate([
+        lag_frames,
+        jnp.stack([wraps(lax.axis_index("feat"), k) for k in range(BAND)]).astype(jnp.int32),
+    ])
     own_core = core(own)
     across = cross(own, 0)
     next_ring = ring(own, 1)
-    after_ring = ring(after(own, next_ring), 2)
+    after_ring = ring(after(own, across), 2)
+    across_core = core(across)
     next_across = cross(next_ring, 1)
-    next_wrap = wrap(next_ring, 1)
-    across_core = core(across)
+    next_beside = beside(next_ring, 1)
     tiles, y = first_tile(
         me, lag_frames, segment_ids,
         [(0, 0, own), (1, 0, own_core), (2, 0, across), (3, 0, across_core)], frames,
     )
-    next_across, next_wrap = lax.optimization_barrier((next_across, next_wrap, y))[:2]
     after_ring = after(after_ring, y)
+    next_across, next_beside = lax.optimization_barrier((next_across, next_beside, y))[:2]
     after_across = cross(after_ring, 2)
-    after_wrap = wrap(after_ring, 2)
-    next_own = straight(next_ring, next_wrap, 1)
-    next_core = core(next_own)
+    after_beside = beside(after_ring, 2)
     next_across_core = core(next_across)
+    next_core_wrap = swap_wrapped(next_beside, 1)
     tiles = later_tile(
-        1, lag_frames, y,
-        [(0, 0, next_own), (1, 0, next_core), (2, 0, next_across), (3, 0, next_across_core)],
-        tiles, frames, 0, width,
-    )
-    after_across, after_wrap, tiles = lax.optimization_barrier((after_across, after_wrap, tiles))
+        1, flags, y,
+        [next_ring, next_beside, next_core_wrap, next_across, next_across_core], tiles, frames,
+    )
+    after_across, after_beside, tiles = lax.optimization_barrier(
+        (after_across, after_beside, tiles)
+    )
     after_across_core = core(after_across)
-    after_own = straight(after_ring, after_wrap, 2)
-    after_core = core(after_own)
+    after_core_wrap = swap_wrapped(after_beside, 2)
     return later_tile(
-        2, lag_frames, y,
-        [(0, 0, after_own), (1, 0, after_core), (2, 0, after_across), (3, 0, after_across_core)],
-        tiles, frames, 0, width, True,
+        2, flags, y,
+        [after_ring, after_beside, after_core_wrap, after_across, after_across_core],
+        tiles, frames,
     )
 
 

time: 116 us -> 112 us (0.966)
  other arithmetic: 2.86 us -> 0.15 us
  waiting for transfers between devices: 58.1 us -> 55.7 us
  local copies, waits for them, and re-layouts: 4.67 us -> 6.47 us
  Pallas kernels: 30.1 us -> 31.5 us
  starting transfers between devices: 19.4 us -> 18.1 us
    ppermute x11, starting transfers between devices: 15.4 us -> 11.8 us  [move(): return lax.ppermute(array, AXES, route)]
    ppermute x11, waiting for transfers between devices: 54.6 us -> 51.5 us  [move(): return lax.ppermute(array, AXES, route)]
    select_n x2 -> x0, other arithmetic: 2.86 us -> none  [straight(): return jnp.where(wraps(lax.axis_index('feat'), k), wrapped, array)]
    ppermute x2, starting transfers between devices: 4 us -> 6.34 us  [swap_wrapped(): return lax.ppermute(array, AXES, route)]
    unnamed x12, local copies, waits for them, and re-layouts: 4.67 us -> 6.47 us
    pallas_call x2, Pallas kernels: 15.7 us -> 16.9 us  [later_tile(): pl.pallas_call(functools.partial(later_kernel, k, frames), out_shape=jax....]
  transfers between devices with their start and end apart: 13 -> 13, of which waited for: 9 -> 7; matrix products, arithmetic and copies ran while one was open for 1% -> 0% of each run, Pallas kernels for 19% -> 21%
where the time goes in v4:
time: 112 us
  waiting for transfers between devices  55.7 us (50%)
  Pallas kernels  31.5 us (28%)
  starting transfers between devices  18.1 us (16%)
  local copies, waits for them, and re-layouts  6.47 us (6%)
    ppermute x11, waiting for transfers between devices, move(): return lax.ppermute(array, AXES, route)  51.5 us
    pallas_call x2, Pallas kernels, later_tile(): pl.pallas_call(functools.partial(later_kernel, k, frames), out_shape=jax....  16.9 us
    pallas_call x1, Pallas kernels, first_tile(): pl.pallas_call(functools.partial(first_kernel, places, frames, n), out_sh...  14.6 us
    ppermute x11, starting transfers between devices, move(): return lax.ppermute(array, AXES, route)  11.8 us
    unnamed x12, local copies, waits for them, and re-layouts  6.47 us
    ppermute x2, starting transfers between devices, swap_wrapped(): return lax.ppermute(array, AXES, route)  6.34 us
    ppermute x2, waiting for transfers between devices, swap_wrapped(): return lax.ppermute(array, AXES, route)  4.15 us
  transfers between devices with their start and end apart: 13, of which 7 were waited for; matrix products, arithmetic and copies ran while one was open for 0% of the time, Pallas kernels for 21%

profile of v4, /device:TPU:121, one launch (start us, length us, event | category | flops | bytes accessed | tf_op | source)
XLA Modules:
  0.0 112.2 jit_solution(4171636369855948742)
XLA Ops:
  0.0 2.7 %collective-permute-start.1 = (bf16[192,3200]{1,0:T(8,128)(2,1)}, bf16[192,3200]{1,0:T(8,128)(2,1)}, u32[]{:S(2)}, u32[]{:S(2)}) collective-permute-start(bf16[192,3200]{1,0:T(8,128)(2,1)} %refs_0_.1), channel_id=1, source_target_pairs={{0,2},{1,3},{2,0},{3,1},{4,6},{5,7},{6,4},{7,5},{8,10},{9,11},{10,... | collective-permute-start | bytes 3686408 | tf_op jit(solution)/shard_map/ppermute | solution.py:238
  2.7 0.5 collective-permute-start.6
  3.2 1.2 %collective-permute-start = (bf16[192,3200]{1,0:T(8,128)(2,1)}, bf16[192,3200]{1,0:T(8,128)(2,1)}, u32[]{:S(2)}, u32[]{:S(2)}) collective-permute-start(bf16[192,3200]{1,0:T(8,128)(2,1)} %refs_0_.1), channel_id=1, source_target_pairs={{0,1},{1,0},{2,3},{3,2},{4,5},{5,4},{6,7},{7,6},{8,9},{9,8},{10,11... | collective-permute-start | bytes 3686408 | tf_op jit(solution)/shard_map/ppermute | solution.py:238
  4.4 25.3 %collective-permute-done.1.refs_2_ = bf16[192,3200]{1,0:T(8,128)(2,1)} collective-permute-done((bf16[192,3200]{1,0:T(8,128)(2,1)}, bf16[192,3200]{1,0:T(8,128)(2,1)}, u32[]{:S(2)}, u32[]{:S(2)}) %collective-permute-start.1) | collective-permute-done | bytes 1228832 | tf_op jit(solution)/shard_map/ppermute | solution.py:238
  29.7 1.5 %collective-permute-start.2 = (bf16[192,3200]{1,0:T(8,128)(2,1)}, bf16[192,3200]{1,0:T(8,128)(2,1)}, u32[]{:S(2)}, u32[]{:S(2)}) collective-permute-start(bf16[192,3200]{1,0:T(8,128)(2,1)} %collective-permute-done.1.refs_2_), channel_id=1, source_target_pairs={{0,1},{1,0},{2,3},{3,2},{4,5},{5,4},{6,7},{7,6},{8,9},{9,8},{10,11... | collective-permute-start | bytes 3686408 | tf_op jit(solution)/shard_map/ppermute | solution.py:238
  31.3 2.6 %collective-permute-done.6.refs_0_ = bf16[192,3200]{1,0:T(8,128)(2,1)S(1)} collective-permute-done((bf16[192,3200]{1,0:T(8,128)(2,1)}, bf16[192,3200]{1,0:T(8,128)(2,1)S(1)}, u32[]{:S(2)}, u32[]{:S(2)}) %collective-permute-start.6) | collective-permute-done | bytes 1228832 | tf_op jit(solution)/shard_map/ppermute | solution.py:238
  33.8 0.9 collective-permute-start.7
  34.7 0.0 collective-permute-start.8
  34.7 0.5 collective-permute-start.3
  35.2 0.0 collective-permute-done.refs_1_
  35.2 0.0 collective-permute-done.2.refs_3_
  35.3 0.0 copy-start.2
  35.3 1.3 %copy-done.2 = bf16[192,3200]{1,0:T(8,128)(2,1)S(1)} copy-done((bf16[192,3200]{1,0:T(8,128)(2,1)S(1)}, bf16[192,3200]{1,0:T(8,128)(2,1)}, u32[]{:S(2)}) %copy-start.2) | copy-done | bytes 1228824
  36.6 0.0 copy-start.3
  36.6 0.7 copy-done.3
  37.3 0.0 copy-start.4
  37.3 0.7 copy-done.4
  37.9 0.0 copy-start.5
  37.9 14.6 %first_tile.1 = (bf16[3,800,3200]{2,1,0:T(8,128)(2,1)}, bf16[3,800,768]{2,1,0:T(8,128)(2,1)S(1)}) custom-call(s32[1]{0:T(128)} %bitcast.3.me_ref, s32[3]{0:T(128)S(1)} %copy-done.4, s32[768]{0:T(1024)S(1)} %copy-done.3, bf16[192,3200]{1,0:T(8,128)(2,1)S(1)} %copy-done.2, bf16[192,3200]{1,0:T(8,128)(2,1)} %collective-permute-done.refs_1_, ...), custom_call_target="tpu_custom_call" | custom-call | flops 10695475200 | bytes 10035200 | tf_op jit(solution)/shard_map/first_tile/pallas_call | solution.py:156
  52.6 0.0 copy-start
  52.6 1.8 %copy-done = bf16[3,800,768]{2,1,0:T(8,128)(2,1)} copy-done((bf16[3,800,768]{2,1,0:T(8,128)(2,1)}, bf16[3,800,768]{2,1,0:T(8,128)(2,1)S(1)}, u32[]{:S(2)}) %copy-start) | copy-done | bytes 3686424
  54.3 7.5 %collective-permute-done.7.refs_3_ = bf16[192,3200]{1,0:T(8,128)(2,1)} collective-permute-done((bf16[192,3200]{1,0:T(8,128)(2,1)S(1)}, bf16[192,3200]{1,0:T(8,128)(2,1)}, u32[]{:S(2)}, u32[]{:S(2)}) %collective-permute-start.7) | collective-permute-done | bytes 1228832 | tf_op jit(solution)/shard_map/ppermute | solution.py:238
  61.8 0.0 collective-permute-done.8.refs_1_
  61.8 2.8 %collective-permute-start.10 = (bf16[192,3200]{1,0:T(8,128)(2,1)}, bf16[192,3200]{1,0:T(8,128)(2,1)}, u32[]{:S(2)}, u32[]{:S(2)}) collective-permute-start(bf16[192,3200]{1,0:T(8,128)(2,1)} %collective-permute-done.7.refs_3_), channel_id=1, source_target_pairs={{0,1},{1,0},{2,3},{3,2},{4,5},{5,4},{6,7},{7,6},{8,9},{9,8},{10,11... | collective-permute-start | bytes 3686408 | tf_op jit(solution)/shard_map/ppermute | solution.py:238
  64.6 1.9 %collective-permute-start.9 = (bf16[192,3200]{1,0:T(8,128)(2,1)}, bf16[192,3200]{1,0:T(8,128)(2,1)}, u32[]{:S(2)}, u32[]{:S(2)}) collective-permute-start(bf16[192,3200]{1,0:T(8,128)(2,1)} %collective-permute-done.8.refs_1_), channel_id=1, source_target_pairs={{60,61},{61,60},{62,63},{63,62},{124,125},{125,124},{126,127},{127... | collective-permute-start | bytes 3686408 | tf_op jit(solution)/shard_map/ppermute | solution.py:257
  66.5 0.0 collective-permute-done.3.refs_0_
  66.5 1.5 %collective-permute-start.4 = (bf16[192,3200]{1,0:T(8,128)(2,1)S(1)}, bf16[192,3200]{1,0:T(8,128)(2,1)}, u32[]{:S(2)}, u32[]{:S(2)}) collective-permute-start(bf16[192,3200]{1,0:T(8,128)(2,1)S(1)} %collective-permute-done.3.refs_0_), channel_id=1, source_target_pairs={{0,2},{1,3},{2,0},{3,1},{4,6},{5,7},{6,4},{7,5},{8,10},{9,11},{10,... | collective-permute-start | bytes 3686408 | tf_op jit(solution)/shard_map/ppermute | solution.py:238
  68.1 0.0 collective-permute-start.5
  68.1 0.1 add_convert_fusion
  68.2 0.0 copy-done.5
  68.2 0.1 pad_add_fusion.flags
  68.2 0.0 collective-permute-done.10.refs_4_
  68.2 1.5 %collective-permute-done.9.refs_2_ = bf16[192,3200]{1,0:T(8,128)(2,1)} collective-permute-done((bf16[192,3200]{1,0:T(8,128)(2,1)}, bf16[192,3200]{1,0:T(8,128)(2,1)}, u32[]{:S(2)}, u32[]{:S(2)}) %collective-permute-start.9) | collective-permute-done | bytes 1228832 | tf_op jit(solution)/shard_map/ppermute | solution.py:257
  69.7 0.0 copy-start.1
  69.8 2.0 %copy-done.1 = bf16[3,800,768]{2,1,0:T(8,128)(2,1)S(1)} copy-done((bf16[3,800,768]{2,1,0:T(8,128)(2,1)S(1)}, bf16[3,800,768]{2,1,0:T(8,128)(2,1)}, u32[]{:S(2)}) %copy-start.1) | copy-done | bytes 3686424
  71.8 8.8 %later_tile.2.refs_5_ = bf16[3,800,3200]{2,1,0:T(8,128)(2,1)} custom-call(s32[6]{0:T(128)S(1)} %pad_add_fusion.flags, bf16[3,800,768]{2,1,0:T(8,128)(2,1)S(1)} %copy-done.1, bf16[192,3200]{1,0:T(8,128)(2,1)S(1)} %collective-permute-done.6.refs_0_, bf16[192,3200]{1,0:T(8,128)(2,1)} %collective-permute-done.8.refs_1_, ...), custom_call_target="tpu_custom_call", output_to_operand_aliasing={{}: (7, {})} | custom-call | flops 7864320000 | bytes 10035200 | tf_op jit(solution)/shard_map/later_tile/pallas_call | solution.py:202
  80.6 14.4 %collective-permute-done.4.refs_3_ = bf16[192,3200]{1,0:T(8,128)(2,1)} collective-permute-done((bf16[192,3200]{1,0:T(8,128)(2,1)S(1)}, bf16[192,3200]{1,0:T(8,128)(2,1)}, u32[]{:S(2)}, u32[]{:S(2)}) %collective-permute-start.4) | collective-permute-done | bytes 1228832 | tf_op jit(solution)/shard_map/ppermute | solution.py:238
  95.1 0.0 collective-permute-done.5.refs_1_
  95.1 4.4 %collective-permute-start.11 = (bf16[192,3200]{1,0:T(8,128)(2,1)}, bf16[192,3200]{1,0:T(8,128)(2,1)S(1)}, u32[]{:S(2)}, u32[]{:S(2)}) collective-permute-start(bf16[192,3200]{1,0:T(8,128)(2,1)} %collective-permute-done.5.refs_1_), channel_id=1, source_target_pairs={{56,57},{57,56},{58,59},{59,58},{60,61},{61,60},{62,63},{63,62},{1... | collective-permute-start | bytes 3686408 | tf_op jit(solution)/shard_map/ppermute | solution.py:257
  99.5 0.1 collective-permute-start.12
  99.6 2.6 %collective-permute-done.11.refs_2_ = bf16[192,3200]{1,0:T(8,128)(2,1)S(1)} collective-permute-done((bf16[192,3200]{1,0:T(8,128)(2,1)}, bf16[192,3200]{1,0:T(8,128)(2,1)S(1)}, u32[]{:S(2)}, u32[]{:S(2)}) %collective-permute-start.11) | collective-permute-done | bytes 1228832 | tf_op jit(solution)/shard_map/ppermute | solution.py:257
  102.3 1.8 %collective-permute-done.12.refs_4_ = bf16[192,3200]{1,0:T(8,128)(2,1)S(1)} collective-permute-done((bf16[192,3200]{1,0:T(8,128)(2,1)}, bf16[192,3200]{1,0:T(8,128)(2,1)S(1)}, u32[]{:S(2)}, u32[]{:S(2)}) %collective-permute-start.12) | collective-permute-done | bytes 1228832 | tf_op jit(solution)/shard_map/ppermute | solution.py:238
  104.0 8.0 %later_tile.3 = bf16[3,800,3200]{2,1,0:T(8,128)(2,1)} custom-call(s32[6]{0:T(128)S(1)} %pad_add_fusion.flags, bf16[3,800,768]{2,1,0:T(8,128)(2,1)S(1)} %copy-done.1, bf16[192,3200]{1,0:T(8,128)(2,1)S(1)} %collective-permute-done.3.refs_0_, bf16[192,3200]{1,0:T(8,128)(2,1)} %collective-permute-done.5.refs_1_, ...), custom_call_target="tpu_custom_call", output_to_operand_aliasing={{}: (7, {})} | custom-call | flops 7864320000 | bytes 10035200 | tf_op jit(solution)/shard_map/later_tile/pallas_call | solution.py:202
Async XLA Ops:
  0.0 29.7 %collective-permute-start.1 = (bf16[192,3200]{1,0:T(8,128)(2,1)}, bf16[192,3200]{1,0:T(8,128)(2,1)}, u32[]{:S(2)}, u32[]{:S(2)}) collective-permute-start(bf16[192,3200]{1,0:T(8,128)(2,1)} %refs_0_.1), channel_id=1, source_target_pairs={{0,2},{1,3},{2,0},{3,1},{4,6},{5,7},{6,4},{7,5},{8,10},{9,11},{10,... | collective-permute-start | bytes 3686408 | tf_op jit(solution)/shard_map/ppermute | solution.py:238
  2.7 31.1 %collective-permute-start.6 = (bf16[192,3200]{1,0:T(8,128)(2,1)}, bf16[192,3200]{1,0:T(8,128)(2,1)S(1)}, u32[]{:S(2)}, u32[]{:S(2)}) collective-permute-start(bf16[192,3200]{1,0:T(8,128)(2,1)} %refs_0_.1), channel_id=1, source_target_pairs={{0,60},{1,61},{2,62},{3,63},{4,0},{5,1},{6,2},{7,3},{8,4},{9,5},{1... | collective-permute-start | bytes 3686408 | tf_op jit(solution)/shard_map/ppermute | solution.py:238
  3.2 32.0 %collective-permute-start = (bf16[192,3200]{1,0:T(8,128)(2,1)}, bf16[192,3200]{1,0:T(8,128)(2,1)}, u32[]{:S(2)}, u32[]{:S(2)}) collective-permute-start(bf16[192,3200]{1,0:T(8,128)(2,1)} %refs_0_.1), channel_id=1, source_target_pairs={{0,1},{1,0},{2,3},{3,2},{4,5},{5,4},{6,7},{7,6},{8,9},{9,8},{10,11... | collective-permute-start | bytes 3686408 | tf_op jit(solution)/shard_map/ppermute | solution.py:238
  29.7 5.5 %collective-permute-start.2 = (bf16[192,3200]{1,0:T(8,128)(2,1)}, bf16[192,3200]{1,0:T(8,128)(2,1)}, u32[]{:S(2)}, u32[]{:S(2)}) collective-permute-start(bf16[192,3200]{1,0:T(8,128)(2,1)} %collective-permute-done.1.refs_2_), channel_id=1, source_target_pairs={{0,1},{1,0},{2,3},{3,2},{4,5},{5,4},{6,7},{7,6},{8,9},{9,8},{10,11... | collective-permute-start | bytes 3686408 | tf_op jit(solution)/shard_map/ppermute | solution.py:238
  33.8 28.0 %collective-permute-start.7 = (bf16[192,3200]{1,0:T(8,128)(2,1)S(1)}, bf16[192,3200]{1,0:T(8,128)(2,1)}, u32[]{:S(2)}, u32[]{:S(2)}) collective-permute-start(bf16[192,3200]{1,0:T(8,128)(2,1)S(1)} %collective-permute-done.6.refs_0_), channel_id=1, source_target_pairs={{0,2},{1,3},{2,0},{3,1},{4,6},{5,7},{6,4},{7,5},{8,10},{9,11},{10,... | collective-permute-start | bytes 3686408 | tf_op jit(solution)/shard_map/ppermute | solution.py:238
  34.7 27.1 %collective-permute-start.8 = (bf16[192,3200]{1,0:T(8,128)(2,1)S(1)}, bf16[192,3200]{1,0:T(8,128)(2,1)}, u32[]{:S(2)}, u32[]{:S(2)}) collective-permute-start(bf16[192,3200]{1,0:T(8,128)(2,1)S(1)} %collective-permute-done.6.refs_0_), channel_id=1, source_target_pairs={{0,1},{1,0},{2,3},{3,2},{4,5},{5,4},{6,7},{7,6},{8,9},{9,8},{10,11... | collective-permute-start | bytes 3686408 | tf_op jit(solution)/shard_map/ppermute | solution.py:238
  34.7 31.8 %collective-permute-start.3 = (bf16[192,3200]{1,0:T(8,128)(2,1)}, bf16[192,3200]{1,0:T(8,128)(2,1)S(1)}, u32[]{:S(2)}, u32[]{:S(2)}) collective-permute-start(bf16[192,3200]{1,0:T(8,128)(2,1)} %refs_0_.1), channel_id=1, source_target_pairs={{0,56},{1,57},{2,58},{3,59},{4,60},{5,61},{6,62},{7,63},{8,0},{9,1... | collective-permute-start | bytes 3686408 | tf_op jit(solution)/shard_map/ppermute | solution.py:238
  35.3 1.3 %copy-start.2 = (bf16[192,3200]{1,0:T(8,128)(2,1)S(1)}, bf16[192,3200]{1,0:T(8,128)(2,1)}, u32[]{:S(2)}) copy-start(bf16[192,3200]{1,0:T(8,128)(2,1)} %refs_0_.1) | copy-start | bytes 3686404
  36.6 0.7 copy-start.3
  37.3 0.7 copy-start.4
  37.9 30.2 %copy-start.5 = (s32[3]{0:T(128)S(1)}, s32[3]{0:T(128)}, u32[]{:S(2)}) copy-start(s32[3]{0:T(128)} %lag_ref.1) | copy-start | bytes 40
  52.6 1.8 %copy-start = (bf16[3,800,768]{2,1,0:T(8,128)(2,1)}, bf16[3,800,768]{2,1,0:T(8,128)(2,1)S(1)}, u32[]{:S(2)}) copy-start(bf16[3,800,768]{2,1,0:T(8,128)(2,1)S(1)} %get-tuple-element.14.y) | copy-start | bytes 11059204
  61.8 6.4 %collective-permute-start.10 = (bf16[192,3200]{1,0:T(8,128)(2,1)}, bf16[192,3200]{1,0:T(8,128)(2,1)}, u32[]{:S(2)}, u32[]{:S(2)}) collective-permute-start(bf16[192,3200]{1,0:T(8,128)(2,1)} %collective-permute-done.7.refs_3_), channel_id=1, source_target_pairs={{0,1},{1,0},{2,3},{3,2},{4,5},{5,4},{6,7},{7,6},{8,9},{9,8},{10,11... | collective-permute-start | bytes 3686408 | tf_op jit(solution)/shard_map/ppermute | solution.py:238
  64.6 5.1 %collective-permute-start.9 = (bf16[192,3200]{1,0:T(8,128)(2,1)}, bf16[192,3200]{1,0:T(8,128)(2,1)}, u32[]{:S(2)}, u32[]{:S(2)}) collective-permute-start(bf16[192,3200]{1,0:T(8,128)(2,1)} %collective-permute-done.8.refs_1_), channel_id=1, source_target_pairs={{60,61},{61,60},{62,63},{63,62},{124,125},{125,124},{126,127},{127... | collective-permute-start | bytes 3686408 | tf_op jit(solution)/shard_map/ppermute | solution.py:257
  66.5 28.5 %collective-permute-start.4 = (bf16[192,3200]{1,0:T(8,128)(2,1)S(1)}, bf16[192,3200]{1,0:T(8,128)(2,1)}, u32[]{:S(2)}, u32[]{:S(2)}) collective-permute-start(bf16[192,3200]{1,0:T(8,128)(2,1)S(1)} %collective-permute-done.3.refs_0_), channel_id=1, source_target_pairs={{0,2},{1,3},{2,0},{3,1},{4,6},{5,7},{6,4},{7,5},{8,10},{9,11},{10,... | collective-permute-start | bytes 3686408 | tf_op jit(solution)/shard_map/ppermute | solution.py:238
  68.1 27.0 %collective-permute-start.5 = (bf16[192,3200]{1,0:T(8,128)(2,1)S(1)}, bf16[192,3200]{1,0:T(8,128)(2,1)}, u32[]{:S(2)}, u32[]{:S(2)}) collective-permute-start(bf16[192,3200]{1,0:T(8,128)(2,1)S(1)} %collective-permute-done.3.refs_0_), channel_id=1, source_target_pairs={{0,1},{1,0},{2,3},{3,2},{4,5},{5,4},{6,7},{7,6},{8,9},{9,8},{10,11... | collective-permute-start | bytes 3686408 | tf_op jit(solution)/shard_map/ppermute | solution.py:238
  69.7 2.0 %copy-start.1 = (bf16[3,800,768]{2,1,0:T(8,128)(2,1)S(1)}, bf16[3,800,768]{2,1,0:T(8,128)(2,1)}, u32[]{:S(2)}) copy-start(bf16[3,800,768]{2,1,0:T(8,128)(2,1)} %copy-done) | copy-start | bytes 11059204
  95.1 7.2 %collective-permute-start.11 = (bf16[192,3200]{1,0:T(8,128)(2,1)}, bf16[192,3200]{1,0:T(8,128)(2,1)S(1)}, u32[]{:S(2)}, u32[]{:S(2)}) collective-permute-start(bf16[192,3200]{1,0:T(8,128)(2,1)} %collective-permute-done.5.refs_1_), channel_id=1, source_target_pairs={{56,57},{57,56},{58,59},{59,58},{60,61},{61,60},{62,63},{63,62},{1... | collective-permute-start | bytes 3686408 | tf_op jit(solution)/shard_map/ppermute | solution.py:257
  99.5 4.5 %collective-permute-start.12 = (bf16[192,3200]{1,0:T(8,128)(2,1)}, bf16[192,3200]{1,0:T(8,128)(2,1)S(1)}, u32[]{:S(2)}, u32[]{:S(2)}) collective-permute-start(bf16[192,3200]{1,0:T(8,128)(2,1)} %collective-permute-done.4.refs_3_), channel_id=1, source_target_pairs={{0,1},{1,0},{2,3},{3,2},{4,5},{5,4},{6,7},{7,6},{8,9},{9,8},{10,11... | collective-permute-start | bytes 3686408 | tf_op jit(solution)/shard_map/ppermute | solution.py:238

commit v5 on v4

--- a/solution.py
+++ b/solution.py
@@ -15,7 +15,8 @@
 
 
 def spans(first, last):
-    return [(c, min(CHUNK, last - c)) for c in range(first, last, CHUNK)]
+    edges = [first, *range(first + CHUNK // 2, last, CHUNK), last]
+    return [(a, b - a) for a, b in zip(edges, edges[1:])]
 
 
 def center(sources, out, cols, wrapped=None):
@@ -218,6 +219,28 @@
     )(flags, y, *pieces, tiles)
 
 
+def fetch_kernel(n, *refs):
+    sems = refs[2 * n]
+    copies = [pltpu.make_async_copy(refs[j], refs[n + j], sems.at[j]) for j in range(n)]
+    for copy in copies:
+        copy.start()
+    for copy in copies:
+        copy.wait()
+
+
+def fetch(*arrays):
+    n = len(arrays)
+    return pl.pallas_call(
+        functools.partial(fetch_kernel, n),
+        out_shape=tuple(jax.ShapeDtypeStruct(a.shape, a.dtype) for a in arrays),
+        in_specs=[HBM_SPEC] * n,
+        out_specs=(VMEM_SPEC,) * n,
+        scratch_shapes=[pltpu.SemaphoreType.DMA((n,))],
+        compiler_params=pltpu.CompilerParams(vmem_limit_bytes=VMEM),
+        name="fetch",
+    )(*arrays)
+
+
 def after(array, *done):
     return lax.optimization_barrier((array, *done))[0]
 
@@ -267,7 +290,7 @@
     own_core = core(own)
     across = cross(own, 0)
     next_ring = ring(own, 1)
-    after_ring = ring(after(own, across), 2)
+    after_ring = ring(next_ring, 1)
     across_core = core(across)
     next_across = cross(next_ring, 1)
     next_beside = beside(next_ring, 1)
@@ -290,6 +313,7 @@
     )
     after_across_core = core(after_across)
     after_core_wrap = swap_wrapped(after_beside, 2)
+    after_across, after_beside = fetch(after_across, after_beside)
     return later_tile(
         2, flags, y,
         [after_ring, after_beside, after_core_wrap, after_across, after_across_core],

time: 112 us -> 110 us (0.982)
  Pallas kernels: 31.5 us -> 30.3 us
    pallas_call x2, Pallas kernels: 16.9 us -> 14.4 us  [later_tile(): pl.pallas_call(functools.partial(later_kernel, k, frames), out_shape=jax....]
    ppermute x11, waiting for transfers between devices: 51.5 us -> 53.4 us  [move(): return lax.ppermute(array, AXES, route)]
    ppermute x2, waiting for transfers between devices: 4.15 us -> 2.47 us  [swap_wrapped(): return lax.ppermute(array, AXES, route)]
    pallas_call x0 -> x1, Pallas kernels: none -> 1.68 us  [fetch(): pl.pallas_call(functools.partial(fetch_kernel, n), out_shape=tuple((jax.S...]
    unnamed x12 -> x14, local copies, waits for them, and re-layouts: 6.47 us -> 6.47 us
  transfers between devices with their start and end apart: 13 -> 13, of which waited for: 7 -> 7; matrix products, arithmetic and copies ran while one was open for 0% -> 0% of each run, Pallas kernels for 21% -> 22%
where the time goes in v5:
time: 110 us
  waiting for transfers between devices  55.8 us (51%)
  Pallas kernels  30.3 us (28%)
  starting transfers between devices  17.1 us (16%)
  local copies, waits for them, and re-layouts  6.47 us (6%)
    ppermute x11, waiting for transfers between devices, move(): return lax.ppermute(array, AXES, route)  53.4 us
    pallas_call x2, Pallas kernels, later_tile(): pl.pallas_call(functools.partial(later_kernel, k, frames), out_shape=jax....  14.4 us
    pallas_call x1, Pallas kernels, first_tile(): pl.pallas_call(functools.partial(first_kernel, places, frames, n), out_sh...  14.3 us
    ppermute x11, starting transfers between devices, move(): return lax.ppermute(array, AXES, route)  11.3 us
    unnamed x14, local copies, waits for them, and re-layouts  6.47 us
    ppermute x2, starting transfers between devices, swap_wrapped(): return lax.ppermute(array, AXES, route)  5.81 us
    ppermute x2, waiting for transfers between devices, swap_wrapped(): return lax.ppermute(array, AXES, route)  2.47 us
  transfers between devices with their start and end apart: 13, of which 7 were waited for; matrix products, arithmetic and copies ran while one was open for 0% of the time, Pallas kernels for 22%

profile of v5, /device:TPU:121, one launch (start us, length us, event | category | flops | bytes accessed | tf_op | source)
XLA Modules:
  0.0 110.1 jit_solution(13487672238524028938)
XLA Ops:
  0.0 2.7 %collective-permute-start.1 = (bf16[192,3200]{1,0:T(8,128)(2,1)}, bf16[192,3200]{1,0:T(8,128)(2,1)}, u32[]{:S(2)}, u32[]{:S(2)}) collective-permute-start(bf16[192,3200]{1,0:T(8,128)(2,1)} %refs_0_.1), channel_id=1, source_target_pairs={{0,2},{1,3},{2,0},{3,1},{4,6},{5,7},{6,4},{7,5},{8,10},{9,11},{10,... | collective-permute-start | bytes 3686408 | tf_op jit(solution)/shard_map/ppermute | solution.py:261
  2.7 0.5 collective-permute-start.3
  3.2 1.2 %collective-permute-start = (bf16[192,3200]{1,0:T(8,128)(2,1)}, bf16[192,3200]{1,0:T(8,128)(2,1)}, u32[]{:S(2)}, u32[]{:S(2)}) collective-permute-start(bf16[192,3200]{1,0:T(8,128)(2,1)} %refs_0_.1), channel_id=1, source_target_pairs={{0,1},{1,0},{2,3},{3,2},{4,5},{5,4},{6,7},{7,6},{8,9},{9,8},{10,11... | collective-permute-start | bytes 3686408 | tf_op jit(solution)/shard_map/ppermute | solution.py:261
  4.4 25.3 %collective-permute-done.1.refs_2_ = bf16[192,3200]{1,0:T(8,128)(2,1)} collective-permute-done((bf16[192,3200]{1,0:T(8,128)(2,1)}, bf16[192,3200]{1,0:T(8,128)(2,1)}, u32[]{:S(2)}, u32[]{:S(2)}) %collective-permute-start.1) | collective-permute-done | bytes 1228832 | tf_op jit(solution)/shard_map/ppermute | solution.py:261
  29.7 1.5 %collective-permute-start.2 = (bf16[192,3200]{1,0:T(8,128)(2,1)}, bf16[192,3200]{1,0:T(8,128)(2,1)}, u32[]{:S(2)}, u32[]{:S(2)}) collective-permute-start(bf16[192,3200]{1,0:T(8,128)(2,1)} %collective-permute-done.1.refs_2_), channel_id=1, source_target_pairs={{0,1},{1,0},{2,3},{3,2},{4,5},{5,4},{6,7},{7,6},{8,9},{9,8},{10,11... | collective-permute-start | bytes 3686408 | tf_op jit(solution)/shard_map/ppermute | solution.py:261
  31.3 2.6 %collective-permute-done.3.refs_0_ = bf16[192,3200]{1,0:T(8,128)(2,1)S(1)} collective-permute-done((bf16[192,3200]{1,0:T(8,128)(2,1)}, bf16[192,3200]{1,0:T(8,128)(2,1)S(1)}, u32[]{:S(2)}, u32[]{:S(2)}) %collective-permute-start.3) | collective-permute-done | bytes 1228832 | tf_op jit(solution)/shard_map/ppermute | solution.py:261
  33.8 0.9 collective-permute-start.7
  34.7 0.0 collective-permute-start.8
  34.7 0.0 collective-permute-start.4
  34.8 0.0 collective-permute-done.refs_1_
  34.8 0.0 collective-permute-done.2.refs_3_
  34.8 0.0 copy-start.3
  34.8 1.3 %copy-done.3 = bf16[192,3200]{1,0:T(8,128)(2,1)S(1)} copy-done((bf16[192,3200]{1,0:T(8,128)(2,1)S(1)}, bf16[192,3200]{1,0:T(8,128)(2,1)}, u32[]{:S(2)}) %copy-start.3) | copy-done | bytes 1228824
  36.0 0.0 copy-start.4
  36.1 0.7 copy-done.4
  36.7 0.0 copy-start.5
  36.7 0.7 copy-done.5
  37.4 0.0 copy-start.6
  37.4 14.3 %first_tile.1 = (bf16[3,800,3200]{2,1,0:T(8,128)(2,1)}, bf16[3,800,768]{2,1,0:T(8,128)(2,1)S(1)}) custom-call(s32[1]{0:T(128)} %bitcast.3.me_ref, s32[3]{0:T(128)S(1)} %copy-done.5, s32[768]{0:T(1024)S(1)} %copy-done.4, bf16[192,3200]{1,0:T(8,128)(2,1)S(1)} %copy-done.3, bf16[192,3200]{1,0:T(8,128)(2,1)} %collective-permute-done.refs_1_, ...), custom_call_target="tpu_custom_call" | custom-call | flops 10695475200 | bytes 10035200 | tf_op jit(solution)/shard_map/first_tile/pallas_call | solution.py:157
  51.7 0.0 copy-start
  51.7 1.8 %copy-done = bf16[3,800,768]{2,1,0:T(8,128)(2,1)} copy-done((bf16[3,800,768]{2,1,0:T(8,128)(2,1)}, bf16[3,800,768]{2,1,0:T(8,128)(2,1)S(1)}, u32[]{:S(2)}) %copy-start) | copy-done | bytes 3686424
  53.5 8.4 %collective-permute-done.7.refs_3_ = bf16[192,3200]{1,0:T(8,128)(2,1)} collective-permute-done((bf16[192,3200]{1,0:T(8,128)(2,1)S(1)}, bf16[192,3200]{1,0:T(8,128)(2,1)}, u32[]{:S(2)}, u32[]{:S(2)}) %collective-permute-start.7) | collective-permute-done | bytes 1228832 | tf_op jit(solution)/shard_map/ppermute | solution.py:261
  61.8 0.0 collective-permute-done.8.refs_1_
  61.8 2.8 %collective-permute-start.10 = (bf16[192,3200]{1,0:T(8,128)(2,1)}, bf16[192,3200]{1,0:T(8,128)(2,1)}, u32[]{:S(2)}, u32[]{:S(2)}) collective-permute-start(bf16[192,3200]{1,0:T(8,128)(2,1)} %collective-permute-done.7.refs_3_), channel_id=1, source_target_pairs={{0,1},{1,0},{2,3},{3,2},{4,5},{5,4},{6,7},{7,6},{8,9},{9,8},{10,11... | collective-permute-start | bytes 3686408 | tf_op jit(solution)/shard_map/ppermute | solution.py:261
  64.6 1.9 %collective-permute-start.9 = (bf16[192,3200]{1,0:T(8,128)(2,1)}, bf16[192,3200]{1,0:T(8,128)(2,1)}, u32[]{:S(2)}, u32[]{:S(2)}) collective-permute-start(bf16[192,3200]{1,0:T(8,128)(2,1)} %collective-permute-done.8.refs_1_), channel_id=1, source_target_pairs={{60,61},{61,60},{62,63},{63,62},{124,125},{125,124},{126,127},{127... | collective-permute-start | bytes 3686408 | tf_op jit(solution)/shard_map/ppermute | solution.py:280
  66.5 0.0 collective-permute-done.4.refs_0_
  66.5 1.5 %collective-permute-start.5 = (bf16[192,3200]{1,0:T(8,128)(2,1)S(1)}, bf16[192,3200]{1,0:T(8,128)(2,1)}, u32[]{:S(2)}, u32[]{:S(2)}) collective-permute-start(bf16[192,3200]{1,0:T(8,128)(2,1)S(1)} %collective-permute-done.4.refs_0_), channel_id=1, source_target_pairs={{0,2},{1,3},{2,0},{3,1},{4,6},{5,7},{6,4},{7,5},{8,10},{9,11},{10,... | collective-permute-start | bytes 3686408 | tf_op jit(solution)/shard_map/ppermute | solution.py:261
  68.1 0.0 collective-permute-start.6
  68.1 0.1 add_convert_fusion
  68.2 0.0 copy-done.6
  68.2 0.1 pad_add_fusion.flags
  68.2 0.0 collective-permute-done.10.refs_4_
  68.2 1.5 %collective-permute-done.9.refs_2_ = bf16[192,3200]{1,0:T(8,128)(2,1)} collective-permute-done((bf16[192,3200]{1,0:T(8,128)(2,1)}, bf16[192,3200]{1,0:T(8,128)(2,1)}, u32[]{:S(2)}, u32[]{:S(2)}) %collective-permute-start.9) | collective-permute-done | bytes 1228832 | tf_op jit(solution)/shard_map/ppermute | solution.py:280
  69.7 0.0 copy-start.1
  69.8 2.0 %copy-done.1 = bf16[3,800,768]{2,1,0:T(8,128)(2,1)S(1)} copy-done((bf16[3,800,768]{2,1,0:T(8,128)(2,1)S(1)}, bf16[3,800,768]{2,1,0:T(8,128)(2,1)}, u32[]{:S(2)}) %copy-start.1) | copy-done | bytes 3686424
  71.8 0.0 copy-start.2
  71.8 8.4 %later_tile.2.refs_5_ = bf16[3,800,3200]{2,1,0:T(8,128)(2,1)} custom-call(s32[6]{0:T(128)S(1)} %pad_add_fusion.flags, bf16[3,800,768]{2,1,0:T(8,128)(2,1)S(1)} %copy-done.1, bf16[192,3200]{1,0:T(8,128)(2,1)S(1)} %collective-permute-done.3.refs_0_, bf16[192,3200]{1,0:T(8,128)(2,1)} %collective-permute-done.8.refs_1_, ...), custom_call_target="tpu_custom_call", output_to_operand_aliasing={{}: (7, {})} | custom-call | flops 7864320000 | bytes 10035200 | tf_op jit(solution)/shard_map/later_tile/pallas_call | solution.py:203
  80.2 15.4 %collective-permute-done.5.refs_0_ = bf16[192,3200]{1,0:T(8,128)(2,1)} collective-permute-done((bf16[192,3200]{1,0:T(8,128)(2,1)S(1)}, bf16[192,3200]{1,0:T(8,128)(2,1)}, u32[]{:S(2)}, u32[]{:S(2)}) %collective-permute-start.5) | collective-permute-done | bytes 1228832 | tf_op jit(solution)/shard_map/ppermute | solution.py:261
  95.6 0.0 collective-permute-done.6.refs_1_
  95.6 3.9 %collective-permute-start.11 = (bf16[192,3200]{1,0:T(8,128)(2,1)}, bf16[192,3200]{1,0:T(8,128)(2,1)S(1)}, u32[]{:S(2)}, u32[]{:S(2)}) collective-permute-start(bf16[192,3200]{1,0:T(8,128)(2,1)} %collective-permute-done.6.refs_1_), channel_id=1, source_target_pairs={{56,57},{57,56},{58,59},{59,58},{60,61},{61,60},{62,63},{63,62},{1... | collective-permute-start | bytes 3686408 | tf_op jit(solution)/shard_map/ppermute | solution.py:280
  99.5 0.1 collective-permute-start.12
  99.6 1.7 %fetch.1 = (bf16[192,3200]{1,0:T(8,128)(2,1)S(1)}, bf16[192,3200]{1,0:T(8,128)(2,1)S(1)}) custom-call(bf16[192,3200]{1,0:T(8,128)(2,1)} %collective-permute-done.5.refs_0_, bf16[192,3200]{1,0:T(8,128)(2,1)} %collective-permute-done.6.refs_1_), custom_call_target="tpu_custom_call" | custom-call | tf_op jit(solution)/shard_map/fetch/pallas_call | solution.py:233
  101.3 1.0 collective-permute-done.11.refs_2_
  102.3 1.8 %collective-permute-done.12.refs_4_ = bf16[192,3200]{1,0:T(8,128)(2,1)S(1)} collective-permute-done((bf16[192,3200]{1,0:T(8,128)(2,1)}, bf16[192,3200]{1,0:T(8,128)(2,1)S(1)}, u32[]{:S(2)}, u32[]{:S(2)}) %collective-permute-start.12) | collective-permute-done | bytes 1228832 | tf_op jit(solution)/shard_map/ppermute | solution.py:261
  104.0 0.0 copy-done.2
  104.0 5.9 %later_tile.3 = bf16[3,800,3200]{2,1,0:T(8,128)(2,1)} custom-call(s32[6]{0:T(128)S(1)} %pad_add_fusion.flags, bf16[3,800,768]{2,1,0:T(8,128)(2,1)S(1)} %copy-done.2, bf16[192,3200]{1,0:T(8,128)(2,1)S(1)} %collective-permute-done.4.refs_0_, bf16[192,3200]{1,0:T(8,128)(2,1)S(1)} %get-tuple-element.22.refs_1_, ...), custom_call_target="tpu_custom_call", output_to_operand_aliasing={{}: (7, {})} | custom-call | flops 7864320000 | bytes 10035200 | tf_op jit(solution)/shard_map/later_tile/pallas_call | solution.py:203
Async XLA Ops:
  0.0 29.7 %collective-permute-start.1 = (bf16[192,3200]{1,0:T(8,128)(2,1)}, bf16[192,3200]{1,0:T(8,128)(2,1)}, u32[]{:S(2)}, u32[]{:S(2)}) collective-permute-start(bf16[192,3200]{1,0:T(8,128)(2,1)} %refs_0_.1), channel_id=1, source_target_pairs={{0,2},{1,3},{2,0},{3,1},{4,6},{5,7},{6,4},{7,5},{8,10},{9,11},{10,... | collective-permute-start | bytes 3686408 | tf_op jit(solution)/shard_map/ppermute | solution.py:261
  2.7 31.1 %collective-permute-start.3 = (bf16[192,3200]{1,0:T(8,128)(2,1)}, bf16[192,3200]{1,0:T(8,128)(2,1)S(1)}, u32[]{:S(2)}, u32[]{:S(2)}) collective-permute-start(bf16[192,3200]{1,0:T(8,128)(2,1)} %refs_0_.1), channel_id=1, source_target_pairs={{0,60},{1,61},{2,62},{3,63},{4,0},{5,1},{6,2},{7,3},{8,4},{9,5},{1... | collective-permute-start | bytes 3686408 | tf_op jit(solution)/shard_map/ppermute | solution.py:261
  3.2 31.5 %collective-permute-start = (bf16[192,3200]{1,0:T(8,128)(2,1)}, bf16[192,3200]{1,0:T(8,128)(2,1)}, u32[]{:S(2)}, u32[]{:S(2)}) collective-permute-start(bf16[192,3200]{1,0:T(8,128)(2,1)} %refs_0_.1), channel_id=1, source_target_pairs={{0,1},{1,0},{2,3},{3,2},{4,5},{5,4},{6,7},{7,6},{8,9},{9,8},{10,11... | collective-permute-start | bytes 3686408 | tf_op jit(solution)/shard_map/ppermute | solution.py:261
  29.7 5.0 %collective-permute-start.2 = (bf16[192,3200]{1,0:T(8,128)(2,1)}, bf16[192,3200]{1,0:T(8,128)(2,1)}, u32[]{:S(2)}, u32[]{:S(2)}) collective-permute-start(bf16[192,3200]{1,0:T(8,128)(2,1)} %collective-permute-done.1.refs_2_), channel_id=1, source_target_pairs={{0,1},{1,0},{2,3},{3,2},{4,5},{5,4},{6,7},{7,6},{8,9},{9,8},{10,11... | collective-permute-start | bytes 3686408 | tf_op jit(solution)/shard_map/ppermute | solution.py:261
  33.8 28.0 %collective-permute-start.7 = (bf16[192,3200]{1,0:T(8,128)(2,1)S(1)}, bf16[192,3200]{1,0:T(8,128)(2,1)}, u32[]{:S(2)}, u32[]{:S(2)}) collective-permute-start(bf16[192,3200]{1,0:T(8,128)(2,1)S(1)} %collective-permute-done.3.refs_0_), channel_id=1, source_target_pairs={{0,2},{1,3},{2,0},{3,1},{4,6},{5,7},{6,4},{7,5},{8,10},{9,11},{10,... | collective-permute-start | bytes 3686408 | tf_op jit(solution)/shard_map/ppermute | solution.py:261
  34.7 27.1 %collective-permute-start.8 = (bf16[192,3200]{1,0:T(8,128)(2,1)S(1)}, bf16[192,3200]{1,0:T(8,128)(2,1)}, u32[]{:S(2)}, u32[]{:S(2)}) collective-permute-start(bf16[192,3200]{1,0:T(8,128)(2,1)S(1)} %collective-permute-done.3.refs_0_), channel_id=1, source_target_pairs={{0,1},{1,0},{2,3},{3,2},{4,5},{5,4},{6,7},{7,6},{8,9},{9,8},{10,11... | collective-permute-start | bytes 3686408 | tf_op jit(solution)/shard_map/ppermute | solution.py:261
  34.7 31.8 %collective-permute-start.4 = (bf16[192,3200]{1,0:T(8,128)(2,1)S(1)}, bf16[192,3200]{1,0:T(8,128)(2,1)S(1)}, u32[]{:S(2)}, u32[]{:S(2)}) collective-permute-start(bf16[192,3200]{1,0:T(8,128)(2,1)S(1)} %collective-permute-done.3.refs_0_), channel_id=1, source_target_pairs={{0,60},{1,61},{2,62},{3,63},{4,0},{5,1},{6,2},{7,3},{8,4},{9,5},{1... | collective-permute-start | bytes 3686408 | tf_op jit(solution)/shard_map/ppermute | solution.py:261
  34.8 1.3 %copy-start.3 = (bf16[192,3200]{1,0:T(8,128)(2,1)S(1)}, bf16[192,3200]{1,0:T(8,128)(2,1)}, u32[]{:S(2)}) copy-start(bf16[192,3200]{1,0:T(8,128)(2,1)} %refs_0_.1) | copy-start | bytes 3686404
  36.0 0.7 copy-start.4
  36.7 0.7 copy-start.5
  37.4 30.8 %copy-start.6 = (s32[3]{0:T(128)S(1)}, s32[3]{0:T(128)}, u32[]{:S(2)}) copy-start(s32[3]{0:T(128)} %lag_ref.1) | copy-start | bytes 40
  51.7 1.8 %copy-start = (bf16[3,800,768]{2,1,0:T(8,128)(2,1)}, bf16[3,800,768]{2,1,0:T(8,128)(2,1)S(1)}, u32[]{:S(2)}) copy-start(bf16[3,800,768]{2,1,0:T(8,128)(2,1)S(1)} %get-tuple-element.15.y) | copy-start | bytes 11059204
  61.8 6.4 %collective-permute-start.10 = (bf16[192,3200]{1,0:T(8,128)(2,1)}, bf16[192,3200]{1,0:T(8,128)(2,1)}, u32[]{:S(2)}, u32[]{:S(2)}) collective-permute-start(bf16[192,3200]{1,0:T(8,128)(2,1)} %collective-permute-done.7.refs_3_), channel_id=1, source_target_pairs={{0,1},{1,0},{2,3},{3,2},{4,5},{5,4},{6,7},{7,6},{8,9},{9,8},{10,11... | collective-permute-start | bytes 3686408 | tf_op jit(solution)/shard_map/ppermute | solution.py:261
  64.6 5.1 %collective-permute-start.9 = (bf16[192,3200]{1,0:T(8,128)(2,1)}, bf16[192,3200]{1,0:T(8,128)(2,1)}, u32[]{:S(2)}, u32[]{:S(2)}) collective-permute-start(bf16[192,3200]{1,0:T(8,128)(2,1)} %collective-permute-done.8.refs_1_), channel_id=1, source_target_pairs={{60,61},{61,60},{62,63},{63,62},{124,125},{125,124},{126,127},{127... | collective-permute-start | bytes 3686408 | tf_op jit(solution)/shard_map/ppermute | solution.py:280
  66.5 29.1 %collective-permute-start.5 = (bf16[192,3200]{1,0:T(8,128)(2,1)S(1)}, bf16[192,3200]{1,0:T(8,128)(2,1)}, u32[]{:S(2)}, u32[]{:S(2)}) collective-permute-start(bf16[192,3200]{1,0:T(8,128)(2,1)S(1)} %collective-permute-done.4.refs_0_), channel_id=1, source_target_pairs={{0,2},{1,3},{2,0},{3,1},{4,6},{5,7},{6,4},{7,5},{8,10},{9,11},{10,... | collective-permute-start | bytes 3686408 | tf_op jit(solution)/shard_map/ppermute | solution.py:261
  68.1 27.5 %collective-permute-start.6 = (bf16[192,3200]{1,0:T(8,128)(2,1)S(1)}, bf16[192,3200]{1,0:T(8,128)(2,1)}, u32[]{:S(2)}, u32[]{:S(2)}) collective-permute-start(bf16[192,3200]{1,0:T(8,128)(2,1)S(1)} %collective-permute-done.4.refs_0_), channel_id=1, source_target_pairs={{0,1},{1,0},{2,3},{3,2},{4,5},{5,4},{6,7},{7,6},{8,9},{9,8},{10,11... | collective-permute-start | bytes 3686408 | tf_op jit(solution)/shard_map/ppermute | solution.py:261
  69.7 2.0 %copy-start.1 = (bf16[3,800,768]{2,1,0:T(8,128)(2,1)S(1)}, bf16[3,800,768]{2,1,0:T(8,128)(2,1)}, u32[]{:S(2)}) copy-start(bf16[3,800,768]{2,1,0:T(8,128)(2,1)} %copy-done) | copy-start | bytes 11059204
  71.8 32.2 %copy-start.2 = (bf16[3,800,768]{2,1,0:T(8,128)(2,1)S(1)}, bf16[3,800,768]{2,1,0:T(8,128)(2,1)}, u32[]{:S(2)}) copy-start(bf16[3,800,768]{2,1,0:T(8,128)(2,1)} %copy-done) | copy-start | bytes 11059204
  95.6 6.6 %collective-permute-start.11 = (bf16[192,3200]{1,0:T(8,128)(2,1)}, bf16[192,3200]{1,0:T(8,128)(2,1)S(1)}, u32[]{:S(2)}, u32[]{:S(2)}) collective-permute-start(bf16[192,3200]{1,0:T(8,128)(2,1)} %collective-permute-done.6.refs_1_), channel_id=1, source_target_pairs={{56,57},{57,56},{58,59},{59,58},{60,61},{61,60},{62,63},{63,62},{1... | collective-permute-start | bytes 3686408 | tf_op jit(solution)/shard_map/ppermute | solution.py:280
  99.5 4.5 %collective-permute-start.12 = (bf16[192,3200]{1,0:T(8,128)(2,1)}, bf16[192,3200]{1,0:T(8,128)(2,1)S(1)}, u32[]{:S(2)}, u32[]{:S(2)}) collective-permute-start(bf16[192,3200]{1,0:T(8,128)(2,1)} %collective-permute-done.5.refs_0_), channel_id=1, source_target_pairs={{0,1},{1,0},{2,3},{3,2},{4,5},{5,4},{6,7},{7,6},{8,9},{9,8},{10,11... | collective-permute-start | bytes 3686408 | tf_op jit(solution)/shard_map/ppermute | solution.py:261

commit v6 on v5

--- a/solution.py
+++ b/solution.py
@@ -299,19 +299,19 @@
         [(0, 0, own), (1, 0, own_core), (2, 0, across), (3, 0, across_core)], frames,
     )
     after_ring = after(after_ring, y)
-    next_across, next_beside = lax.optimization_barrier((next_across, next_beside, y))[:2]
+    next_beside = after(next_beside, y)
+    next_across = after(next_across, y)
     after_across = cross(after_ring, 2)
     after_beside = beside(after_ring, 2)
+    next_core_wrap = swap_wrapped(next_beside, 1)
     next_across_core = core(next_across)
-    next_core_wrap = swap_wrapped(next_beside, 1)
     tiles = later_tile(
         1, flags, y,
         [next_ring, next_beside, next_core_wrap, next_across, next_across_core], tiles, frames,
     )
-    after_across, after_beside, tiles = lax.optimization_barrier(
-        (after_across, after_beside, tiles)
-    )
+    after_across, tiles = lax.optimization_barrier((after_across, tiles))
     after_across_core = core(after_across)
+    after_beside, tiles = lax.optimization_barrier((after_beside, tiles))
     after_core_wrap = swap_wrapped(after_beside, 2)
     after_across, after_beside = fetch(after_across, after_beside)
     return later_tile(

time: 110 us -> 109 us (level)
  waiting for transfers between devices: 55.8 us -> 54.1 us
    ppermute x2, starting transfers between devices: 5.81 us -> 9.48 us  [swap_wrapped(): return lax.ppermute(array, AXES, route)]
    ppermute x11, starting transfers between devices: 11.3 us -> 7.98 us  [move(): return lax.ppermute(array, AXES, route)]
    ppermute x11, waiting for transfers between devices: 53.4 us -> 51.5 us  [move(): return lax.ppermute(array, AXES, route)]
  transfers between devices with their start and end apart: 13 -> 13, of which waited for: 7 -> 8; matrix products, arithmetic and copies ran while one was open for 0% -> 0% of each run, Pallas kernels for 22% -> 22%
where the time goes in v6:
time: 109 us
  waiting for transfers between devices  54.1 us (50%)
  Pallas kernels  30.3 us (28%)
  starting transfers between devices  17.5 us (16%)
  local copies, waits for them, and re-layouts  6.46 us (6%)
    ppermute x11, waiting for transfers between devices, move(): return lax.ppermute(array, AXES, route)  51.5 us
    pallas_call x2, Pallas kernels, later_tile(): pl.pallas_call(functools.partial(later_kernel, k, frames), out_shape=jax....  14.4 us
    pallas_call x1, Pallas kernels, first_tile(): pl.pallas_call(functools.partial(first_kernel, places, frames, n), out_sh...  14.3 us
    ppermute x2, starting transfers between devices, swap_wrapped(): return lax.ppermute(array, AXES, route)  9.48 us
    ppermute x11, starting transfers between devices, move(): return lax.ppermute(array, AXES, route)  7.98 us
    unnamed x14, local copies, waits for them, and re-layouts  6.46 us
    ppermute x2, waiting for transfers between devices, swap_wrapped(): return lax.ppermute(array, AXES, route)  2.61 us
  transfers between devices with their start and end apart: 13, of which 8 were waited for; matrix products, arithmetic and copies ran while one was open for 0% of the time, Pallas kernels for 22%

profile of v6, /device:TPU:121, one launch (start us, length us, event | category | flops | bytes accessed | tf_op | source)
XLA Modules:
  0.0 108.7 jit_solution(13597299870307768001)
XLA Ops:
  0.0 2.7 %collective-permute-start.1 = (bf16[192,3200]{1,0:T(8,128)(2,1)}, bf16[192,3200]{1,0:T(8,128)(2,1)}, u32[]{:S(2)}, u32[]{:S(2)}) collective-permute-start(bf16[192,3200]{1,0:T(8,128)(2,1)} %refs_0_.1), channel_id=1, source_target_pairs={{0,2},{1,3},{2,0},{3,1},{4,6},{5,7},{6,4},{7,5},{8,10},{9,11},{10,... | collective-permute-start | bytes 3686408 | tf_op jit(solution)/shard_map/ppermute | solution.py:261
  2.7 0.5 collective-permute-start.3
  3.2 1.2 %collective-permute-start = (bf16[192,3200]{1,0:T(8,128)(2,1)}, bf16[192,3200]{1,0:T(8,128)(2,1)}, u32[]{:S(2)}, u32[]{:S(2)}) collective-permute-start(bf16[192,3200]{1,0:T(8,128)(2,1)} %refs_0_.1), channel_id=1, source_target_pairs={{0,1},{1,0},{2,3},{3,2},{4,5},{5,4},{6,7},{7,6},{8,9},{9,8},{10,11... | collective-permute-start | bytes 3686408 | tf_op jit(solution)/shard_map/ppermute | solution.py:261
  4.4 25.3 %collective-permute-done.1.refs_2_ = bf16[192,3200]{1,0:T(8,128)(2,1)} collective-permute-done((bf16[192,3200]{1,0:T(8,128)(2,1)}, bf16[192,3200]{1,0:T(8,128)(2,1)}, u32[]{:S(2)}, u32[]{:S(2)}) %collective-permute-start.1) | collective-permute-done | bytes 1228832 | tf_op jit(solution)/shard_map/ppermute | solution.py:261
  29.7 1.5 %collective-permute-start.2 = (bf16[192,3200]{1,0:T(8,128)(2,1)}, bf16[192,3200]{1,0:T(8,128)(2,1)}, u32[]{:S(2)}, u32[]{:S(2)}) collective-permute-start(bf16[192,3200]{1,0:T(8,128)(2,1)} %collective-permute-done.1.refs_2_), channel_id=1, source_target_pairs={{0,1},{1,0},{2,3},{3,2},{4,5},{5,4},{6,7},{7,6},{8,9},{9,8},{10,11... | collective-permute-start | bytes 3686408 | tf_op jit(solution)/shard_map/ppermute | solution.py:261
  31.3 2.6 %collective-permute-done.3.refs_0_ = bf16[192,3200]{1,0:T(8,128)(2,1)S(1)} collective-permute-done((bf16[192,3200]{1,0:T(8,128)(2,1)}, bf16[192,3200]{1,0:T(8,128)(2,1)S(1)}, u32[]{:S(2)}, u32[]{:S(2)}) %collective-permute-start.3) | collective-permute-done | bytes 1228832 | tf_op jit(solution)/shard_map/ppermute | solution.py:261
  33.8 0.3 collective-permute-start.6
  34.2 0.6 collective-permute-start.8
  34.7 0.0 collective-permute-start.4
  34.7 0.0 collective-permute-done.refs_1_
  34.7 0.0 collective-permute-done.2.refs_3_
  34.7 0.0 copy-start.3
  34.7 1.3 %copy-done.3 = bf16[192,3200]{1,0:T(8,128)(2,1)S(1)} copy-done((bf16[192,3200]{1,0:T(8,128)(2,1)S(1)}, bf16[192,3200]{1,0:T(8,128)(2,1)}, u32[]{:S(2)}) %copy-start.3) | copy-done | bytes 1228824
  36.0 0.0 copy-start.4
  36.0 0.7 copy-done.4
  36.7 0.0 copy-start.5
  36.7 0.7 copy-done.5
  37.4 0.0 copy-start.6
  37.4 14.3 %first_tile.1 = (bf16[3,800,3200]{2,1,0:T(8,128)(2,1)}, bf16[3,800,768]{2,1,0:T(8,128)(2,1)S(1)}) custom-call(s32[1]{0:T(128)} %bitcast.3.me_ref, s32[3]{0:T(128)S(1)} %copy-done.5, s32[768]{0:T(1024)S(1)} %copy-done.4, bf16[192,3200]{1,0:T(8,128)(2,1)S(1)} %copy-done.3, bf16[192,3200]{1,0:T(8,128)(2,1)} %collective-permute-done.refs_1_, ...), custom_call_target="tpu_custom_call" | custom-call | flops 10695475200 | bytes 10035200 | tf_op jit(solution)/shard_map/first_tile/pallas_call | solution.py:157
  51.6 0.0 copy-start
  51.6 1.8 %copy-done = bf16[3,800,768]{2,1,0:T(8,128)(2,1)} copy-done((bf16[3,800,768]{2,1,0:T(8,128)(2,1)}, bf16[3,800,768]{2,1,0:T(8,128)(2,1)S(1)}, u32[]{:S(2)}) %copy-start) | copy-done | bytes 3686424
  53.4 7.2 %collective-permute-done.6.refs_1_ = bf16[192,3200]{1,0:T(8,128)(2,1)} collective-permute-done((bf16[192,3200]{1,0:T(8,128)(2,1)S(1)}, bf16[192,3200]{1,0:T(8,128)(2,1)}, u32[]{:S(2)}, u32[]{:S(2)}) %collective-permute-start.6) | collective-permute-done | bytes 1228832 | tf_op jit(solution)/shard_map/ppermute | solution.py:261
  60.6 4.7 %collective-permute-start.7 = (bf16[192,3200]{1,0:T(8,128)(2,1)}, bf16[192,3200]{1,0:T(8,128)(2,1)}, u32[]{:S(2)}, u32[]{:S(2)}) collective-permute-start(bf16[192,3200]{1,0:T(8,128)(2,1)} %collective-permute-done.6.refs_1_), channel_id=1, source_target_pairs={{60,61},{61,60},{62,63},{63,62},{124,125},{125,124},{126,127},{127... | collective-permute-start | bytes 3686408 | tf_op jit(solution)/shard_map/ppermute | solution.py:280
  65.3 0.0 collective-permute-done.8.refs_3_
  65.3 0.1 collective-permute-start.9
  65.4 0.0 collective-permute-done.4.refs_0_
  65.4 0.9 collective-permute-start.5
  66.4 0.0 collective-permute-start.10
  66.4 0.1 add_convert_fusion
  66.4 0.0 copy-done.6
  66.4 0.1 pad_add_fusion.flags
  66.5 1.7 %collective-permute-done.7.refs_2_ = bf16[192,3200]{1,0:T(8,128)(2,1)} collective-permute-done((bf16[192,3200]{1,0:T(8,128)(2,1)}, bf16[192,3200]{1,0:T(8,128)(2,1)}, u32[]{:S(2)}, u32[]{:S(2)}) %collective-permute-start.7) | collective-permute-done | bytes 1228832 | tf_op jit(solution)/shard_map/ppermute | solution.py:280
  68.2 1.8 %collective-permute-done.9.refs_4_ = bf16[192,3200]{1,0:T(8,128)(2,1)} collective-permute-done((bf16[192,3200]{1,0:T(8,128)(2,1)}, bf16[192,3200]{1,0:T(8,128)(2,1)}, u32[]{:S(2)}, u32[]{:S(2)}) %collective-permute-start.9) | collective-permute-done | bytes 1228832 | tf_op jit(solution)/shard_map/ppermute | solution.py:261
  69.9 0.0 copy-start.1
  69.9 2.0 %copy-done.1 = bf16[3,800,768]{2,1,0:T(8,128)(2,1)S(1)} copy-done((bf16[3,800,768]{2,1,0:T(8,128)(2,1)S(1)}, bf16[3,800,768]{2,1,0:T(8,128)(2,1)}, u32[]{:S(2)}) %copy-start.1) | copy-done | bytes 3686424
  72.0 0.0 copy-start.2
  72.0 8.4 %later_tile.2.refs_5_ = bf16[3,800,3200]{2,1,0:T(8,128)(2,1)} custom-call(s32[6]{0:T(128)S(1)} %pad_add_fusion.flags, bf16[3,800,768]{2,1,0:T(8,128)(2,1)S(1)} %copy-done.1, bf16[192,3200]{1,0:T(8,128)(2,1)S(1)} %collective-permute-done.3.refs_0_, bf16[192,3200]{1,0:T(8,128)(2,1)} %collective-permute-done.6.refs_1_, ...), custom_call_target="tpu_custom_call", output_to_operand_aliasing={{}: (7, {})} | custom-call | flops 7864320000 | bytes 10035200 | tf_op jit(solution)/shard_map/later_tile/pallas_call | solution.py:203
  80.4 12.9 %collective-permute-done.5.refs_0_ = bf16[192,3200]{1,0:T(8,128)(2,1)} collective-permute-done((bf16[192,3200]{1,0:T(8,128)(2,1)S(1)}, bf16[192,3200]{1,0:T(8,128)(2,1)}, u32[]{:S(2)}, u32[]{:S(2)}) %collective-permute-start.5) | collective-permute-done | bytes 1228832 | tf_op jit(solution)/shard_map/ppermute | solution.py:261
  93.3 0.0 collective-permute-done.10.refs_1_
  93.3 4.8 %collective-permute-start.11 = (bf16[192,3200]{1,0:T(8,128)(2,1)}, bf16[192,3200]{1,0:T(8,128)(2,1)S(1)}, u32[]{:S(2)}, u32[]{:S(2)}) collective-permute-start(bf16[192,3200]{1,0:T(8,128)(2,1)} %collective-permute-done.10.refs_1_), channel_id=1, source_target_pairs={{56,57},{57,56},{58,59},{59,58},{60,61},{61,60},{62,63},{63,62},{1... | collective-permute-start | bytes 3686408 | tf_op jit(solution)/shard_map/ppermute | solution.py:280
  98.2 0.1 collective-permute-start.12
  98.2 1.7 %fetch.1 = (bf16[192,3200]{1,0:T(8,128)(2,1)S(1)}, bf16[192,3200]{1,0:T(8,128)(2,1)S(1)}) custom-call(bf16[192,3200]{1,0:T(8,128)(2,1)} %collective-permute-done.5.refs_0_, bf16[192,3200]{1,0:T(8,128)(2,1)} %collective-permute-done.10.refs_1_), custom_call_target="tpu_custom_call" | custom-call | tf_op jit(solution)/shard_map/fetch/pallas_call | solution.py:233
  99.9 1.0 collective-permute-done.11.refs_2_
  100.9 1.8 %collective-permute-done.12.refs_4_ = bf16[192,3200]{1,0:T(8,128)(2,1)S(1)} collective-permute-done((bf16[192,3200]{1,0:T(8,128)(2,1)}, bf16[192,3200]{1,0:T(8,128)(2,1)S(1)}, u32[]{:S(2)}, u32[]{:S(2)}) %collective-permute-start.12) | collective-permute-done | bytes 1228832 | tf_op jit(solution)/shard_map/ppermute | solution.py:261
  102.6 0.0 copy-done.2
  102.6 5.9 %later_tile.3 = bf16[3,800,3200]{2,1,0:T(8,128)(2,1)} custom-call(s32[6]{0:T(128)S(1)} %pad_add_fusion.flags, bf16[3,800,768]{2,1,0:T(8,128)(2,1)S(1)} %copy-done.2, bf16[192,3200]{1,0:T(8,128)(2,1)S(1)} %collective-permute-done.4.refs_0_, bf16[192,3200]{1,0:T(8,128)(2,1)S(1)} %get-tuple-element.24.refs_1_, ...), custom_call_target="tpu_custom_call", output_to_operand_aliasing={{}: (7, {})} | custom-call | flops 7864320000 | bytes 10035200 | tf_op jit(solution)/shard_map/later_tile/pallas_call | solution.py:203
Async XLA Ops:
  0.0 29.7 %collective-permute-start.1 = (bf16[192,3200]{1,0:T(8,128)(2,1)}, bf16[192,3200]{1,0:T(8,128)(2,1)}, u32[]{:S(2)}, u32[]{:S(2)}) collective-permute-start(bf16[192,3200]{1,0:T(8,128)(2,1)} %refs_0_.1), channel_id=1, source_target_pairs={{0,2},{1,3},{2,0},{3,1},{4,6},{5,7},{6,4},{7,5},{8,10},{9,11},{10,... | collective-permute-start | bytes 3686408 | tf_op jit(solution)/shard_map/ppermute | solution.py:261
  2.7 31.1 %collective-permute-start.3 = (bf16[192,3200]{1,0:T(8,128)(2,1)}, bf16[192,3200]{1,0:T(8,128)(2,1)S(1)}, u32[]{:S(2)}, u32[]{:S(2)}) collective-permute-start(bf16[192,3200]{1,0:T(8,128)(2,1)} %refs_0_.1), channel_id=1, source_target_pairs={{0,60},{1,61},{2,62},{3,63},{4,0},{5,1},{6,2},{7,3},{8,4},{9,5},{1... | collective-permute-start | bytes 3686408 | tf_op jit(solution)/shard_map/ppermute | solution.py:261
  3.2 31.5 %collective-permute-start = (bf16[192,3200]{1,0:T(8,128)(2,1)}, bf16[192,3200]{1,0:T(8,128)(2,1)}, u32[]{:S(2)}, u32[]{:S(2)}) collective-permute-start(bf16[192,3200]{1,0:T(8,128)(2,1)} %refs_0_.1), channel_id=1, source_target_pairs={{0,1},{1,0},{2,3},{3,2},{4,5},{5,4},{6,7},{7,6},{8,9},{9,8},{10,11... | collective-permute-start | bytes 3686408 | tf_op jit(solution)/shard_map/ppermute | solution.py:261
  29.7 5.0 %collective-permute-start.2 = (bf16[192,3200]{1,0:T(8,128)(2,1)}, bf16[192,3200]{1,0:T(8,128)(2,1)}, u32[]{:S(2)}, u32[]{:S(2)}) collective-permute-start(bf16[192,3200]{1,0:T(8,128)(2,1)} %collective-permute-done.1.refs_2_), channel_id=1, source_target_pairs={{0,1},{1,0},{2,3},{3,2},{4,5},{5,4},{6,7},{7,6},{8,9},{9,8},{10,11... | collective-permute-start | bytes 3686408 | tf_op jit(solution)/shard_map/ppermute | solution.py:261
  33.8 26.8 %collective-permute-start.6 = (bf16[192,3200]{1,0:T(8,128)(2,1)S(1)}, bf16[192,3200]{1,0:T(8,128)(2,1)}, u32[]{:S(2)}, u32[]{:S(2)}) collective-permute-start(bf16[192,3200]{1,0:T(8,128)(2,1)S(1)} %collective-permute-done.3.refs_0_), channel_id=1, source_target_pairs={{0,1},{1,0},{2,3},{3,2},{4,5},{5,4},{6,7},{7,6},{8,9},{9,8},{10,11... | collective-permute-start | bytes 3686408 | tf_op jit(solution)/shard_map/ppermute | solution.py:261
  34.2 31.1 %collective-permute-start.8 = (bf16[192,3200]{1,0:T(8,128)(2,1)S(1)}, bf16[192,3200]{1,0:T(8,128)(2,1)}, u32[]{:S(2)}, u32[]{:S(2)}) collective-permute-start(bf16[192,3200]{1,0:T(8,128)(2,1)S(1)} %collective-permute-done.3.refs_0_), channel_id=1, source_target_pairs={{0,2},{1,3},{2,0},{3,1},{4,6},{5,7},{6,4},{7,5},{8,10},{9,11},{10,... | collective-permute-start | bytes 3686408 | tf_op jit(solution)/shard_map/ppermute | solution.py:261
  34.7 30.7 %collective-permute-start.4 = (bf16[192,3200]{1,0:T(8,128)(2,1)S(1)}, bf16[192,3200]{1,0:T(8,128)(2,1)S(1)}, u32[]{:S(2)}, u32[]{:S(2)}) collective-permute-start(bf16[192,3200]{1,0:T(8,128)(2,1)S(1)} %collective-permute-done.3.refs_0_), channel_id=1, source_target_pairs={{0,60},{1,61},{2,62},{3,63},{4,0},{5,1},{6,2},{7,3},{8,4},{9,5},{1... | collective-permute-start | bytes 3686408 | tf_op jit(solution)/shard_map/ppermute | solution.py:261
  34.7 1.3 %copy-start.3 = (bf16[192,3200]{1,0:T(8,128)(2,1)S(1)}, bf16[192,3200]{1,0:T(8,128)(2,1)}, u32[]{:S(2)}) copy-start(bf16[192,3200]{1,0:T(8,128)(2,1)} %refs_0_.1) | copy-start | bytes 3686404
  36.0 0.7 copy-start.4
  36.7 0.7 copy-start.5
  37.4 29.1 %copy-start.6 = (s32[3]{0:T(128)S(1)}, s32[3]{0:T(128)}, u32[]{:S(2)}) copy-start(s32[3]{0:T(128)} %lag_ref.1) | copy-start | bytes 40
  51.6 1.8 %copy-start = (bf16[3,800,768]{2,1,0:T(8,128)(2,1)}, bf16[3,800,768]{2,1,0:T(8,128)(2,1)S(1)}, u32[]{:S(2)}) copy-start(bf16[3,800,768]{2,1,0:T(8,128)(2,1)S(1)} %get-tuple-element.16.y) | copy-start | bytes 11059204
  60.6 7.6 %collective-permute-start.7 = (bf16[192,3200]{1,0:T(8,128)(2,1)}, bf16[192,3200]{1,0:T(8,128)(2,1)}, u32[]{:S(2)}, u32[]{:S(2)}) collective-permute-start(bf16[192,3200]{1,0:T(8,128)(2,1)} %collective-permute-done.6.refs_1_), channel_id=1, source_target_pairs={{60,61},{61,60},{62,63},{63,62},{124,125},{125,124},{126,127},{127... | collective-permute-start | bytes 3686408 | tf_op jit(solution)/shard_map/ppermute | solution.py:280
  65.3 4.6 %collective-permute-start.9 = (bf16[192,3200]{1,0:T(8,128)(2,1)}, bf16[192,3200]{1,0:T(8,128)(2,1)}, u32[]{:S(2)}, u32[]{:S(2)}) collective-permute-start(bf16[192,3200]{1,0:T(8,128)(2,1)} %collective-permute-done.8.refs_3_), channel_id=1, source_target_pairs={{0,1},{1,0},{2,3},{3,2},{4,5},{5,4},{6,7},{7,6},{8,9},{9,8},{10,11... | collective-permute-start | bytes 3686408 | tf_op jit(solution)/shard_map/ppermute | solution.py:261
  65.4 27.9 %collective-permute-start.5 = (bf16[192,3200]{1,0:T(8,128)(2,1)S(1)}, bf16[192,3200]{1,0:T(8,128)(2,1)}, u32[]{:S(2)}, u32[]{:S(2)}) collective-permute-start(bf16[192,3200]{1,0:T(8,128)(2,1)S(1)} %collective-permute-done.4.refs_0_), channel_id=1, source_target_pairs={{0,2},{1,3},{2,0},{3,1},{4,6},{5,7},{6,4},{7,5},{8,10},{9,11},{10,... | collective-permute-start | bytes 3686408 | tf_op jit(solution)/shard_map/ppermute | solution.py:261
  66.4 27.0 %collective-permute-start.10 = (bf16[192,3200]{1,0:T(8,128)(2,1)S(1)}, bf16[192,3200]{1,0:T(8,128)(2,1)}, u32[]{:S(2)}, u32[]{:S(2)}) collective-permute-start(bf16[192,3200]{1,0:T(8,128)(2,1)S(1)} %collective-permute-done.4.refs_0_), channel_id=1, source_target_pairs={{0,1},{1,0},{2,3},{3,2},{4,5},{5,4},{6,7},{7,6},{8,9},{9,8},{10,11... | collective-permute-start | bytes 3686408 | tf_op jit(solution)/shard_map/ppermute | solution.py:261
  69.9 2.0 %copy-start.1 = (bf16[3,800,768]{2,1,0:T(8,128)(2,1)S(1)}, bf16[3,800,768]{2,1,0:T(8,128)(2,1)}, u32[]{:S(2)}) copy-start(bf16[3,800,768]{2,1,0:T(8,128)(2,1)} %copy-done) | copy-start | bytes 11059204
  72.0 30.7 %copy-start.2 = (bf16[3,800,768]{2,1,0:T(8,128)(2,1)S(1)}, bf16[3,800,768]{2,1,0:T(8,128)(2,1)}, u32[]{:S(2)}) copy-start(bf16[3,800,768]{2,1,0:T(8,128)(2,1)} %copy-done) | copy-start | bytes 11059204
  93.3 7.5 %collective-permute-start.11 = (bf16[192,3200]{1,0:T(8,128)(2,1)}, bf16[192,3200]{1,0:T(8,128)(2,1)S(1)}, u32[]{:S(2)}, u32[]{:S(2)}) collective-permute-start(bf16[192,3200]{1,0:T(8,128)(2,1)} %collective-permute-done.10.refs_1_), channel_id=1, source_target_pairs={{56,57},{57,56},{58,59},{59,58},{60,61},{61,60},{62,63},{63,62},{1... | collective-permute-start | bytes 3686408 | tf_op jit(solution)/shard_map/ppermute | solution.py:280
  98.2 4.5 %collective-permute-start.12 = (bf16[192,3200]{1,0:T(8,128)(2,1)}, bf16[192,3200]{1,0:T(8,128)(2,1)S(1)}, u32[]{:S(2)}, u32[]{:S(2)}) collective-permute-start(bf16[192,3200]{1,0:T(8,128)(2,1)} %collective-permute-done.5.refs_0_), channel_id=1, source_target_pairs={{0,1},{1,0},{2,3},{3,2},{4,5},{5,4},{6,7},{7,6},{8,9},{9,8},{10,11... | collective-permute-start | bytes 3686408 | tf_op jit(solution)/shard_map/ppermute | solution.py:261

commit v7 on v6

--- a/solution.py
+++ b/solution.py
@@ -15,7 +15,7 @@
 
 
 def spans(first, last):
-    edges = [first, *range(first + CHUNK // 2, last, CHUNK), last]
+    edges = [first, *range(first + CHUNK // 2, last - 128, CHUNK), last - 128, last]
     return [(a, b - a) for a, b in zip(edges, edges[1:])]
 
 

time: 109 us -> 109 us (level)
  no operation moved by 1% of the time
where the time goes in v7:
time: 109 us
  waiting for transfers between devices  54.1 us (50%)
  Pallas kernels  30.3 us (28%)
  starting transfers between devices  17.5 us (16%)
  local copies, waits for them, and re-layouts  6.46 us (6%)
    ppermute x11, waiting for transfers between devices, move(): return lax.ppermute(array, AXES, route)  51.5 us
    pallas_call x2, Pallas kernels, later_tile(): pl.pallas_call(functools.partial(later_kernel, k, frames), out_shape=jax....  14.3 us
    pallas_call x1, Pallas kernels, first_tile(): pl.pallas_call(functools.partial(first_kernel, places, frames, n), out_sh...  14.3 us
    ppermute x2, starting transfers between devices, swap_wrapped(): return lax.ppermute(array, AXES, route)  9.48 us
    ppermute x11, starting transfers between devices, move(): return lax.ppermute(array, AXES, route)  7.98 us
    unnamed x14, local copies, waits for them, and re-layouts  6.46 us
    ppermute x2, waiting for transfers between devices, swap_wrapped(): return lax.ppermute(array, AXES, route)  2.61 us
  transfers between devices with their start and end apart: 13, of which 8 were waited for; matrix products, arithmetic and copies ran while one was open for 0% of the time, Pallas kernels for 22%

profile of v7, /device:TPU:121, one launch (start us, length us, event | category | flops | bytes accessed | tf_op | source)
XLA Modules:
  0.0 108.7 jit_solution(14501474905077279162)
XLA Ops:
  0.0 2.7 %collective-permute-start.1 = (bf16[192,3200]{1,0:T(8,128)(2,1)}, bf16[192,3200]{1,0:T(8,128)(2,1)}, u32[]{:S(2)}, u32[]{:S(2)}) collective-permute-start(bf16[192,3200]{1,0:T(8,128)(2,1)} %refs_0_.1), channel_id=1, source_target_pairs={{0,2},{1,3},{2,0},{3,1},{4,6},{5,7},{6,4},{7,5},{8,10},{9,11},{10,... | collective-permute-start | bytes 3686408 | tf_op jit(solution)/shard_map/ppermute | solution.py:261
  2.7 0.5 collective-permute-start.3
  3.2 1.2 %collective-permute-start = (bf16[192,3200]{1,0:T(8,128)(2,1)}, bf16[192,3200]{1,0:T(8,128)(2,1)}, u32[]{:S(2)}, u32[]{:S(2)}) collective-permute-start(bf16[192,3200]{1,0:T(8,128)(2,1)} %refs_0_.1), channel_id=1, source_target_pairs={{0,1},{1,0},{2,3},{3,2},{4,5},{5,4},{6,7},{7,6},{8,9},{9,8},{10,11... | collective-permute-start | bytes 3686408 | tf_op jit(solution)/shard_map/ppermute | solution.py:261
  4.4 25.3 %collective-permute-done.1.refs_2_ = bf16[192,3200]{1,0:T(8,128)(2,1)} collective-permute-done((bf16[192,3200]{1,0:T(8,128)(2,1)}, bf16[192,3200]{1,0:T(8,128)(2,1)}, u32[]{:S(2)}, u32[]{:S(2)}) %collective-permute-start.1) | collective-permute-done | bytes 1228832 | tf_op jit(solution)/shard_map/ppermute | solution.py:261
  29.7 1.5 %collective-permute-start.2 = (bf16[192,3200]{1,0:T(8,128)(2,1)}, bf16[192,3200]{1,0:T(8,128)(2,1)}, u32[]{:S(2)}, u32[]{:S(2)}) collective-permute-start(bf16[192,3200]{1,0:T(8,128)(2,1)} %collective-permute-done.1.refs_2_), channel_id=1, source_target_pairs={{0,1},{1,0},{2,3},{3,2},{4,5},{5,4},{6,7},{7,6},{8,9},{9,8},{10,11... | collective-permute-start | bytes 3686408 | tf_op jit(solution)/shard_map/ppermute | solution.py:261
  31.3 2.6 %collective-permute-done.3.refs_0_ = bf16[192,3200]{1,0:T(8,128)(2,1)S(1)} collective-permute-done((bf16[192,3200]{1,0:T(8,128)(2,1)}, bf16[192,3200]{1,0:T(8,128)(2,1)S(1)}, u32[]{:S(2)}, u32[]{:S(2)}) %collective-permute-start.3) | collective-permute-done | bytes 1228832 | tf_op jit(solution)/shard_map/ppermute | solution.py:261
  33.8 0.3 collective-permute-start.6
  34.2 0.6 collective-permute-start.8
  34.7 0.0 collective-permute-start.4
  34.7 0.0 collective-permute-done.refs_1_
  34.7 0.0 collective-permute-done.2.refs_3_
  34.7 0.0 copy-start.3
  34.7 1.3 %copy-done.3 = bf16[192,3200]{1,0:T(8,128)(2,1)S(1)} copy-done((bf16[192,3200]{1,0:T(8,128)(2,1)S(1)}, bf16[192,3200]{1,0:T(8,128)(2,1)}, u32[]{:S(2)}) %copy-start.3) | copy-done | bytes 1228824
  36.0 0.0 copy-start.4
  36.0 0.7 copy-done.4
  36.7 0.0 copy-start.5
  36.7 0.7 copy-done.5
  37.4 0.0 copy-start.6
  37.4 14.3 %first_tile.1 = (bf16[3,800,3200]{2,1,0:T(8,128)(2,1)}, bf16[3,800,768]{2,1,0:T(8,128)(2,1)S(1)}) custom-call(s32[1]{0:T(128)} %bitcast.3.me_ref, s32[3]{0:T(128)S(1)} %copy-done.5, s32[768]{0:T(1024)S(1)} %copy-done.4, bf16[192,3200]{1,0:T(8,128)(2,1)S(1)} %copy-done.3, bf16[192,3200]{1,0:T(8,128)(2,1)} %collective-permute-done.refs_1_, ...), custom_call_target="tpu_custom_call" | custom-call | flops 10695475200 | bytes 10035200 | tf_op jit(solution)/shard_map/first_tile/pallas_call | solution.py:157
  51.6 0.0 copy-start
  51.6 1.8 %copy-done = bf16[3,800,768]{2,1,0:T(8,128)(2,1)} copy-done((bf16[3,800,768]{2,1,0:T(8,128)(2,1)}, bf16[3,800,768]{2,1,0:T(8,128)(2,1)S(1)}, u32[]{:S(2)}) %copy-start) | copy-done | bytes 3686424
  53.4 7.2 %collective-permute-done.6.refs_1_ = bf16[192,3200]{1,0:T(8,128)(2,1)} collective-permute-done((bf16[192,3200]{1,0:T(8,128)(2,1)S(1)}, bf16[192,3200]{1,0:T(8,128)(2,1)}, u32[]{:S(2)}, u32[]{:S(2)}) %collective-permute-start.6) | collective-permute-done | bytes 1228832 | tf_op jit(solution)/shard_map/ppermute | solution.py:261
  60.6 4.7 %collective-permute-start.7 = (bf16[192,3200]{1,0:T(8,128)(2,1)}, bf16[192,3200]{1,0:T(8,128)(2,1)}, u32[]{:S(2)}, u32[]{:S(2)}) collective-permute-start(bf16[192,3200]{1,0:T(8,128)(2,1)} %collective-permute-done.6.refs_1_), channel_id=1, source_target_pairs={{60,61},{61,60},{62,63},{63,62},{124,125},{125,124},{126,127},{127... | collective-permute-start | bytes 3686408 | tf_op jit(solution)/shard_map/ppermute | solution.py:280
  65.3 0.0 collective-permute-done.8.refs_3_
  65.3 0.1 collective-permute-start.9
  65.4 0.0 collective-permute-done.4.refs_0_
  65.4 0.9 collective-permute-start.5
  66.4 0.0 collective-permute-start.10
  66.4 0.1 add_convert_fusion
  66.4 0.0 copy-done.6
  66.4 0.1 pad_add_fusion.flags
  66.5 1.7 %collective-permute-done.7.refs_2_ = bf16[192,3200]{1,0:T(8,128)(2,1)} collective-permute-done((bf16[192,3200]{1,0:T(8,128)(2,1)}, bf16[192,3200]{1,0:T(8,128)(2,1)}, u32[]{:S(2)}, u32[]{:S(2)}) %collective-permute-start.7) | collective-permute-done | bytes 1228832 | tf_op jit(solution)/shard_map/ppermute | solution.py:280
  68.2 1.8 %collective-permute-done.9.refs_4_ = bf16[192,3200]{1,0:T(8,128)(2,1)} collective-permute-done((bf16[192,3200]{1,0:T(8,128)(2,1)}, bf16[192,3200]{1,0:T(8,128)(2,1)}, u32[]{:S(2)}, u32[]{:S(2)}) %collective-permute-start.9) | collective-permute-done | bytes 1228832 | tf_op jit(solution)/shard_map/ppermute | solution.py:261
  69.9 0.0 copy-start.1
  69.9 2.0 %copy-done.1 = bf16[3,800,768]{2,1,0:T(8,128)(2,1)S(1)} copy-done((bf16[3,800,768]{2,1,0:T(8,128)(2,1)S(1)}, bf16[3,800,768]{2,1,0:T(8,128)(2,1)}, u32[]{:S(2)}) %copy-start.1) | copy-done | bytes 3686424
  72.0 0.0 copy-start.2
  72.0 8.4 %later_tile.2.refs_5_ = bf16[3,800,3200]{2,1,0:T(8,128)(2,1)} custom-call(s32[6]{0:T(128)S(1)} %pad_add_fusion.flags, bf16[3,800,768]{2,1,0:T(8,128)(2,1)S(1)} %copy-done.1, bf16[192,3200]{1,0:T(8,128)(2,1)S(1)} %collective-permute-done.3.refs_0_, bf16[192,3200]{1,0:T(8,128)(2,1)} %collective-permute-done.6.refs_1_, ...), custom_call_target="tpu_custom_call", output_to_operand_aliasing={{}: (7, {})} | custom-call | flops 7864320000 | bytes 10035200 | tf_op jit(solution)/shard_map/later_tile/pallas_call | solution.py:203
  80.4 13.0 %collective-permute-done.5.refs_0_ = bf16[192,3200]{1,0:T(8,128)(2,1)} collective-permute-done((bf16[192,3200]{1,0:T(8,128)(2,1)S(1)}, bf16[192,3200]{1,0:T(8,128)(2,1)}, u32[]{:S(2)}, u32[]{:S(2)}) %collective-permute-start.5) | collective-permute-done | bytes 1228832 | tf_op jit(solution)/shard_map/ppermute | solution.py:261
  93.3 0.0 collective-permute-done.10.refs_1_
  93.3 4.8 %collective-permute-start.11 = (bf16[192,3200]{1,0:T(8,128)(2,1)}, bf16[192,3200]{1,0:T(8,128)(2,1)S(1)}, u32[]{:S(2)}, u32[]{:S(2)}) collective-permute-start(bf16[192,3200]{1,0:T(8,128)(2,1)} %collective-permute-done.10.refs_1_), channel_id=1, source_target_pairs={{56,57},{57,56},{58,59},{59,58},{60,61},{61,60},{62,63},{63,62},{1... | collective-permute-start | bytes 3686408 | tf_op jit(solution)/shard_map/ppermute | solution.py:280
  98.2 0.1 collective-permute-start.12
  98.2 1.7 %fetch.1 = (bf16[192,3200]{1,0:T(8,128)(2,1)S(1)}, bf16[192,3200]{1,0:T(8,128)(2,1)S(1)}) custom-call(bf16[192,3200]{1,0:T(8,128)(2,1)} %collective-permute-done.5.refs_0_, bf16[192,3200]{1,0:T(8,128)(2,1)} %collective-permute-done.10.refs_1_), custom_call_target="tpu_custom_call" | custom-call | tf_op jit(solution)/shard_map/fetch/pallas_call | solution.py:233
  99.9 1.0 collective-permute-done.11.refs_2_
  100.9 1.8 %collective-permute-done.12.refs_4_ = bf16[192,3200]{1,0:T(8,128)(2,1)S(1)} collective-permute-done((bf16[192,3200]{1,0:T(8,128)(2,1)}, bf16[192,3200]{1,0:T(8,128)(2,1)S(1)}, u32[]{:S(2)}, u32[]{:S(2)}) %collective-permute-start.12) | collective-permute-done | bytes 1228832 | tf_op jit(solution)/shard_map/ppermute | solution.py:261
  102.6 0.0 copy-done.2
  102.6 5.9 %later_tile.3 = bf16[3,800,3200]{2,1,0:T(8,128)(2,1)} custom-call(s32[6]{0:T(128)S(1)} %pad_add_fusion.flags, bf16[3,800,768]{2,1,0:T(8,128)(2,1)S(1)} %copy-done.2, bf16[192,3200]{1,0:T(8,128)(2,1)S(1)} %collective-permute-done.4.refs_0_, bf16[192,3200]{1,0:T(8,128)(2,1)S(1)} %get-tuple-element.24.refs_1_, ...), custom_call_target="tpu_custom_call", output_to_operand_aliasing={{}: (7, {})} | custom-call | flops 7864320000 | bytes 10035200 | tf_op jit(solution)/shard_map/later_tile/pallas_call | solution.py:203
Async XLA Ops:
  0.0 29.7 %collective-permute-start.1 = (bf16[192,3200]{1,0:T(8,128)(2,1)}, bf16[192,3200]{1,0:T(8,128)(2,1)}, u32[]{:S(2)}, u32[]{:S(2)}) collective-permute-start(bf16[192,3200]{1,0:T(8,128)(2,1)} %refs_0_.1), channel_id=1, source_target_pairs={{0,2},{1,3},{2,0},{3,1},{4,6},{5,7},{6,4},{7,5},{8,10},{9,11},{10,... | collective-permute-start | bytes 3686408 | tf_op jit(solution)/shard_map/ppermute | solution.py:261
  2.7 31.1 %collective-permute-start.3 = (bf16[192,3200]{1,0:T(8,128)(2,1)}, bf16[192,3200]{1,0:T(8,128)(2,1)S(1)}, u32[]{:S(2)}, u32[]{:S(2)}) collective-permute-start(bf16[192,3200]{1,0:T(8,128)(2,1)} %refs_0_.1), channel_id=1, source_target_pairs={{0,60},{1,61},{2,62},{3,63},{4,0},{5,1},{6,2},{7,3},{8,4},{9,5},{1... | collective-permute-start | bytes 3686408 | tf_op jit(solution)/shard_map/ppermute | solution.py:261
  3.2 31.5 %collective-permute-start = (bf16[192,3200]{1,0:T(8,128)(2,1)}, bf16[192,3200]{1,0:T(8,128)(2,1)}, u32[]{:S(2)}, u32[]{:S(2)}) collective-permute-start(bf16[192,3200]{1,0:T(8,128)(2,1)} %refs_0_.1), channel_id=1, source_target_pairs={{0,1},{1,0},{2,3},{3,2},{4,5},{5,4},{6,7},{7,6},{8,9},{9,8},{10,11... | collective-permute-start | bytes 3686408 | tf_op jit(solution)/shard_map/ppermute | solution.py:261
  29.7 5.0 %collective-permute-start.2 = (bf16[192,3200]{1,0:T(8,128)(2,1)}, bf16[192,3200]{1,0:T(8,128)(2,1)}, u32[]{:S(2)}, u32[]{:S(2)}) collective-permute-start(bf16[192,3200]{1,0:T(8,128)(2,1)} %collective-permute-done.1.refs_2_), channel_id=1, source_target_pairs={{0,1},{1,0},{2,3},{3,2},{4,5},{5,4},{6,7},{7,6},{8,9},{9,8},{10,11... | collective-permute-start | bytes 3686408 | tf_op jit(solution)/shard_map/ppermute | solution.py:261
  33.8 26.8 %collective-permute-start.6 = (bf16[192,3200]{1,0:T(8,128)(2,1)S(1)}, bf16[192,3200]{1,0:T(8,128)(2,1)}, u32[]{:S(2)}, u32[]{:S(2)}) collective-permute-start(bf16[192,3200]{1,0:T(8,128)(2,1)S(1)} %collective-permute-done.3.refs_0_), channel_id=1, source_target_pairs={{0,1},{1,0},{2,3},{3,2},{4,5},{5,4},{6,7},{7,6},{8,9},{9,8},{10,11... | collective-permute-start | bytes 3686408 | tf_op jit(solution)/shard_map/ppermute | solution.py:261
  34.2 31.1 %collective-permute-start.8 = (bf16[192,3200]{1,0:T(8,128)(2,1)S(1)}, bf16[192,3200]{1,0:T(8,128)(2,1)}, u32[]{:S(2)}, u32[]{:S(2)}) collective-permute-start(bf16[192,3200]{1,0:T(8,128)(2,1)S(1)} %collective-permute-done.3.refs_0_), channel_id=1, source_target_pairs={{0,2},{1,3},{2,0},{3,1},{4,6},{5,7},{6,4},{7,5},{8,10},{9,11},{10,... | collective-permute-start | bytes 3686408 | tf_op jit(solution)/shard_map/ppermute | solution.py:261
  34.7 30.7 %collective-permute-start.4 = (bf16[192,3200]{1,0:T(8,128)(2,1)S(1)}, bf16[192,3200]{1,0:T(8,128)(2,1)S(1)}, u32[]{:S(2)}, u32[]{:S(2)}) collective-permute-start(bf16[192,3200]{1,0:T(8,128)(2,1)S(1)} %collective-permute-done.3.refs_0_), channel_id=1, source_target_pairs={{0,60},{1,61},{2,62},{3,63},{4,0},{5,1},{6,2},{7,3},{8,4},{9,5},{1... | collective-permute-start | bytes 3686408 | tf_op jit(solution)/shard_map/ppermute | solution.py:261
  34.7 1.3 %copy-start.3 = (bf16[192,3200]{1,0:T(8,128)(2,1)S(1)}, bf16[192,3200]{1,0:T(8,128)(2,1)}, u32[]{:S(2)}) copy-start(bf16[192,3200]{1,0:T(8,128)(2,1)} %refs_0_.1) | copy-start | bytes 3686404
  36.0 0.7 copy-start.4
  36.7 0.7 copy-start.5
  37.4 29.1 %copy-start.6 = (s32[3]{0:T(128)S(1)}, s32[3]{0:T(128)}, u32[]{:S(2)}) copy-start(s32[3]{0:T(128)} %lag_ref.1) | copy-start | bytes 40
  51.6 1.8 %copy-start = (bf16[3,800,768]{2,1,0:T(8,128)(2,1)}, bf16[3,800,768]{2,1,0:T(8,128)(2,1)S(1)}, u32[]{:S(2)}) copy-start(bf16[3,800,768]{2,1,0:T(8,128)(2,1)S(1)} %get-tuple-element.16.y) | copy-start | bytes 11059204
  60.6 7.6 %collective-permute-start.7 = (bf16[192,3200]{1,0:T(8,128)(2,1)}, bf16[192,3200]{1,0:T(8,128)(2,1)}, u32[]{:S(2)}, u32[]{:S(2)}) collective-permute-start(bf16[192,3200]{1,0:T(8,128)(2,1)} %collective-permute-done.6.refs_1_), channel_id=1, source_target_pairs={{60,61},{61,60},{62,63},{63,62},{124,125},{125,124},{126,127},{127... | collective-permute-start | bytes 3686408 | tf_op jit(solution)/shard_map/ppermute | solution.py:280
  65.3 4.6 %collective-permute-start.9 = (bf16[192,3200]{1,0:T(8,128)(2,1)}, bf16[192,3200]{1,0:T(8,128)(2,1)}, u32[]{:S(2)}, u32[]{:S(2)}) collective-permute-start(bf16[192,3200]{1,0:T(8,128)(2,1)} %collective-permute-done.8.refs_3_), channel_id=1, source_target_pairs={{0,1},{1,0},{2,3},{3,2},{4,5},{5,4},{6,7},{7,6},{8,9},{9,8},{10,11... | collective-permute-start | bytes 3686408 | tf_op jit(solution)/shard_map/ppermute | solution.py:261
  65.4 27.9 %collective-permute-start.5 = (bf16[192,3200]{1,0:T(8,128)(2,1)S(1)}, bf16[192,3200]{1,0:T(8,128)(2,1)}, u32[]{:S(2)}, u32[]{:S(2)}) collective-permute-start(bf16[192,3200]{1,0:T(8,128)(2,1)S(1)} %collective-permute-done.4.refs_0_), channel_id=1, source_target_pairs={{0,2},{1,3},{2,0},{3,1},{4,6},{5,7},{6,4},{7,5},{8,10},{9,11},{10,... | collective-permute-start | bytes 3686408 | tf_op jit(solution)/shard_map/ppermute | solution.py:261
  66.4 27.0 %collective-permute-start.10 = (bf16[192,3200]{1,0:T(8,128)(2,1)S(1)}, bf16[192,3200]{1,0:T(8,128)(2,1)}, u32[]{:S(2)}, u32[]{:S(2)}) collective-permute-start(bf16[192,3200]{1,0:T(8,128)(2,1)S(1)} %collective-permute-done.4.refs_0_), channel_id=1, source_target_pairs={{0,1},{1,0},{2,3},{3,2},{4,5},{5,4},{6,7},{7,6},{8,9},{9,8},{10,11... | collective-permute-start | bytes 3686408 | tf_op jit(solution)/shard_map/ppermute | solution.py:261
  69.9 2.0 %copy-start.1 = (bf16[3,800,768]{2,1,0:T(8,128)(2,1)S(1)}, bf16[3,800,768]{2,1,0:T(8,128)(2,1)}, u32[]{:S(2)}) copy-start(bf16[3,800,768]{2,1,0:T(8,128)(2,1)} %copy-done) | copy-start | bytes 11059204
  72.0 30.7 %copy-start.2 = (bf16[3,800,768]{2,1,0:T(8,128)(2,1)S(1)}, bf16[3,800,768]{2,1,0:T(8,128)(2,1)}, u32[]{:S(2)}) copy-start(bf16[3,800,768]{2,1,0:T(8,128)(2,1)} %copy-done) | copy-start | bytes 11059204
  93.3 7.5 %collective-permute-start.11 = (bf16[192,3200]{1,0:T(8,128)(2,1)}, bf16[192,3200]{1,0:T(8,128)(2,1)S(1)}, u32[]{:S(2)}, u32[]{:S(2)}) collective-permute-start(bf16[192,3200]{1,0:T(8,128)(2,1)} %collective-permute-done.10.refs_1_), channel_id=1, source_target_pairs={{56,57},{57,56},{58,59},{59,58},{60,61},{61,60},{62,63},{63,62},{1... | collective-permute-start | bytes 3686408 | tf_op jit(solution)/shard_map/ppermute | solution.py:280
  98.2 4.5 %collective-permute-start.12 = (bf16[192,3200]{1,0:T(8,128)(2,1)}, bf16[192,3200]{1,0:T(8,128)(2,1)S(1)}, u32[]{:S(2)}, u32[]{:S(2)}) collective-permute-start(bf16[192,3200]{1,0:T(8,128)(2,1)} %collective-permute-done.5.refs_0_), channel_id=1, source_target_pairs={{0,1},{1,0},{2,3},{3,2},{4,5},{5,4},{6,7},{7,6},{8,9},{9,8},{10,11... | collective-permute-start | bytes 3686408 | tf_op jit(solution)/shard_map/ppermute | solution.py:261
